TPU v7x, 32 devices: a whole 2x2x4 slice. The times are simulated.
32 devices in a mesh: rep: 8 (over y, x, core), shard: 4 (over z).
Axes of the slice: x: 2, y: 2, z: 4, core: 2. Of those that a mesh axis runs over, the one named last changes fastest.
Arguments:
- token_pool: bfloat16 [8, 384, 2048], P('rep'), may hold values from -6 to 6
- row_index: int32 [8, 2, 1, 512], P('rep'), may hold values from 0 to 383
- weights: bfloat16 [1, 2048, 1024], P(None, None, 'shard'), may hold values from -4 to 4
- targets: bfloat16 [8, 1, 512, 1024], P('rep', None, None, 'shard'), may hold values from -2 to 2
Outputs:
- new_weights: bfloat16 [1, 2048, 1024], P(None, None, 'shard')
All inputs are finite; a program needn't handle non-finite values.
Results may differ from a plain program's by a relative error of at most 0.013.
Values may be sent and summed in bfloat16 or wider, within the bound.
No kernel may reach another device: no remote copies, remote signals or barrier semaphores. Data moves between devices by JAX's collectives and lax.ppermute only.
A program may use at most 64 MiB of HBM per device.

v0:
```python
import math

import jax
import jax.numpy as jnp
from jax import lax
from jax.sharding import PartitionSpec as P

STEPS = 4
CUT = 2


LEARN_RATE = 0.3
MOMENTUM = 0.9
EPSILON = 1e-06


def swapped(shard, axis, apart):
    return lax.ppermute(shard, axis, [(i, i ^ 1 << apart) for i in range(lax.axis_size(axis))])


def local_steps(pool_rows, indices, goals, start_weights):
    running = start_weights.astype(jnp.float32)
    velocity = jnp.zeros_like(running)
    inv_width = 1.0 / math.sqrt(pool_rows.shape[1])
    batch_rows = indices.shape[0] // STEPS
    inv_batch = 1.0 / math.sqrt(batch_rows)
    for step_index in range(STEPS):
        picked = indices[step_index * batch_rows : (step_index + 1) * batch_rows]
        inputs = jnp.take(pool_rows, picked, axis=0)
        wanted = goals[step_index * batch_rows : (step_index + 1) * batch_rows].astype(jnp.float32)
        hidden = (
            jnp.dot(inputs, running.astype(jnp.bfloat16), preferred_element_type=jnp.float32)
            * inv_width
        )
        sigma = jax.nn.sigmoid(hidden)
        slope = sigma * (1.0 + hidden * (1.0 - sigma))
        grad_hidden = ((hidden * sigma - wanted) * slope).astype(jnp.bfloat16)
        gradient = jnp.dot(inputs.T, grad_hidden, preferred_element_type=jnp.float32) * inv_batch
        velocity = MOMENTUM * velocity + gradient
        running = running - LEARN_RATE * velocity
    return (running - start_weights.astype(jnp.float32)).astype(jnp.bfloat16)


def pair_coefs(cross_total, left_total, right_total):
    left_coef = 1.0 - cross_total / (2.0 * (left_total + EPSILON))
    right_coef = 1.0 - cross_total / (2.0 * (right_total + EPSILON))
    return (left_coef, right_coef)


def halving_combine(delta, rep_place, levels, column_group, group_count):
    current = delta.astype(jnp.float32)
    for level_index in range(levels):
        half_rows = current.shape[0] // 2
        upper = rep_place >> level_index & 1
        kept = lax.dynamic_slice_in_dim(current, upper * half_rows, half_rows, 0)
        outgoing = lax.dynamic_slice_in_dim(current, (1 - upper) * half_rows, half_rows, 0)
        incoming = swapped(outgoing, "rep", level_index)
        cross = jnp.sum(kept * incoming)
        own_square = jnp.sum(kept * kept)
        other_square = jnp.sum(incoming * incoming)
        lower_side = upper == 0
        left_square = jnp.where(lower_side, own_square, other_square)
        right_square = jnp.where(lower_side, other_square, own_square)
        rep_groups = lax.axis_size("rep") >> level_index + 1
        rep_marks = jnp.arange(rep_groups, dtype=jnp.int32) == rep_place >> level_index + 1
        column_marks = jnp.arange(group_count, dtype=jnp.int32) == column_group
        marker = (rep_marks[:, None] & column_marks[None, :]).astype(jnp.float32)
        summed = lax.psum(
            (cross * marker, left_square * marker, right_square * marker), ("rep", "shard")
        )
        cross_total = jnp.sum(summed[0] * marker)
        left_total = jnp.sum(summed[1] * marker)
        right_total = jnp.sum(summed[2] * marker)
        left_coef, right_coef = pair_coefs(cross_total, left_total, right_total)
        kept_coef = jnp.where(lower_side, left_coef, right_coef)
        incoming_coef = jnp.where(lower_side, right_coef, left_coef)
        current = kept_coef * kept + incoming_coef * incoming
    return current.astype(jnp.bfloat16)


def reversed_order(gathered, levels):
    segment_rows = gathered.shape[0] >> levels
    shaped = gathered.reshape((2,) * levels + (segment_rows, gathered.shape[1]))
    order = tuple(range(levels - 1, -1, -1)) + (levels, levels + 1)
    return jnp.transpose(shaped, order).reshape(gathered.shape)


def body(token_pool, row_index, weights, targets):
    rep_count = lax.axis_size("rep")
    levels = rep_count.bit_length() - 1
    rep_place = lax.axis_index("rep")
    column_group = lax.axis_index("shard") // CUT
    group_count = lax.axis_size("shard") // CUT
    pool_rows = token_pool[0]
    chosen_rows = lax.dynamic_index_in_dim(row_index[0], column_group, 0, keepdims=False)
    start_weights = weights[0]
    delta = local_steps(pool_rows, chosen_rows[0], targets[0, 0], start_weights)
    segment = halving_combine(delta, rep_place, levels, column_group, group_count)
    gathered = lax.all_gather(segment, "rep", axis=0, tiled=True)
    gathered = reversed_order(gathered, levels)
    results = [
        (start_weights.astype(jnp.float32) + gathered.astype(jnp.float32)).astype(jnp.bfloat16)
    ]
    return jnp.stack(results, 0)


def solution(mesh):
    in_specs = (
        P("rep", None, None),
        P("rep", None, None, None),
        P(None, None, "shard"),
        P("rep", None, None, "shard"),
    )
    out_specs = P(None, None, "shard")
    return jax.shard_map(body, mesh=mesh, in_specs=in_specs, out_specs=out_specs, check_vma=False)
```

profile of v0, /device:TPU:0, one launch (start us, length us, event | category | flops | bytes accessed | tf_op | source)
XLA Modules:
  0.0 245.9 jit_solution(17195400572351028302)
XLA Ops:
  6.5 0.0 copy-start
  6.5 0.0 all-gather.2.cloned.1.call-start
  6.5 0.8 compare_and_fusion
  7.4 0.6 copy-done
  8.0 0.9 gather_fusion
  8.9 1.7 gather_fusion.1
  10.7 1.7 gather_fusion.2
  12.4 0.0 copy-start.1
  12.4 0.0 copy-start.5
  12.4 1.8 gather_fusion.3
  14.2 0.0 copy-done.1
  14.2 0.0 copy-done.5
  14.2 2.3 fusion.17
  16.5 0.0 copy-start.3
  16.5 5.0 %fusion.5 = f32[2048,256]{1,0:T(8,128)} fusion(f32[2048,256]{1,0:T(8,128)} %fusion.17, bf16[128,2048]{1,0:T(8,128)(2,1)} %gather_fusion.1, pred[128]{0:T(512)(128)(4,1)S(1)} %get-tuple-element.45, bf16[1,2048,256]{2,1,0:T(8,128)(2,1)S(1)} %copy-done.1, bf16[1,1,512,256]{3,2,1,0:T(8,128)(2,1)S(1)} %copy-done.5), kind=kOutput, calls=%fused_computation.12 | convolution fusion | flops 273055744 | bytes 8455168 | tf_op jit(solution)/shard_map/dot_general | solution.py:38
  21.5 0.0 copy-done.3
  21.5 5.4 %fusion.4 = f32[2048,256]{1,0:T(8,128)} fusion(f32[2048,256]{1,0:T(8,128)} %fusion.5, bf16[128,2048]{1,0:T(8,128)(2,1)S(1)} %copy-done.3, pred[128]{0:T(512)(128)(4,1)S(1)} %get-tuple-element.43, f32[2048,256]{1,0:T(8,128)} %fusion.17, bf16[1,2048,256]{2,1,0:T(8,128)(2,1)S(1)} %copy-done.1, bf16[1,1,512,256]{3,2,1,0:T(8,128)(2,1)S(1)} %copy-done.5), kind=kOutput, calls=%fused_computation.10 | convolution fusion | flops 274104320 | bytes 10552320 | tf_op jit(solution)/shard_map/dot_general | solution.py:38
  26.9 8.1 %fusion.7 = f32[2048,256]{1,0:T(8,128)} fusion(f32[2048,256]{1,0:T(8,128)} %fusion.4, bf16[1,2048,256]{2,1,0:T(8,128)(2,1)S(1)} %copy-done.1, bf16[128,2048]{1,0:T(8,128)(2,1)} %gather_fusion.3, pred[128]{0:T(512)(128)(4,1)S(1)} %get-tuple-element.35, f32[2048,256]{1,0:T(8,128)} %fusion.5, f32[2048,256]{1,0:T(8,128)} %fusion.17, ...), kind=kOutput, calls=%fused_computation.15 | convolution fusion | flops 281444352 | bytes 17892352 | tf_op jit(solution)/shard_map/dot_general | solution.py:38
  35.0 2.3 constant_dynamic-slice_fusion.5
  37.3 0.5 collective-permute-start
  37.7 2.6 %collective-permute-done = f32[1024,256]{1,0:T(8,128)} collective-permute-done((f32[1024,256]{1,0:T(8,128)}, f32[1024,256]{1,0:T(8,128)}, u32[]{:S(2)}, u32[]{:S(2)}) %collective-permute-start) | collective-permute-done | bytes 1048608 | tf_op jit(solution)/shard_map/ppermute | solution.py:18
  40.3 2.4 multiply_reduce_fusion.1
  45.3 0.6 and_select_fusion.5
  45.9 41.9 %all-reduce.2 = (f32[4,2]{0,1:T(2,128)S(1)}, f32[4,2]{0,1:T(2,128)S(1)}, f32[4,2]{0,1:T(2,128)S(1)}) all-reduce(f32[4,2]{0,1:T(2,128)S(1)} %get-tuple-element.53, f32[4,2]{0,1:T(2,128)S(1)} %get-tuple-element.54, f32[4,2]{0,1:T(2,128)S(1)} %get-tuple-element.52), channel_id=1, replica_groups=mesh['rep'=8,'shard'=4] {'rep','shard'}, use_global_device_ids=true, to_apply=%region_5.7 | all-reduce | flops 24 | bytes 192 | tf_op jit(solution)/shard_map/psum | solution.py:68
  87.8 0.7 fusion.62
  91.0 1.7 multiply_add_fusion
  92.7 0.0 copy-start.2
  92.7 1.0 copy-done.2
  93.6 0.8 constant_dynamic-slice_fusion.4
  94.4 2.3 collective-permute-start.1
  96.7 10.8 %collective-permute-done.1 = f32[512,256]{1,0:T(8,128)S(1)} collective-permute-done((f32[512,256]{1,0:T(8,128)}, f32[512,256]{1,0:T(8,128)S(1)}, u32[]{:S(2)}, u32[]{:S(2)}) %collective-permute-start.1) | collective-permute-done | bytes 524320 | tf_op jit(solution)/shard_map/ppermute | solution.py:18
  107.5 0.0 copy-start.4
  107.5 2.1 multiply_reduce_fusion.4
  112.2 0.6 and_select_fusion.11
  112.9 40.0 %all-reduce.1 = (f32[2,2]{1,0:T(2,128)S(1)}, f32[2,2]{1,0:T(2,128)S(1)}, f32[2,2]{1,0:T(2,128)S(1)}) all-reduce(f32[2,2]{1,0:T(2,128)S(1)} %get-tuple-element.51, f32[2,2]{1,0:T(2,128)S(1)} %get-tuple-element.50, f32[2,2]{1,0:T(2,128)S(1)} %get-tuple-element.49), channel_id=1, replica_groups=mesh['rep'=8,'shard'=4] {'rep','shard'}, use_global_device_ids=true, to_apply=%region_14.16 | all-reduce | flops 12 | bytes 96 | tf_op jit(solution)/shard_map/psum | solution.py:68
  152.9 0.8 fusion.59
  156.2 0.0 copy-done.4
  156.2 1.3 multiply_add_fusion.1
  157.5 0.7 constant_dynamic-slice_fusion.3
  158.2 2.3 collective-permute-start.2
  160.5 5.2 %collective-permute-done.2 = f32[256,256]{1,0:T(8,128)S(1)} collective-permute-done((f32[256,256]{1,0:T(8,128)}, f32[256,256]{1,0:T(8,128)S(1)}, u32[]{:S(2)}, u32[]{:S(2)}) %collective-permute-start.2) | collective-permute-done | bytes 262176 | tf_op jit(solution)/shard_map/ppermute | solution.py:18
  165.7 0.8 multiply_reduce_fusion.7
  168.8 0.7 broadcast_select_fusion.30
  169.6 39.1 %all-reduce = (f32[1,2]{1,0:T(1,128)S(1)}, f32[1,2]{1,0:T(1,128)S(1)}, f32[1,2]{1,0:T(1,128)S(1)}) all-reduce(f32[1,2]{1,0:T(1,128)S(1)} %get-tuple-element.56, f32[1,2]{1,0:T(1,128)S(1)} %get-tuple-element.55, f32[1,2]{1,0:T(1,128)S(1)} %get-tuple-element.33), channel_id=1, replica_groups=mesh['rep'=8,'shard'=4] {'rep','shard'}, use_global_device_ids=true, to_apply=%region_23.25 | all-reduce | flops 6 | bytes 48 | tf_op jit(solution)/shard_map/psum | solution.py:68
  208.7 0.7 select_reduce_fusion.1
  211.8 0.7 add_convert_fusion.1
  212.5 0.0 all-gather.2.cloned.1.call-update
  212.6 23.6 %all-gather.2.cloned.1.call-done = bf16[2048,256]{1,0:T(8,128)(2,1)} async-done(((bf16[256,256]{1,0:T(8,128)(2,1)}), bf16[2048,256]{1,0:T(8,128)(2,1)}) %all-gather.2.cloned.1.call-update) | async-done | bytes 1048592 | tf_op jit(solution)/shard_map/all_gather | solution.py:99
  236.1 1.4 convert_bitcast_fusion
  237.5 0.1 copy.6
  237.7 1.4 add_convert_fusion
  (6 shorter events, 0.0 us)
Async XLA Ops:
  6.5 1.5 copy-start
  6.5 229.6 %all-gather.2.cloned.1.call-start = ((), (), s32[]{:S(2)}) async-start(), calls=%async_computation | async-start | bytes 1179648 | tf_op jit(solution)/shard_map/all_gather | solution.py:99
  12.4 1.8 copy-start.1
  12.4 1.8 copy-start.5
  16.5 5.0 %copy-start.3 = (bf16[128,2048]{1,0:T(8,128)(2,1)S(1)}, bf16[128,2048]{1,0:T(8,128)(2,1)}, u32[]{:S(2)}) copy-start(bf16[128,2048]{1,0:T(8,128)(2,1)} %gather_fusion.2) | copy-start | bytes 1572868
  37.3 3.1 %collective-permute-start = (f32[1024,256]{1,0:T(8,128)}, f32[1024,256]{1,0:T(8,128)}, u32[]{:S(2)}, u32[]{:S(2)}) collective-permute-start(f32[1024,256]{1,0:T(8,128)} %constant_dynamic-slice_fusion.5), channel_id=1, source_target_pairs={{0,4},{4,0},{8,12},{12,8},{16,20},{20,16},{24,28},{28,24},{1,5},{5... | collective-permute-start | bytes 3145736 | tf_op jit(solution)/shard_map/ppermute | solution.py:18
  92.7 1.0 copy-start.2
  94.4 13.1 %collective-permute-start.1 = (f32[512,256]{1,0:T(8,128)}, f32[512,256]{1,0:T(8,128)S(1)}, u32[]{:S(2)}, u32[]{:S(2)}) collective-permute-start(f32[512,256]{1,0:T(8,128)} %constant_dynamic-slice_fusion.4), channel_id=1, source_target_pairs={{0,8},{4,12},{8,0},{12,4},{16,24},{20,28},{24,16},{28,20},{1,9},{5... | collective-permute-start | bytes 1572872 | tf_op jit(solution)/shard_map/ppermute | solution.py:18
  107.5 48.7 %copy-start.4 = (f32[512,256]{1,0:T(8,128)}, f32[512,256]{1,0:T(8,128)S(1)}, u32[]{:S(2)}) copy-start(f32[512,256]{1,0:T(8,128)S(1)} %collective-permute-done.1) | copy-start | bytes 1572868
  158.2 7.4 %collective-permute-start.2 = (f32[256,256]{1,0:T(8,128)}, f32[256,256]{1,0:T(8,128)S(1)}, u32[]{:S(2)}, u32[]{:S(2)}) collective-permute-start(f32[256,256]{1,0:T(8,128)} %constant_dynamic-slice_fusion.3), channel_id=1, source_target_pairs={{0,16},{4,20},{8,24},{12,28},{16,0},{20,4},{24,8},{28,12},{1,17},{... | collective-permute-start | bytes 786440 | tf_op jit(solution)/shard_map/ppermute | solution.py:18
Sparse Core Ops, SparseCore 0:
  212.7 23.4 all-gather.1
where the time goes:
time: 247 us; the launch traced here: 246 us
  blocking collectives  121 us (49%)
  waiting for transfers between devices  42.1 us (17%)
  between operations  28.6 us (12%)
  matrix products  20.8 us (8%)
  other arithmetic  16.6 us (7%)
  local copies, waits for them, and re-layouts  11.7 us (5%)
  starting transfers between devices  5 us (2%)
    psum x3, blocking collectives, halving_combine(): lax.psum((cross * marker, left_square * marker, right_square * marker), (...  121 us
    all_gather x1, waiting for transfers between devices, body(): gathered = lax.all_gather(segment, 'rep', axis=0, tiled=True)  23.6 us
    dot_general x4, matrix products, local_steps(): jnp.dot(inputs.T, grad_hidden, preferred_element_type=jnp.float32)  20.8 us
    ppermute x3, waiting for transfers between devices, swapped(): lax.ppermute(shard, axis, [(i, i ^ 1 << apart) for i in range(lax.axis_si...  18.6 us
    gather x4, local copies, waits for them, and re-layouts, local_steps(): inputs = jnp.take(pool_rows, picked, axis=0)  6.15 us
    reduce_sum x3, other arithmetic, halving_combine(): own_square = jnp.sum(kept * kept)  5.24 us
    ppermute x3, starting transfers between devices, swapped(): lax.ppermute(shard, axis, [(i, i ^ 1 << apart) for i in range(lax.axis_si...  5 us
  transfers between devices with their start and end apart: 4, of which 4 were waited for; matrix products, arithmetic and copies ran while one was open for 0% of the time, Pallas kernels for 0%

commit v1 on v0

v1 whole, which is shorter than its diff:
```python
import math

import jax
import jax.numpy as jnp
from jax import lax
from jax.experimental import pallas as pl
from jax.experimental.pallas import tpu as pltpu
from jax.sharding import PartitionSpec as P

FF = 512
STEPS = 4
LEARN_RATE = 0.3
MOMENTUM = 0.9
EPSILON = 1e-06
LOADS = 4
LATE = 3
VMEM_LIMIT = 48 * 1024 * 1024

F32 = jnp.float32
BF16 = jnp.bfloat16


def reach(steps_between):
    return LEARN_RATE * sum(MOMENTUM**k for k in range(steps_between))


def contract(a, b, dims):
    return lax.dot_general(a, b, (dims, ((), ())), preferred_element_type=F32)


def local_kernel(cut, idx_hbm, pool_hbm, w_hbm, goal_hbm, *rest):
    outs, own_ref = rest[:-7], rest[-7]
    idx_ref, pool_ref, w_ref, goal_ref, x_ref, sems = rest[-6:]
    parts = len(outs)
    pool_rows, width = pool_ref.shape
    total_rows = idx_ref.shape[-1]
    batch = total_rows // STEPS
    seg = width // parts
    inv_width = 1.0 / math.sqrt(width)
    inv_batch = 1.0 / math.sqrt(batch)
    share = width // LOADS
    pieces = [pl.ds(n * share, share) for n in range(LOADS)]

    idx_load = pltpu.make_async_copy(
        idx_hbm.at[lax.axis_index("shard") // cut], idx_ref, sems.at[len(pieces) + 2]
    )
    idx_load.start()
    pool_loads = []
    for n in range(LOADS):
        rows = pl.ds(n * (pool_rows // LOADS), pool_rows // LOADS)
        load = pltpu.make_async_copy(pool_hbm.at[rows], pool_ref.at[rows], sems.at[n])
        load.start()
        pool_loads.append(load)
    w_load = pltpu.make_async_copy(w_hbm, w_ref, sems.at[len(pieces)])
    goal_load = pltpu.make_async_copy(goal_hbm, goal_ref, sems.at[len(pieces) + 1])

    idx_load.wait()
    place = lax.broadcasted_iota(jnp.int32, (batch, pool_rows), 1)
    hits = []
    for t in range(STEPS):
        picked = jnp.broadcast_to(idx_ref[:, t * batch : (t + 1) * batch], (8, batch))
        picked = picked.astype(F32).T[:, :1].astype(jnp.int32)
        hits.append(jnp.where(place == picked, 1.0, 0.0).astype(BF16))
    one_hot = jnp.concatenate(hits, axis=0)
    pool_loads[0].wait()
    w_load.start()
    goal_load.start()
    for load in pool_loads[1:]:
        load.wait()
    for piece in pieces:
        x_ref[:, piece] = jnp.dot(
            one_hot, pool_ref[:, piece], preferred_element_type=F32
        ).astype(BF16)
    w_load.wait()
    goal_load.wait()
    base = jnp.dot(x_ref[...], w_ref[...], preferred_element_type=F32) * inv_width

    overlaps = {}
    for s in range(0, STEPS - 1, 2):
        stop = min(s + 2, STEPS - 1)
        overlaps[s] = contract(
            x_ref[(s + 1) * batch :, :], x_ref[s * batch : stop * batch, :], ((1,), (1,))
        )

    spread = []
    for s in range(STEPS - 1):
        first = s // 2 * 2
        halves = []
        for t in range(s + 1, STEPS):
            down, across = (t - first - 1) * batch, (s - first) * batch
            block = overlaps[first][down : down + batch, across : across + batch]
            block = block * (reach(t - s) * inv_batch * inv_width)
            high = block.astype(BF16)
            halves += [high, (block - high.astype(F32)).astype(BF16)]
        spread.append(jnp.concatenate(halves, axis=0))

    hidden = [base[t * batch : (t + 1) * batch] for t in range(STEPS)]
    final = []
    for s in range(STEPS):
        sigma = jax.nn.sigmoid(hidden[s])
        wanted = goal_ref[s * batch : (s + 1) * batch, :].astype(F32)
        grad = (hidden[s] * sigma - wanted) * (sigma * (1.0 + hidden[s] * (1.0 - sigma)))
        if s < STEPS - 1:
            moved = jnp.dot(spread[s], grad.astype(BF16), preferred_element_type=F32)
            for n, t in enumerate(range(s + 1, STEPS)):
                at = 2 * n * batch
                hidden[t] = hidden[t] - (
                    moved[at : at + batch] + moved[at + batch : at + 2 * batch]
                )
        final.append((grad * (-reach(STEPS - s) * inv_batch)).T.astype(BF16))

    turned = jnp.concatenate(final, axis=1)
    me = lax.axis_index("rep")
    own_ref[...] = w_ref[pl.ds(pl.multiple_of(me * seg, seg), seg), :]
    for distance, out_ref in zip(distances(parts), outs):
        target = me ^ distance
        held = max(seg, 128)
        at = pl.multiple_of(target * seg // held * held, held)
        moved = jnp.dot(turned, x_ref[:, pl.ds(at, held)], preferred_element_type=F32)
        share = moved[:, :seg]
        for place in range(1, held // seg):
            own = target % (held // seg) == place
            share = jnp.where(own, moved[:, place * seg : (place + 1) * seg], share)
        out_ref[...] = share.astype(BF16)


def distances(parts):
    def far(distance):
        return (distance == 1, distance & 1, -(distance >> 1).bit_count(), distance)

    return [0, *sorted(range(1, parts), key=far)]


def pair_list(count):
    return [(i, j) for i in range(count) for j in range(i, count)]


def gram_kernel(order, known, *refs):
    count = len(order)
    deltas, before, out_ref = refs[:count], refs[count:-1], refs[-1]
    rows, seg = deltas[0].shape
    lanes = min(128, seg)
    block = min(8, count)
    tall = 16
    me = lax.axis_index("rep")
    down = lax.broadcasted_iota(jnp.int32, out_ref.shape, 0)
    across = lax.broadcasted_iota(jnp.int32, out_ref.shape, 1)
    table = before[0][...] if before else jnp.zeros(out_ref.shape, F32)
    for first in range(0, count, block):
        for second in range(first, count, block):
            pairs = [
                (i, j)
                for i in range(first, min(first + block, count))
                for j in range(second, min(second + block, count))
                if i <= j and j >= known
            ]
            if not pairs:
                continue
            members = sorted({k for pair in pairs for k in pair})

            def step(at, sums, pairs=pairs, members=members):
                sums = list(sums)
                row = pl.multiple_of(at * tall, tall)
                for lane in range(0, seg, lanes):
                    held = {
                        k: deltas[k][pl.ds(row, tall), lane : lane + lanes].astype(F32)
                        for k in members
                    }
                    for n, (i, j) in enumerate(pairs):
                        product = held[i] * held[j]
                        sums[n] = sums[n] + (product[:8] + product[8:])
                return tuple(sums)

            zeros = tuple(jnp.zeros((8, lanes), F32) for _ in pairs)
            sums = lax.fori_loop(0, rows // tall, step, zeros)
            for n, (i, j) in enumerate(pairs):
                value = jnp.sum(jnp.sum(sums[n], axis=0, keepdims=True), axis=1, keepdims=True)
                mine, other = me ^ order[i], me ^ order[j]
                spot = ((down == mine) & (across == other)) | ((down == other) & (across == mine))
                table = jnp.where(spot, value, table)
    out_ref[...] = table


def tree_weights(gram, count):
    weights = [None] * count
    current = dict(gram)
    width = 1
    while count > 1:
        left, right = [], []
        for i in range(0, count, 2):
            cross = current[i, i + 1]
            left_square = jnp.maximum(current[i, i], 0.0)
            right_square = jnp.maximum(current[i + 1, i + 1], 0.0)
            left.append(1.0 - cross / (2.0 * (left_square + EPSILON)))
            right.append(1.0 - cross / (2.0 * (right_square + EPSILON)))
        for i in range(count):
            scale = (right if i % 2 else left)[i // 2]
            for k in range(i * width, (i + 1) * width):
                weights[k] = scale if weights[k] is None else weights[k] * scale
        merged = {}
        for i in range(count // 2):
            for j in range(i, count // 2):

                def entry(a, b):
                    return current[min(a, b), max(a, b)]

                merged[i, j] = left[i] * (
                    left[j] * entry(2 * i, 2 * j) + right[j] * entry(2 * i, 2 * j + 1)
                ) + right[i] * (
                    left[j] * entry(2 * i + 1, 2 * j) + right[j] * entry(2 * i + 1, 2 * j + 1)
                )
        current = merged
        count //= 2
        width *= 2
    return weights


def combine_kernel(gram_ref, own_ref, *rest):
    deltas, out_ref = rest[:-1], rest[-1]
    count = len(deltas)
    me = lax.axis_index("rep")
    table = gram_ref[0]
    for member in range(1, gram_ref.shape[0]):
        table = table + gram_ref[member]
    gram = {(i, j): table[i : i + 1, j : j + 1] for i, j in pair_list(count)}
    weights = tree_weights(gram, count)
    total = None
    for distance, delta in zip(distances(count), deltas):
        weight = weights[0]
        for k in range(1, count):
            weight = jnp.where((me ^ distance) == k, weights[k], weight)
        term = weight * delta[...].astype(F32)
        total = term if total is None else total + term
    combined = total.T.astype(BF16).astype(F32)
    out_ref[...] = (own_ref[...].astype(F32) + combined).astype(BF16)


def place_kernel(*refs):
    pieces, (out_ref, sems) = refs[:-2], refs[-2:]
    seg = pieces[0].shape[0]
    me = lax.axis_index("rep")
    moves = []
    for distance, piece in enumerate(pieces):
        at = pl.multiple_of((me ^ distance) * seg, seg)
        move = pltpu.make_async_copy(piece, out_ref.at[pl.ds(at, seg)], sems.at[distance])
        move.start()
        moves.append(move)
    for move in moves:
        move.wait()


def call(kernel, out_shape, in_specs, scratch=(), out_specs=None):
    extra = {} if out_specs is None else {"out_specs": out_specs}
    return pl.pallas_call(
        kernel,
        out_shape=out_shape,
        in_specs=in_specs,
        scratch_shapes=scratch,
        compiler_params=pltpu.CompilerParams(vmem_limit_bytes=VMEM_LIMIT),
        **extra,
    )


def hold(value):
    return pltpu.with_memory_space_constraint(value, pltpu.HBM)


def flipped(value, replica_bits, shard_bits=0):
    replicas, shards = lax.axis_size("rep"), lax.axis_size("shard")
    pairs = [
        (i * shards + j, (i ^ replica_bits) * shards + (j ^ shard_bits))
        for i in range(replicas)
        for j in range(shards)
    ]
    return lax.ppermute(value, ("rep", "shard"), pairs)


def body(token_pool, row_index, weights, targets):
    parts = lax.axis_size("rep")
    width, columns = weights.shape[1:]
    cut = FF // columns
    seg = width // parts
    rows = row_index.shape[-1]
    pool_rows = token_pool.shape[1]
    near = pl.BlockSpec(memory_space=pltpu.VMEM)
    far = pl.BlockSpec(memory_space=pltpu.HBM)
    any_place = pl.BlockSpec(memory_space=pl.ANY)

    def local(*refs):
        local_kernel(cut, *refs)

    order = distances(parts)
    *sent, own_weights = call(
        local,
        [jax.ShapeDtypeStruct((columns, seg), BF16)] * parts
        + [jax.ShapeDtypeStruct((seg, columns), BF16)],
        [far] * 4,
        [
            pltpu.VMEM((1, rows), jnp.int32),
            pltpu.VMEM((pool_rows, width), BF16),
            pltpu.VMEM((width, columns), BF16),
            pltpu.VMEM((rows, columns), BF16),
            pltpu.VMEM((rows, width), BF16),
            pltpu.SemaphoreType.DMA((LOADS + 3,)),
        ],
    )(hold(row_index[0]), hold(token_pool[0]), hold(weights[0]), hold(targets[0, 0]))
    deltas = [value if d == 0 else flipped(value, d) for d, value in zip(order, sent)]

    tall = -(-parts // 8) * 8
    table = jax.ShapeDtypeStruct((tall, 128), F32)
    late = LATE if parts > LATE + 1 else 0
    soon = order[: parts - late]
    leaves = dict(zip(order, deltas))

    def first_gram(*refs):
        gram_kernel(soon, 0, *refs)

    def full_gram(*refs):
        gram_kernel(order, len(soon), *refs)

    gram = call(first_gram, table, [near] * len(soon))(*(leaves[d] for d in soon))
    if late:
        gram = call(full_gram, table, [near] * (parts + 1))(
            *(leaves[d] for d in order), gram
        )
    shards = lax.axis_size("shard")
    groups = [
        [i * shards + j for i in range(parts) for j in range(first, first + cut)]
        for first in range(0, shards, cut)
    ]
    groups = [group[::-1] for group in groups]
    gram = jnp.broadcast_to(gram, (parts * cut, *gram.shape))
    gram = lax.all_to_all(gram, ("rep", "shard"), 0, 0, axis_index_groups=groups)

    own = call(
        combine_kernel,
        jax.ShapeDtypeStruct((seg, columns), BF16),
        [near] * (parts + 2),
    )(gram, own_weights, *deltas)
    pieces = [own] + [None] * (parts - 1)
    pieces[1] = flipped(own, 1)
    for d in range(2, parts, 2):
        pieces[d + 1] = flipped(own, d + 1)
        pieces[d] = flipped(pieces[d + 1], 1)
    placed = call(
        place_kernel,
        jax.ShapeDtypeStruct((width, columns), BF16),
        [any_place] * parts,
        [pltpu.SemaphoreType.DMA((parts,))],
        far,
    )(*pieces)
    return placed[None]


def solution(mesh):
    in_specs = (
        P("rep", None, None),
        P("rep", None, None, None),
        P(None, None, "shard"),
        P("rep", None, None, "shard"),
    )
    out_specs = P(None, None, "shard")
    return jax.shard_map(body, mesh=mesh, in_specs=in_specs, out_specs=out_specs, check_vma=False)
```

time: 247 us -> 43.2 us (0.17)
  blocking collectives: 121 us -> 8.37 us
  between operations: 28.6 us -> 0.04 us
  waiting for transfers between devices: 42.1 us -> 14.7 us
  matrix products: 20.8 us -> 0 us
  other arithmetic: 16.6 us -> 0 us
  local copies, waits for them, and re-layouts: 11.7 us -> 0.01 us
  Pallas kernels: 0 us -> 8.24 us
  starting transfers between devices: 5 us -> 11.7 us
    psum x3 -> x0, blocking collectives: 121 us -> none  [halving_combine(): lax.psum((cross * marker, left_square * marker, right_square * marker), (...]
    all_gather x1 -> x0, waiting for transfers between devices: 23.6 us -> none  [body(): gathered = lax.all_gather(segment, 'rep', axis=0, tiled=True)]
    dot_general x4 -> x0, matrix products: 20.8 us -> none  [local_steps(): jnp.dot(inputs.T, grad_hidden, preferred_element_type=jnp.float32)]
    all_to_all x0 -> x1, blocking collectives: none -> 8.37 us  [body(): lax.all_to_all(gram, ('rep', 'shard'), 0, 0, axis_index_groups=groups)]
    pallas_call x0 -> x5, Pallas kernels: none -> 8.24 us  [the longest x1 5.16 us: body(): call(local, [jax.ShapeDtypeStruct((columns, seg), BF16)] * parts + [jax.S...]
    reduce_sum x6 -> x0, other arithmetic: 7.36 us -> none  [the longest x3 5.24 us: halving_combine(): own_square = jnp.sum(kept * kept)]
    ppermute x3 -> x14, starting transfers between devices: 5 us -> 11.7 us  [flipped(): return lax.ppermute(value, ('rep', 'shard'), pairs)]
    gather x4 -> x0, local copies, waits for them, and re-layouts: 6.15 us -> none  [local_steps(): inputs = jnp.take(pool_rows, picked, axis=0)]
  transfers between devices with their start and end apart: 4 -> 14, of which waited for: 4 -> 9; matrix products, arithmetic and copies ran while one was open for 0% -> 0% of each run, Pallas kernels for 0% -> 1%
where the time goes in v1:
time: 43.2 us; the launch traced here: 43.1 us
  waiting for transfers between devices  14.7 us (34%)
  starting transfers between devices  11.7 us (27%)
  blocking collectives  8.37 us (19%)
  Pallas kernels  8.24 us (19%)
    ppermute x14, waiting for transfers between devices, flipped(): return lax.ppermute(value, ('rep', 'shard'), pairs)  14.7 us
    ppermute x14, starting transfers between devices, flipped(): return lax.ppermute(value, ('rep', 'shard'), pairs)  11.7 us
    all_to_all x1, blocking collectives, body(): lax.all_to_all(gram, ('rep', 'shard'), 0, 0, axis_index_groups=groups)  8.37 us
    pallas_call x1, Pallas kernels, body(): call(local, [jax.ShapeDtypeStruct((columns, seg), BF16)] * parts + [jax.S...  5.16 us
    pallas_call x1, Pallas kernels, body(): call(place_kernel, jax.ShapeDtypeStruct((width, columns), BF16), [any_pla...  1.02 us
    pallas_call x1, Pallas kernels, body(): call(combine_kernel, jax.ShapeDtypeStruct((seg, columns), BF16), [near] *...  0.91 us
  transfers between devices with their start and end apart: 14, of which 9 were waited for; matrix products, arithmetic and copies ran while one was open for 0% of the time, Pallas kernels for 1%

profile of v1, /device:TPU:0, one launch (start us, length us, event | category | flops | bytes accessed | tf_op | source)
XLA Modules:
  0.0 43.1 jit_solution(5199549990167983025)
XLA Ops:
  0.0 5.2 %shard_map.46 = (bf16[256,256]{1,0:T(8,128)(2,1)S(1)}, bf16[256,256]{1,0:T(8,128)(2,1)S(1)}, bf16[256,256]{1,0:T(8,128)(2,1)S(1)}, bf16[256,256]{1,0:T(8,128)(2,...) custom-call(s32[2,1,512]{2,1,0:T(1,128)} %bitcast.8, ...), custom_call_target="tpu_custom_call" | custom-call | tf_op jit(solution)/shard_map/pallas_call | solution.py:293
  5.2 4.0 %collective-permute-start = (bf16[256,256]{1,0:T(8,128)(2,1)S(1)}, bf16[256,256]{1,0:T(8,128)(2,1)S(1)}, u32[]{:S(2)}, u32[]{:S(2)}) collective-permute-start(bf16[256,256]{1,0:T(8,128)(2,1)S(1)} %get-tuple-element.15), channel_id=1, source_target_pairs={{0,24},{1,25},{2,26},{3,27},{4,28},{5,29},{6,30},{7,31},{8,16},{9,... | collective-permute-start | bytes 393224 | tf_op jit(solution)/shard_map/ppermute | solution.py:275
  9.1 0.5 %collective-permute-start.1 = (bf16[256,256]{1,0:T(8,128)(2,1)S(1)}, bf16[256,256]{1,0:T(8,128)(2,1)S(1)}, u32[]{:S(2)}, u32[]{:S(2)}) collective-permute-start(bf16[256,256]{1,0:T(8,128)(2,1)S(1)} %get-tuple-element.16), channel_id=1, source_target_pairs={{0,8},{1,9},{2,10},{3,11},{4,12},{5,13},{6,14},{7,15},{8,0},{9,1},... | collective-permute-start | bytes 393224 | tf_op jit(solution)/shard_map/ppermute | solution.py:275
  9.7 0.1 collective-permute-start.2
  9.8 1.4 %collective-permute-start.3 = (bf16[256,256]{1,0:T(8,128)(2,1)S(1)}, bf16[256,256]{1,0:T(8,128)(2,1)S(1)}, u32[]{:S(2)}, u32[]{:S(2)}) collective-permute-start(bf16[256,256]{1,0:T(8,128)(2,1)S(1)} %get-tuple-element.18), channel_id=1, source_target_pairs={{0,28},{1,29},{2,30},{3,31},{4,24},{5,25},{6,26},{7,27},{8,20},{9,... | collective-permute-start | bytes 393224 | tf_op jit(solution)/shard_map/ppermute | solution.py:275
  11.2 1.7 %collective-permute-start.4 = (bf16[256,256]{1,0:T(8,128)(2,1)S(1)}, bf16[256,256]{1,0:T(8,128)(2,1)S(1)}, u32[]{:S(2)}, u32[]{:S(2)}) collective-permute-start(bf16[256,256]{1,0:T(8,128)(2,1)S(1)} %get-tuple-element.19), channel_id=1, source_target_pairs={{0,12},{1,13},{2,14},{3,15},{4,8},{5,9},{6,10},{7,11},{8,4},{9,5},... | collective-permute-start | bytes 393224 | tf_op jit(solution)/shard_map/ppermute | solution.py:275
  12.9 0.6 %collective-permute-done.refs_1_.rest_1_ = bf16[256,256]{1,0:T(8,128)(2,1)S(1)} collective-permute-done((bf16[256,256]{1,0:T(8,128)(2,1)S(1)}, bf16[256,256]{1,0:T(8,128)(2,1)S(1)}, u32[]{:S(2)}, u32[]{:S(2)}) %collective-permute-start) | collective-permute-done | bytes 131104 | tf_op jit(solution)/shard_map/ppermute | solution.py:275
  13.5 0.0 collective-permute-start.5
  13.5 3.4 %collective-permute-done.1.refs_2_.rest_2_ = bf16[256,256]{1,0:T(8,128)(2,1)S(1)} collective-permute-done((bf16[256,256]{1,0:T(8,128)(2,1)S(1)}, bf16[256,256]{1,0:T(8,128)(2,1)S(1)}, u32[]{:S(2)}, u32[]{:S(2)}) %collective-permute-start.1) | collective-permute-done | bytes 131104 | tf_op jit(solution)/shard_map/ppermute | solution.py:275
  16.8 0.0 collective-permute-start.6
  16.8 0.0 collective-permute-done.2.refs_3_.rest_3_
  16.8 1.8 %collective-permute-done.3.refs_4_.rest_4_ = bf16[256,256]{1,0:T(8,128)(2,1)S(1)} collective-permute-done((bf16[256,256]{1,0:T(8,128)(2,1)S(1)}, bf16[256,256]{1,0:T(8,128)(2,1)S(1)}, u32[]{:S(2)}, u32[]{:S(2)}) %collective-permute-start.3) | collective-permute-done | bytes 131104 | tf_op jit(solution)/shard_map/ppermute | solution.py:275
  18.7 0.5 %shard_map.47.refs_8_ = f32[8,128]{1,0:T(8,128)S(1)} custom-call(bf16[256,256]{1,0:T(8,128)(2,1)S(1)} %get-tuple-element.14.refs_0_.rest_0_, bf16[256,256]{1,0:T(8,128)(2,1)S(1)} %collective-permute-done.refs_1_.rest_1_, bf16[256,256]{1,0:T(8,128)(2,1)S(1)} %collective-permute-done.1.refs_2_.rest_2_, ...), custom_call_target="tpu_custom_call" | custom-call | tf_op jit(solution)/shard_map/pallas_call | solution.py:321
  19.1 1.2 %collective-permute-done.4.refs_5_.rest_5_ = bf16[256,256]{1,0:T(8,128)(2,1)S(1)} collective-permute-done((bf16[256,256]{1,0:T(8,128)(2,1)S(1)}, bf16[256,256]{1,0:T(8,128)(2,1)S(1)}, u32[]{:S(2)}, u32[]{:S(2)}) %collective-permute-start.4) | collective-permute-done | bytes 131104 | tf_op jit(solution)/shard_map/ppermute | solution.py:275
  20.3 0.7 %collective-permute-done.5.refs_6_.rest_6_ = bf16[256,256]{1,0:T(8,128)(2,1)S(1)} collective-permute-done((bf16[256,256]{1,0:T(8,128)(2,1)S(1)}, bf16[256,256]{1,0:T(8,128)(2,1)S(1)}, u32[]{:S(2)}, u32[]{:S(2)}) %collective-permute-start.5) | collective-permute-done | bytes 131104 | tf_op jit(solution)/shard_map/ppermute | solution.py:275
  21.0 0.0 collective-permute-done.6.refs_7_.rest_7_
  21.0 0.7 %shard_map.48 = f32[8,128]{1,0:T(8,128)S(1)} custom-call(bf16[256,256]{1,0:T(8,128)(2,1)S(1)} %get-tuple-element.14.refs_0_.rest_0_, bf16[256,256]{1,0:T(8,128)(2,1)S(1)} %collective-permute-done.refs_1_.rest_1_, bf16[256,256]{1,0:T(8,128)(2,1)S(1)} %collective-permute-done.1.refs_2_.rest_2_, bf16[256,256]{1,0:T(8,128)(2,1)S(1)} %collective-permute-done.2.refs_3_.rest_3_, ...), custom_call_target="tpu_custom_call" | custom-call | tf_op jit(solution)/shard_map/pallas_call | solution.py:323
  21.7 8.4 %all_to_all.5.gram_ref = f32[16,8,128]{2,1,0:T(8,128)S(1)} all-to-all(f32[16,8,128]{2,1,0:T(8,128)S(1)} %broadcast_in_dim.6), channel_id=1, replica_groups={{29,28,25,24,21,20,17,16,13,12,9,8,5,4,1,0},{31,30,27,26,23,22,19,18,15..., dimensions={0} | all-to-all | bytes 131072 | tf_op jit(solution)/shard_map/all_to_all | solution.py:333
  30.1 0.9 %shard_map.49.refs_0_ = bf16[256,256]{1,0:T(8,128)(2,1)S(1)} custom-call(f32[16,8,128]{2,1,0:T(8,128)S(1)} %all_to_all.5.gram_ref, bf16[256,256]{1,0:T(8,128)(2,1)S(1)} %get-tuple-element.22.own_ref, bf16[256,256]{1,0:T(8,128)(2,1)S(1)} %get-tuple-element.14.refs_0_.rest_0_, bf16[256,256]{1,0:T(8,128)(2,1)S(1)} %collective-permute-done.refs_1_.rest_1_, ...), custom_call_target="tpu_custom_call" | custom-call | tf_op jit(solution)/shard_map/pallas_call | solution.py:335
  31.0 2.0 %collective-permute-start.12 = (bf16[256,256]{1,0:T(8,128)(2,1)S(1)}, bf16[256,256]{1,0:T(8,128)(2,1)S(1)}, u32[]{:S(2)}, u32[]{:S(2)}) collective-permute-start(bf16[256,256]{1,0:T(8,128)(2,1)S(1)} %shard_map.49.refs_0_), channel_id=1, source_target_pairs={{0,28},{1,29},{2,30},{3,31},{4,24},{5,25},{6,26},{7,27},{8,20},{9,... | collective-permute-start | bytes 393224 | tf_op jit(solution)/shard_map/ppermute | solution.py:275
  33.0 0.8 %collective-permute-start.10 = (bf16[256,256]{1,0:T(8,128)(2,1)S(1)}, bf16[256,256]{1,0:T(8,128)(2,1)S(1)}, u32[]{:S(2)}, u32[]{:S(2)}) collective-permute-start(bf16[256,256]{1,0:T(8,128)(2,1)S(1)} %shard_map.49.refs_0_), channel_id=1, source_target_pairs={{0,20},{1,21},{2,22},{3,23},{4,16},{5,17},{6,18},{7,19},{8,28},{9,... | collective-permute-start | bytes 393224 | tf_op jit(solution)/shard_map/ppermute | solution.py:275
  33.7 0.1 collective-permute-start.8
  33.9 0.5 %collective-permute-start.7 = (bf16[256,256]{1,0:T(8,128)(2,1)S(1)}, bf16[256,256]{1,0:T(8,128)(2,1)S(1)}, u32[]{:S(2)}, u32[]{:S(2)}) collective-permute-start(bf16[256,256]{1,0:T(8,128)(2,1)S(1)} %shard_map.49.refs_0_), channel_id=1, source_target_pairs={{0,4},{1,5},{2,6},{3,7},{4,0},{5,1},{6,2},{7,3},{8,12},{9,13},{10,... | collective-permute-start | bytes 393224 | tf_op jit(solution)/shard_map/ppermute | solution.py:275
  34.4 3.3 %collective-permute-done.12.refs_7_ = bf16[256,256]{1,0:T(8,128)(2,1)S(1)} collective-permute-done((bf16[256,256]{1,0:T(8,128)(2,1)S(1)}, bf16[256,256]{1,0:T(8,128)(2,1)S(1)}, u32[]{:S(2)}, u32[]{:S(2)}) %collective-permute-start.12) | collective-permute-done | bytes 131104 | tf_op jit(solution)/shard_map/ppermute | solution.py:275
  37.6 0.1 collective-permute-start.13
  37.8 2.7 %collective-permute-done.10.refs_5_ = bf16[256,256]{1,0:T(8,128)(2,1)S(1)} collective-permute-done((bf16[256,256]{1,0:T(8,128)(2,1)S(1)}, bf16[256,256]{1,0:T(8,128)(2,1)S(1)}, u32[]{:S(2)}, u32[]{:S(2)}) %collective-permute-start.10) | collective-permute-done | bytes 131104 | tf_op jit(solution)/shard_map/ppermute | solution.py:275
  40.5 0.2 collective-permute-start.11
  40.7 0.0 collective-permute-done.8.refs_3_
  40.7 0.3 collective-permute-start.9
  41.0 0.0 collective-permute-done.7.refs_1_
  41.0 0.0 collective-permute-done.13.refs_6_
  41.0 0.8 %collective-permute-done.11.refs_4_ = bf16[256,256]{1,0:T(8,128)(2,1)S(1)} collective-permute-done((bf16[256,256]{1,0:T(8,128)(2,1)S(1)}, bf16[256,256]{1,0:T(8,128)(2,1)S(1)}, u32[]{:S(2)}, u32[]{:S(2)}) %collective-permute-start.11) | collective-permute-done | bytes 131104 | tf_op jit(solution)/shard_map/ppermute | solution.py:275
  41.8 0.2 collective-permute-done.9.refs_2_
  42.0 1.0 %shard_map.50 = bf16[2048,256]{1,0:T(8,128)(2,1)} custom-call(bf16[256,256]{1,0:T(8,128)(2,1)S(1)} %shard_map.49.refs_0_, bf16[256,256]{1,0:T(8,128)(2,1)S(1)} %collective-permute-done.7.refs_1_, bf16[256,256]{1,0:T(8,128)(2,1)S(1)} %collective-permute-done.9.refs_2_, bf16[256,256]{1,0:T(8,128)(2,1)S(1)} %collective-permute-done.8.refs_3_, ...), custom_call_target="tpu_custom_call" | custom-call | tf_op jit(solution)/shard_map/pallas_call | solution.py:345
  (1 shorter events, 0.0 us)
Async XLA Ops:
  5.2 8.3 %collective-permute-start = (bf16[256,256]{1,0:T(8,128)(2,1)S(1)}, bf16[256,256]{1,0:T(8,128)(2,1)S(1)}, u32[]{:S(2)}, u32[]{:S(2)}) collective-permute-start(bf16[256,256]{1,0:T(8,128)(2,1)S(1)} %get-tuple-element.15), channel_id=1, source_target_pairs={{0,24},{1,25},{2,26},{3,27},{4,28},{5,29},{6,30},{7,31},{8,16},{9,... | collective-permute-start | bytes 393224 | tf_op jit(solution)/shard_map/ppermute | solution.py:275
  9.1 7.7 %collective-permute-start.1 = (bf16[256,256]{1,0:T(8,128)(2,1)S(1)}, bf16[256,256]{1,0:T(8,128)(2,1)S(1)}, u32[]{:S(2)}, u32[]{:S(2)}) collective-permute-start(bf16[256,256]{1,0:T(8,128)(2,1)S(1)} %get-tuple-element.16), channel_id=1, source_target_pairs={{0,8},{1,9},{2,10},{3,11},{4,12},{5,13},{6,14},{7,15},{8,0},{9,1},... | collective-permute-start | bytes 393224 | tf_op jit(solution)/shard_map/ppermute | solution.py:275
  9.7 7.2 %collective-permute-start.2 = (bf16[256,256]{1,0:T(8,128)(2,1)S(1)}, bf16[256,256]{1,0:T(8,128)(2,1)S(1)}, u32[]{:S(2)}, u32[]{:S(2)}) collective-permute-start(bf16[256,256]{1,0:T(8,128)(2,1)S(1)} %get-tuple-element.17), channel_id=1, source_target_pairs={{0,16},{1,17},{2,18},{3,19},{4,20},{5,21},{6,22},{7,23},{8,24},{9,... | collective-permute-start | bytes 393224 | tf_op jit(solution)/shard_map/ppermute | solution.py:275
  9.8 8.9 %collective-permute-start.3 = (bf16[256,256]{1,0:T(8,128)(2,1)S(1)}, bf16[256,256]{1,0:T(8,128)(2,1)S(1)}, u32[]{:S(2)}, u32[]{:S(2)}) collective-permute-start(bf16[256,256]{1,0:T(8,128)(2,1)S(1)} %get-tuple-element.18), channel_id=1, source_target_pairs={{0,28},{1,29},{2,30},{3,31},{4,24},{5,25},{6,26},{7,27},{8,20},{9,... | collective-permute-start | bytes 393224 | tf_op jit(solution)/shard_map/ppermute | solution.py:275
  11.2 9.1 %collective-permute-start.4 = (bf16[256,256]{1,0:T(8,128)(2,1)S(1)}, bf16[256,256]{1,0:T(8,128)(2,1)S(1)}, u32[]{:S(2)}, u32[]{:S(2)}) collective-permute-start(bf16[256,256]{1,0:T(8,128)(2,1)S(1)} %get-tuple-element.19), channel_id=1, source_target_pairs={{0,12},{1,13},{2,14},{3,15},{4,8},{5,9},{6,10},{7,11},{8,4},{9,5},... | collective-permute-start | bytes 393224 | tf_op jit(solution)/shard_map/ppermute | solution.py:275
  13.5 7.5 %collective-permute-start.5 = (bf16[256,256]{1,0:T(8,128)(2,1)S(1)}, bf16[256,256]{1,0:T(8,128)(2,1)S(1)}, u32[]{:S(2)}, u32[]{:S(2)}) collective-permute-start(bf16[256,256]{1,0:T(8,128)(2,1)S(1)} %get-tuple-element.20), channel_id=1, source_target_pairs={{0,20},{1,21},{2,22},{3,23},{4,16},{5,17},{6,18},{7,19},{8,28},{9,... | collective-permute-start | bytes 393224 | tf_op jit(solution)/shard_map/ppermute | solution.py:275
  16.8 4.2 %collective-permute-start.6 = (bf16[256,256]{1,0:T(8,128)(2,1)S(1)}, bf16[256,256]{1,0:T(8,128)(2,1)S(1)}, u32[]{:S(2)}, u32[]{:S(2)}) collective-permute-start(bf16[256,256]{1,0:T(8,128)(2,1)S(1)} %get-tuple-element.21), channel_id=1, source_target_pairs={{0,4},{1,5},{2,6},{3,7},{4,0},{5,1},{6,2},{7,3},{8,12},{9,13},{10,... | collective-permute-start | bytes 393224 | tf_op jit(solution)/shard_map/ppermute | solution.py:275
  31.0 6.7 %collective-permute-start.12 = (bf16[256,256]{1,0:T(8,128)(2,1)S(1)}, bf16[256,256]{1,0:T(8,128)(2,1)S(1)}, u32[]{:S(2)}, u32[]{:S(2)}) collective-permute-start(bf16[256,256]{1,0:T(8,128)(2,1)S(1)} %shard_map.49.refs_0_), channel_id=1, source_target_pairs={{0,28},{1,29},{2,30},{3,31},{4,24},{5,25},{6,26},{7,27},{8,20},{9,... | collective-permute-start | bytes 393224 | tf_op jit(solution)/shard_map/ppermute | solution.py:275
  33.0 7.5 %collective-permute-start.10 = (bf16[256,256]{1,0:T(8,128)(2,1)S(1)}, bf16[256,256]{1,0:T(8,128)(2,1)S(1)}, u32[]{:S(2)}, u32[]{:S(2)}) collective-permute-start(bf16[256,256]{1,0:T(8,128)(2,1)S(1)} %shard_map.49.refs_0_), channel_id=1, source_target_pairs={{0,20},{1,21},{2,22},{3,23},{4,16},{5,17},{6,18},{7,19},{8,28},{9,... | collective-permute-start | bytes 393224 | tf_op jit(solution)/shard_map/ppermute | solution.py:275
  33.7 6.9 %collective-permute-start.8 = (bf16[256,256]{1,0:T(8,128)(2,1)S(1)}, bf16[256,256]{1,0:T(8,128)(2,1)S(1)}, u32[]{:S(2)}, u32[]{:S(2)}) collective-permute-start(bf16[256,256]{1,0:T(8,128)(2,1)S(1)} %shard_map.49.refs_0_), channel_id=1, source_target_pairs={{0,12},{1,13},{2,14},{3,15},{4,8},{5,9},{6,10},{7,11},{8,4},{9,5},... | collective-permute-start | bytes 393224 | tf_op jit(solution)/shard_map/ppermute | solution.py:275
  33.9 7.1 %collective-permute-start.7 = (bf16[256,256]{1,0:T(8,128)(2,1)S(1)}, bf16[256,256]{1,0:T(8,128)(2,1)S(1)}, u32[]{:S(2)}, u32[]{:S(2)}) collective-permute-start(bf16[256,256]{1,0:T(8,128)(2,1)S(1)} %shard_map.49.refs_0_), channel_id=1, source_target_pairs={{0,4},{1,5},{2,6},{3,7},{4,0},{5,1},{6,2},{7,3},{8,12},{9,13},{10,... | collective-permute-start | bytes 393224 | tf_op jit(solution)/shard_map/ppermute | solution.py:275
  37.6 3.4 %collective-permute-start.13 = (bf16[256,256]{1,0:T(8,128)(2,1)S(1)}, bf16[256,256]{1,0:T(8,128)(2,1)S(1)}, u32[]{:S(2)}, u32[]{:S(2)}) collective-permute-start(bf16[256,256]{1,0:T(8,128)(2,1)S(1)} %collective-permute-done.12.refs_7_), channel_id=1, source_target_pairs={{0,4},{1,5},{2,6},{3,7},{4,0},{5,1},{6,2},{7,3},{8,12},{9,13},{10,... | collective-permute-start | bytes 393224 | tf_op jit(solution)/shard_map/ppermute | solution.py:275
  40.5 1.3 %collective-permute-start.11 = (bf16[256,256]{1,0:T(8,128)(2,1)S(1)}, bf16[256,256]{1,0:T(8,128)(2,1)S(1)}, u32[]{:S(2)}, u32[]{:S(2)}) collective-permute-start(bf16[256,256]{1,0:T(8,128)(2,1)S(1)} %collective-permute-done.10.refs_5_), channel_id=1, source_target_pairs={{0,4},{1,5},{2,6},{3,7},{4,0},{5,1},{6,2},{7,3},{8,12},{9,13},{10,... | collective-permute-start | bytes 393224 | tf_op jit(solution)/shard_map/ppermute | solution.py:275
  40.7 1.4 %collective-permute-start.9 = (bf16[256,256]{1,0:T(8,128)(2,1)S(1)}, bf16[256,256]{1,0:T(8,128)(2,1)S(1)}, u32[]{:S(2)}, u32[]{:S(2)}) collective-permute-start(bf16[256,256]{1,0:T(8,128)(2,1)S(1)} %collective-permute-done.8.refs_3_), channel_id=1, source_target_pairs={{0,4},{1,5},{2,6},{3,7},{4,0},{5,1},{6,2},{7,3},{8,12},{9,13},{10,... | collective-permute-start | bytes 393224 | tf_op jit(solution)/shard_map/ppermute | solution.py:275

commit v2 on v1

--- a/solution.py
+++ b/solution.py
@@ -28,14 +28,31 @@
     return lax.dot_general(a, b, (dims, ((), ())), preferred_element_type=F32)
 
 
-def local_kernel(cut, idx_hbm, pool_hbm, w_hbm, goal_hbm, *rest):
-    outs, own_ref = rest[:-7], rest[-7]
-    idx_ref, pool_ref, w_ref, goal_ref, x_ref, sems = rest[-6:]
-    parts = len(outs)
+def share_rows(turned_ref, x_ref, distance, out_ref):
+    seg = out_ref.shape[1]
+    target = lax.axis_index("rep") ^ distance
+    held = max(seg, 128)
+    at = pl.multiple_of(target * seg // held * held, held)
+    moved = jnp.dot(turned_ref[...], x_ref[:, pl.ds(at, held)], preferred_element_type=F32)
+    share = moved[:, :seg]
+    for place in range(1, held // seg):
+        own = target % (held // seg) == place
+        share = jnp.where(own, moved[:, place * seg : (place + 1) * seg], share)
+    out_ref[...] = share.astype(BF16)
+
+
+def share_kernel(order, turned_ref, x_ref, *rest):
+    for distance, out_ref in zip(order, rest[-len(order) :]):
+        share_rows(turned_ref, x_ref, distance, out_ref)
+
+
+def local_kernel(cut, partner, idx_hbm, pool_hbm, w_hbm, goal_hbm, *rest):
+    first_ref, own_ref, turned_ref, x_ref = rest[:4]
+    idx_ref, pool_ref, w_ref, goal_ref, sems = rest[4:]
     pool_rows, width = pool_ref.shape
+    seg = own_ref.shape[0]
     total_rows = idx_ref.shape[-1]
     batch = total_rows // STEPS
-    seg = width // parts
     inv_width = 1.0 / math.sqrt(width)
     inv_batch = 1.0 / math.sqrt(batch)
     share = width // LOADS
@@ -109,19 +126,10 @@
                 )
         final.append((grad * (-reach(STEPS - s) * inv_batch)).T.astype(BF16))
 
-    turned = jnp.concatenate(final, axis=1)
-    me = lax.axis_index("rep")
-    own_ref[...] = w_ref[pl.ds(pl.multiple_of(me * seg, seg), seg), :]
-    for distance, out_ref in zip(distances(parts), outs):
-        target = me ^ distance
-        held = max(seg, 128)
-        at = pl.multiple_of(target * seg // held * held, held)
-        moved = jnp.dot(turned, x_ref[:, pl.ds(at, held)], preferred_element_type=F32)
-        share = moved[:, :seg]
-        for place in range(1, held // seg):
-            own = target % (held // seg) == place
-            share = jnp.where(own, moved[:, place * seg : (place + 1) * seg], share)
-        out_ref[...] = share.astype(BF16)
+    turned_ref[...] = jnp.concatenate(final, axis=1)
+    share_rows(turned_ref, x_ref, partner, first_ref)
+    start = pl.multiple_of(lax.axis_index("rep") * seg, seg)
+    own_ref[...] = w_ref[pl.ds(start, seg), :]
 
 
 def distances(parts):
@@ -286,31 +294,52 @@
     far = pl.BlockSpec(memory_space=pltpu.HBM)
     any_place = pl.BlockSpec(memory_space=pl.ANY)
 
+    order = distances(parts)
+    first = order[1]
+
     def local(*refs):
-        local_kernel(cut, *refs)
-
-    order = distances(parts)
-    *sent, own_weights = call(
+        local_kernel(cut, first, *refs)
+
+    rows_out = jax.ShapeDtypeStruct((columns, seg), BF16)
+    out, own_weights, turned, gathered = call(
         local,
-        [jax.ShapeDtypeStruct((columns, seg), BF16)] * parts
-        + [jax.ShapeDtypeStruct((seg, columns), BF16)],
+        [
+            rows_out,
+            jax.ShapeDtypeStruct((seg, columns), BF16),
+            jax.ShapeDtypeStruct((columns, rows), BF16),
+            jax.ShapeDtypeStruct((rows, width), BF16),
+        ],
         [far] * 4,
         [
             pltpu.VMEM((1, rows), jnp.int32),
             pltpu.VMEM((pool_rows, width), BF16),
             pltpu.VMEM((width, columns), BF16),
             pltpu.VMEM((rows, columns), BF16),
-            pltpu.VMEM((rows, width), BF16),
             pltpu.SemaphoreType.DMA((LOADS + 3,)),
         ],
     )(hold(row_index[0]), hold(token_pool[0]), hold(weights[0]), hold(targets[0, 0]))
-    deltas = [value if d == 0 else flipped(value, d) for d, value in zip(order, sent)]
+    leaves = {first: flipped(out, first)}
+    middle = max(2, parts - 3)
+    for group, after in (
+        ([0, *order[2:middle]], []),
+        (order[middle:], [leaves[first]]),
+    ):
+        if not group:
+            continue
+
+        def shares(*refs, group=group):
+            share_kernel(group, *refs)
+
+        made = call(shares, [rows_out] * len(group), [near] * (2 + len(after)))(
+            turned, gathered, *after
+        )
+        for d, out in zip(group, made):
+            leaves[d] = flipped(out, d) if d else out
 
     tall = -(-parts // 8) * 8
     table = jax.ShapeDtypeStruct((tall, 128), F32)
     late = LATE if parts > LATE + 1 else 0
     soon = order[: parts - late]
-    leaves = dict(zip(order, deltas))
 
     def first_gram(*refs):
         gram_kernel(soon, 0, *refs)
@@ -336,7 +365,7 @@
         combine_kernel,
         jax.ShapeDtypeStruct((seg, columns), BF16),
         [near] * (parts + 2),
-    )(gram, own_weights, *deltas)
+    )(gram, own_weights, *(leaves[d] for d in order))
     pieces = [own] + [None] * (parts - 1)
     pieces[1] = flipped(own, 1)
     for d in range(2, parts, 2):

time: 43.2 us -> 42.8 us (level)
  waiting for transfers between devices: 14.7 us -> 11.3 us
  starting transfers between devices: 11.7 us -> 13.7 us
  Pallas kernels: 8.24 us -> 8.7 us
  blocking collectives: 8.37 us -> 8.82 us
    ppermute x14, waiting for transfers between devices: 14.7 us -> 11.3 us  [flipped(): return lax.ppermute(value, ('rep', 'shard'), pairs)]
    ppermute x14, starting transfers between devices: 11.7 us -> 13.7 us  [flipped(): return lax.ppermute(value, ('rep', 'shard'), pairs)]
    pallas_call x1 -> x3, Pallas kernels: 5.16 us -> 5.62 us  [the longest x1 4.79 us: body(): call(local, [rows_out, jax.ShapeDtypeStruct((seg, columns), BF16), jax.Sh...]
    all_to_all x1, blocking collectives: 8.37 us -> 8.82 us  [body(): lax.all_to_all(gram, ('rep', 'shard'), 0, 0, axis_index_groups=groups)]
  transfers between devices with their start and end apart: 14 -> 14, of which waited for: 9 -> 9; matrix products, arithmetic and copies ran while one was open for 0% -> 0% of each run, Pallas kernels for 1% -> 3%
where the time goes in v2:
time: 42.8 us; the launch traced here: 42.6 us
  starting transfers between devices  13.7 us (32%)
  waiting for transfers between devices  11.3 us (26%)
  blocking collectives  8.82 us (21%)
  Pallas kernels  8.7 us (20%)
    ppermute x14, starting transfers between devices, flipped(): return lax.ppermute(value, ('rep', 'shard'), pairs)  13.7 us
    ppermute x14, waiting for transfers between devices, flipped(): return lax.ppermute(value, ('rep', 'shard'), pairs)  11.3 us
    all_to_all x1, blocking collectives, body(): lax.all_to_all(gram, ('rep', 'shard'), 0, 0, axis_index_groups=groups)  8.82 us
    pallas_call x1, Pallas kernels, body(): call(local, [rows_out, jax.ShapeDtypeStruct((seg, columns), BF16), jax.Sh...  4.79 us
    pallas_call x1, Pallas kernels, body(): call(place_kernel, jax.ShapeDtypeStruct((width, columns), BF16), [any_pla...  1.02 us
    pallas_call x1, Pallas kernels, body(): call(combine_kernel, jax.ShapeDtypeStruct((seg, columns), BF16), [near] *...  0.91 us
  transfers between devices with their start and end apart: 14, of which 9 were waited for; matrix products, arithmetic and copies ran while one was open for 0% of the time, Pallas kernels for 3%

profile of v2, /device:TPU:0, one launch (start us, length us, event | category | flops | bytes accessed | tf_op | source)
XLA Modules:
  0.0 42.6 jit_solution(14647430821460605571)
XLA Ops:
  0.0 4.8 %shard_map.46 = (bf16[256,256]{1,0:T(8,128)(2,1)S(1)}, bf16[256,256]{1,0:T(8,128)(2,1)S(1)}, bf16[256,512]{1,0:T(8,128)(2,1)S(1)}, bf16[512,2048]{1,0:T(8,128)(2,1)S(1)}) custom-call(s32[2,1,512]{2,1,0:T(1,128)} %bitcast.8, bf16[384,2048]{1,0:T(8,128)(2,1)} %bitcast.5, bf16[2048,256]{1,0:T(8,128)(2,1)} %bitcast.6, bf16[512,256]{1,0:T(8,128)(2,1)} %bitcast.7), custom_call_target="tpu_custom_call" | custom-call | tf_op jit(solution)/shard_map/pallas_call | solution.py:304
  4.8 4.0 %collective-permute-start = (bf16[256,256]{1,0:T(8,128)(2,1)S(1)}, bf16[256,256]{1,0:T(8,128)(2,1)S(1)}, u32[]{:S(2)}, u32[]{:S(2)}) collective-permute-start(bf16[256,256]{1,0:T(8,128)(2,1)S(1)} %get-tuple-element.19), channel_id=1, source_target_pairs={{0,24},{1,25},{2,26},{3,27},{4,28},{5,29},{6,30},{7,31},{8,16},{9,... | collective-permute-start | bytes 393224 | tf_op jit(solution)/shard_map/ppermute | solution.py:283
  8.8 0.4 %shard_map.47 = (bf16[256,256]{1,0:T(8,128)(2,1)S(1)}, bf16[256,256]{1,0:T(8,128)(2,1)S(1)}, bf16[256,256]{1,0:T(8,128)(2,1)S(1)}, bf16[256,256]{1,0:T(8,128)(2,1)S(1)}) custom-call(bf16[256,512]{1,0:T(8,128)(2,1)S(1)} %get-tuple-element.16.refs_0_, bf16[512,2048]{1,0:T(8,128)(2,1)S(1)} %get-tuple-element.17.refs_1_), custom_call_target="tpu_custom_call" | custom-call | tf_op jit(solution)/shard_map/pallas_call | solution.py:333
  9.2 0.6 %collective-permute-start.1 = (bf16[256,256]{1,0:T(8,128)(2,1)S(1)}, bf16[256,256]{1,0:T(8,128)(2,1)S(1)}, u32[]{:S(2)}, u32[]{:S(2)}) collective-permute-start(bf16[256,256]{1,0:T(8,128)(2,1)S(1)} %get-tuple-element.20), channel_id=1, source_target_pairs={{0,8},{1,9},{2,10},{3,11},{4,12},{5,13},{6,14},{7,15},{8,0},{9,1},... | collective-permute-start | bytes 393224 | tf_op jit(solution)/shard_map/ppermute | solution.py:283
  9.8 0.1 collective-permute-start.2
  9.9 1.5 %collective-permute-start.3 = (bf16[256,256]{1,0:T(8,128)(2,1)S(1)}, bf16[256,256]{1,0:T(8,128)(2,1)S(1)}, u32[]{:S(2)}, u32[]{:S(2)}) collective-permute-start(bf16[256,256]{1,0:T(8,128)(2,1)S(1)} %get-tuple-element.22), channel_id=1, source_target_pairs={{0,28},{1,29},{2,30},{3,31},{4,24},{5,25},{6,26},{7,27},{8,20},{9,... | collective-permute-start | bytes 393224 | tf_op jit(solution)/shard_map/ppermute | solution.py:283
  11.4 1.7 %collective-permute-done.refs_2_.refs_1_.rest_1_ = bf16[256,256]{1,0:T(8,128)(2,1)S(1)} collective-permute-done((bf16[256,256]{1,0:T(8,128)(2,1)S(1)}, bf16[256,256]{1,0:T(8,128)(2,1)S(1)}, u32[]{:S(2)}, u32[]{:S(2)}) %collective-permute-start) | collective-permute-done | bytes 131104 | tf_op jit(solution)/shard_map/ppermute | solution.py:283
  13.1 0.4 shard_map.48
  13.5 0.1 collective-permute-start.4
  13.6 3.2 %collective-permute-start.5 = (bf16[256,256]{1,0:T(8,128)(2,1)S(1)}, bf16[256,256]{1,0:T(8,128)(2,1)S(1)}, u32[]{:S(2)}, u32[]{:S(2)}) collective-permute-start(bf16[256,256]{1,0:T(8,128)(2,1)S(1)} %get-tuple-element.24), channel_id=1, source_target_pairs={{0,20},{1,21},{2,22},{3,23},{4,16},{5,17},{6,18},{7,19},{8,28},{9,... | collective-permute-start | bytes 393224 | tf_op jit(solution)/shard_map/ppermute | solution.py:283
  16.8 0.0 collective-permute-done.1.refs_2_.rest_2_
  16.8 0.0 collective-permute-start.6
  16.8 1.2 %collective-permute-done.2.refs_3_.rest_3_ = bf16[256,256]{1,0:T(8,128)(2,1)S(1)} collective-permute-done((bf16[256,256]{1,0:T(8,128)(2,1)S(1)}, bf16[256,256]{1,0:T(8,128)(2,1)S(1)}, u32[]{:S(2)}, u32[]{:S(2)}) %collective-permute-start.2) | collective-permute-done | bytes 131104 | tf_op jit(solution)/shard_map/ppermute | solution.py:283
  18.0 0.1 collective-permute-done.3.refs_4_.rest_4_
  18.1 0.5 %shard_map.49.refs_8_ = f32[8,128]{1,0:T(8,128)S(1)} custom-call(bf16[256,256]{1,0:T(8,128)(2,1)S(1)} %get-tuple-element.18.refs_0_.rest_0_, bf16[256,256]{1,0:T(8,128)(2,1)S(1)} %collective-permute-done.refs_2_.refs_1_.rest_1_, bf16[256,256]{1,0:T(8,128)(2,1)S(1)} %collective-permute-done.1.refs_2_.rest_2_, ...), custom_call_target="tpu_custom_call" | custom-call | tf_op jit(solution)/shard_map/pallas_call | solution.py:350
  18.6 1.4 %collective-permute-done.4.refs_5_.rest_5_ = bf16[256,256]{1,0:T(8,128)(2,1)S(1)} collective-permute-done((bf16[256,256]{1,0:T(8,128)(2,1)S(1)}, bf16[256,256]{1,0:T(8,128)(2,1)S(1)}, u32[]{:S(2)}, u32[]{:S(2)}) %collective-permute-start.4) | collective-permute-done | bytes 131104 | tf_op jit(solution)/shard_map/ppermute | solution.py:283
  19.9 0.1 collective-permute-done.5.refs_6_.rest_6_
  20.1 0.0 collective-permute-done.6.refs_7_.rest_7_
  20.1 0.7 %shard_map.50 = f32[8,128]{1,0:T(8,128)S(1)} custom-call(bf16[256,256]{1,0:T(8,128)(2,1)S(1)} %get-tuple-element.18.refs_0_.rest_0_, bf16[256,256]{1,0:T(8,128)(2,1)S(1)} %collective-permute-done.refs_2_.refs_1_.rest_1_, bf16[256,256]{1,0:T(8,128)(2,1)S(1)} %collective-permute-done.1.refs_2_.rest_2_, ...), custom_call_target="tpu_custom_call" | custom-call | tf_op jit(solution)/shard_map/pallas_call | solution.py:352
  20.8 8.8 %all_to_all.5.gram_ref = f32[16,8,128]{2,1,0:T(8,128)S(1)} all-to-all(f32[16,8,128]{2,1,0:T(8,128)S(1)} %broadcast_in_dim.6), channel_id=1, replica_groups={{29,28,25,24,21,20,17,16,13,12,9,8,5,4,1,0},{31,30,27,26,23,22,19,18,15..., dimensions={0} | all-to-all | bytes 131072 | tf_op jit(solution)/shard_map/all_to_all | solution.py:362
  29.6 0.9 %shard_map.51.refs_0_ = bf16[256,256]{1,0:T(8,128)(2,1)S(1)} custom-call(f32[16,8,128]{2,1,0:T(8,128)S(1)} %all_to_all.5.gram_ref, bf16[256,256]{1,0:T(8,128)(2,1)S(1)} %get-tuple-element.26.own_ref, bf16[256,256]{1,0:T(8,128)(2,1)S(1)} %get-tuple-element.18.refs_0_.rest_0_, bf16[256,256]{1,0:T(8,128)(2,1)S(1)} %collective-permute-done.refs_2_.refs_1_.rest_1_, ...), custom_call_target="tpu_custom_call" | custom-call | tf_op jit(solution)/shard_map/pallas_call | solution.py:364
  30.5 2.0 %collective-permute-start.12 = (bf16[256,256]{1,0:T(8,128)(2,1)S(1)}, bf16[256,256]{1,0:T(8,128)(2,1)S(1)}, u32[]{:S(2)}, u32[]{:S(2)}) collective-permute-start(bf16[256,256]{1,0:T(8,128)(2,1)S(1)} %shard_map.51.refs_0_), channel_id=1, source_target_pairs={{0,28},{1,29},{2,30},{3,31},{4,24},{5,25},{6,26},{7,27},{8,20},{9,... | collective-permute-start | bytes 393224 | tf_op jit(solution)/shard_map/ppermute | solution.py:283
  32.5 0.8 %collective-permute-start.10 = (bf16[256,256]{1,0:T(8,128)(2,1)S(1)}, bf16[256,256]{1,0:T(8,128)(2,1)S(1)}, u32[]{:S(2)}, u32[]{:S(2)}) collective-permute-start(bf16[256,256]{1,0:T(8,128)(2,1)S(1)} %shard_map.51.refs_0_), channel_id=1, source_target_pairs={{0,20},{1,21},{2,22},{3,23},{4,16},{5,17},{6,18},{7,19},{8,28},{9,... | collective-permute-start | bytes 393224 | tf_op jit(solution)/shard_map/ppermute | solution.py:283
  33.2 0.2 collective-permute-start.8
  33.5 0.4 %collective-permute-start.7 = (bf16[256,256]{1,0:T(8,128)(2,1)S(1)}, bf16[256,256]{1,0:T(8,128)(2,1)S(1)}, u32[]{:S(2)}, u32[]{:S(2)}) collective-permute-start(bf16[256,256]{1,0:T(8,128)(2,1)S(1)} %shard_map.51.refs_0_), channel_id=1, source_target_pairs={{0,4},{1,5},{2,6},{3,7},{4,0},{5,1},{6,2},{7,3},{8,12},{9,13},{10,... | collective-permute-start | bytes 393224 | tf_op jit(solution)/shard_map/ppermute | solution.py:283
  33.9 3.1 %collective-permute-done.12.refs_7_ = bf16[256,256]{1,0:T(8,128)(2,1)S(1)} collective-permute-done((bf16[256,256]{1,0:T(8,128)(2,1)S(1)}, bf16[256,256]{1,0:T(8,128)(2,1)S(1)}, u32[]{:S(2)}, u32[]{:S(2)}) %collective-permute-start.12) | collective-permute-done | bytes 131104 | tf_op jit(solution)/shard_map/ppermute | solution.py:283
  37.1 0.3 collective-permute-start.13
  37.4 2.6 %collective-permute-done.10.refs_5_ = bf16[256,256]{1,0:T(8,128)(2,1)S(1)} collective-permute-done((bf16[256,256]{1,0:T(8,128)(2,1)S(1)}, bf16[256,256]{1,0:T(8,128)(2,1)S(1)}, u32[]{:S(2)}, u32[]{:S(2)}) %collective-permute-start.10) | collective-permute-done | bytes 131104 | tf_op jit(solution)/shard_map/ppermute | solution.py:283
  40.0 0.2 collective-permute-start.11
  40.2 0.0 collective-permute-done.8.refs_3_
  40.2 0.3 collective-permute-start.9
  40.5 0.0 collective-permute-done.7.refs_1_
  40.5 0.0 collective-permute-done.13.refs_6_
  40.5 0.8 %collective-permute-done.11.refs_4_ = bf16[256,256]{1,0:T(8,128)(2,1)S(1)} collective-permute-done((bf16[256,256]{1,0:T(8,128)(2,1)S(1)}, bf16[256,256]{1,0:T(8,128)(2,1)S(1)}, u32[]{:S(2)}, u32[]{:S(2)}) %collective-permute-start.11) | collective-permute-done | bytes 131104 | tf_op jit(solution)/shard_map/ppermute | solution.py:283
  41.4 0.2 collective-permute-done.9.refs_2_
  41.5 1.0 %shard_map.52 = bf16[2048,256]{1,0:T(8,128)(2,1)} custom-call(bf16[256,256]{1,0:T(8,128)(2,1)S(1)} %shard_map.51.refs_0_, bf16[256,256]{1,0:T(8,128)(2,1)S(1)} %collective-permute-done.7.refs_1_, bf16[256,256]{1,0:T(8,128)(2,1)S(1)} %collective-permute-done.9.refs_2_, bf16[256,256]{1,0:T(8,128)(2,1)S(1)} %collective-permute-done.8.refs_3_, ...), custom_call_target="tpu_custom_call" | custom-call | tf_op jit(solution)/shard_map/pallas_call | solution.py:374
  (1 shorter events, 0.0 us)
Async XLA Ops:
  4.8 8.3 %collective-permute-start = (bf16[256,256]{1,0:T(8,128)(2,1)S(1)}, bf16[256,256]{1,0:T(8,128)(2,1)S(1)}, u32[]{:S(2)}, u32[]{:S(2)}) collective-permute-start(bf16[256,256]{1,0:T(8,128)(2,1)S(1)} %get-tuple-element.19), channel_id=1, source_target_pairs={{0,24},{1,25},{2,26},{3,27},{4,28},{5,29},{6,30},{7,31},{8,16},{9,... | collective-permute-start | bytes 393224 | tf_op jit(solution)/shard_map/ppermute | solution.py:283
  9.2 7.6 %collective-permute-start.1 = (bf16[256,256]{1,0:T(8,128)(2,1)S(1)}, bf16[256,256]{1,0:T(8,128)(2,1)S(1)}, u32[]{:S(2)}, u32[]{:S(2)}) collective-permute-start(bf16[256,256]{1,0:T(8,128)(2,1)S(1)} %get-tuple-element.20), channel_id=1, source_target_pairs={{0,8},{1,9},{2,10},{3,11},{4,12},{5,13},{6,14},{7,15},{8,0},{9,1},... | collective-permute-start | bytes 393224 | tf_op jit(solution)/shard_map/ppermute | solution.py:283
  9.8 8.2 %collective-permute-start.2 = (bf16[256,256]{1,0:T(8,128)(2,1)S(1)}, bf16[256,256]{1,0:T(8,128)(2,1)S(1)}, u32[]{:S(2)}, u32[]{:S(2)}) collective-permute-start(bf16[256,256]{1,0:T(8,128)(2,1)S(1)} %get-tuple-element.21), channel_id=1, source_target_pairs={{0,16},{1,17},{2,18},{3,19},{4,20},{5,21},{6,22},{7,23},{8,24},{9,... | collective-permute-start | bytes 393224 | tf_op jit(solution)/shard_map/ppermute | solution.py:283
  9.9 8.2 %collective-permute-start.3 = (bf16[256,256]{1,0:T(8,128)(2,1)S(1)}, bf16[256,256]{1,0:T(8,128)(2,1)S(1)}, u32[]{:S(2)}, u32[]{:S(2)}) collective-permute-start(bf16[256,256]{1,0:T(8,128)(2,1)S(1)} %get-tuple-element.22), channel_id=1, source_target_pairs={{0,28},{1,29},{2,30},{3,31},{4,24},{5,25},{6,26},{7,27},{8,20},{9,... | collective-permute-start | bytes 393224 | tf_op jit(solution)/shard_map/ppermute | solution.py:283
  13.5 6.5 %collective-permute-start.4 = (bf16[256,256]{1,0:T(8,128)(2,1)S(1)}, bf16[256,256]{1,0:T(8,128)(2,1)S(1)}, u32[]{:S(2)}, u32[]{:S(2)}) collective-permute-start(bf16[256,256]{1,0:T(8,128)(2,1)S(1)} %get-tuple-element.23), channel_id=1, source_target_pairs={{0,12},{1,13},{2,14},{3,15},{4,8},{5,9},{6,10},{7,11},{8,4},{9,5},... | collective-permute-start | bytes 393224 | tf_op jit(solution)/shard_map/ppermute | solution.py:283
  13.6 6.5 %collective-permute-start.5 = (bf16[256,256]{1,0:T(8,128)(2,1)S(1)}, bf16[256,256]{1,0:T(8,128)(2,1)S(1)}, u32[]{:S(2)}, u32[]{:S(2)}) collective-permute-start(bf16[256,256]{1,0:T(8,128)(2,1)S(1)} %get-tuple-element.24), channel_id=1, source_target_pairs={{0,20},{1,21},{2,22},{3,23},{4,16},{5,17},{6,18},{7,19},{8,28},{9,... | collective-permute-start | bytes 393224 | tf_op jit(solution)/shard_map/ppermute | solution.py:283
  16.8 3.3 %collective-permute-start.6 = (bf16[256,256]{1,0:T(8,128)(2,1)S(1)}, bf16[256,256]{1,0:T(8,128)(2,1)S(1)}, u32[]{:S(2)}, u32[]{:S(2)}) collective-permute-start(bf16[256,256]{1,0:T(8,128)(2,1)S(1)} %get-tuple-element.25), channel_id=1, source_target_pairs={{0,4},{1,5},{2,6},{3,7},{4,0},{5,1},{6,2},{7,3},{8,12},{9,13},{10,... | collective-permute-start | bytes 393224 | tf_op jit(solution)/shard_map/ppermute | solution.py:283
  30.5 6.6 %collective-permute-start.12 = (bf16[256,256]{1,0:T(8,128)(2,1)S(1)}, bf16[256,256]{1,0:T(8,128)(2,1)S(1)}, u32[]{:S(2)}, u32[]{:S(2)}) collective-permute-start(bf16[256,256]{1,0:T(8,128)(2,1)S(1)} %shard_map.51.refs_0_), channel_id=1, source_target_pairs={{0,28},{1,29},{2,30},{3,31},{4,24},{5,25},{6,26},{7,27},{8,20},{9,... | collective-permute-start | bytes 393224 | tf_op jit(solution)/shard_map/ppermute | solution.py:283
  32.5 7.5 %collective-permute-start.10 = (bf16[256,256]{1,0:T(8,128)(2,1)S(1)}, bf16[256,256]{1,0:T(8,128)(2,1)S(1)}, u32[]{:S(2)}, u32[]{:S(2)}) collective-permute-start(bf16[256,256]{1,0:T(8,128)(2,1)S(1)} %shard_map.51.refs_0_), channel_id=1, source_target_pairs={{0,20},{1,21},{2,22},{3,23},{4,16},{5,17},{6,18},{7,19},{8,28},{9,... | collective-permute-start | bytes 393224 | tf_op jit(solution)/shard_map/ppermute | solution.py:283
  33.2 6.9 %collective-permute-start.8 = (bf16[256,256]{1,0:T(8,128)(2,1)S(1)}, bf16[256,256]{1,0:T(8,128)(2,1)S(1)}, u32[]{:S(2)}, u32[]{:S(2)}) collective-permute-start(bf16[256,256]{1,0:T(8,128)(2,1)S(1)} %shard_map.51.refs_0_), channel_id=1, source_target_pairs={{0,12},{1,13},{2,14},{3,15},{4,8},{5,9},{6,10},{7,11},{8,4},{9,5},... | collective-permute-start | bytes 393224 | tf_op jit(solution)/shard_map/ppermute | solution.py:283
  33.5 7.0 %collective-permute-start.7 = (bf16[256,256]{1,0:T(8,128)(2,1)S(1)}, bf16[256,256]{1,0:T(8,128)(2,1)S(1)}, u32[]{:S(2)}, u32[]{:S(2)}) collective-permute-start(bf16[256,256]{1,0:T(8,128)(2,1)S(1)} %shard_map.51.refs_0_), channel_id=1, source_target_pairs={{0,4},{1,5},{2,6},{3,7},{4,0},{5,1},{6,2},{7,3},{8,12},{9,13},{10,... | collective-permute-start | bytes 393224 | tf_op jit(solution)/shard_map/ppermute | solution.py:283
  37.1 3.5 %collective-permute-start.13 = (bf16[256,256]{1,0:T(8,128)(2,1)S(1)}, bf16[256,256]{1,0:T(8,128)(2,1)S(1)}, u32[]{:S(2)}, u32[]{:S(2)}) collective-permute-start(bf16[256,256]{1,0:T(8,128)(2,1)S(1)} %collective-permute-done.12.refs_7_), channel_id=1, source_target_pairs={{0,4},{1,5},{2,6},{3,7},{4,0},{5,1},{6,2},{7,3},{8,12},{9,13},{10,... | collective-permute-start | bytes 393224 | tf_op jit(solution)/shard_map/ppermute | solution.py:283
  40.0 1.3 %collective-permute-start.11 = (bf16[256,256]{1,0:T(8,128)(2,1)S(1)}, bf16[256,256]{1,0:T(8,128)(2,1)S(1)}, u32[]{:S(2)}, u32[]{:S(2)}) collective-permute-start(bf16[256,256]{1,0:T(8,128)(2,1)S(1)} %collective-permute-done.10.refs_5_), channel_id=1, source_target_pairs={{0,4},{1,5},{2,6},{3,7},{4,0},{5,1},{6,2},{7,3},{8,12},{9,13},{10,... | collective-permute-start | bytes 393224 | tf_op jit(solution)/shard_map/ppermute | solution.py:283
  40.2 1.4 %collective-permute-start.9 = (bf16[256,256]{1,0:T(8,128)(2,1)S(1)}, bf16[256,256]{1,0:T(8,128)(2,1)S(1)}, u32[]{:S(2)}, u32[]{:S(2)}) collective-permute-start(bf16[256,256]{1,0:T(8,128)(2,1)S(1)} %collective-permute-done.8.refs_3_), channel_id=1, source_target_pairs={{0,4},{1,5},{2,6},{3,7},{4,0},{5,1},{6,2},{7,3},{8,12},{9,13},{10,... | collective-permute-start | bytes 393224 | tf_op jit(solution)/shard_map/ppermute | solution.py:283

commit v3 on v2

--- a/solution.py
+++ b/solution.py
@@ -143,7 +143,7 @@
     return [(i, j) for i in range(count) for j in range(i, count)]
 
 
-def gram_kernel(order, known, *refs):
+def gram_kernel(parts, order, known, *refs):
     count = len(order)
     deltas, before, out_ref = refs[:count], refs[count:-1], refs[-1]
     rows, seg = deltas[0].shape
@@ -152,7 +152,7 @@
     tall = 16
     me = lax.axis_index("rep")
     down = lax.broadcasted_iota(jnp.int32, out_ref.shape, 0)
-    across = lax.broadcasted_iota(jnp.int32, out_ref.shape, 1)
+    spots = down * 128 + lax.broadcasted_iota(jnp.int32, out_ref.shape, 1)
     table = before[0][...] if before else jnp.zeros(out_ref.shape, F32)
     for first in range(0, count, block):
         for second in range(first, count, block):
@@ -180,12 +180,12 @@
                 return tuple(sums)
 
             zeros = tuple(jnp.zeros((8, lanes), F32) for _ in pairs)
-            sums = lax.fori_loop(0, rows // tall, step, zeros)
+            sums = lax.fori_loop(0, rows // tall, step, zeros, unroll=4 if count <= block else 1)
             for n, (i, j) in enumerate(pairs):
                 value = jnp.sum(jnp.sum(sums[n], axis=0, keepdims=True), axis=1, keepdims=True)
                 mine, other = me ^ order[i], me ^ order[j]
-                spot = ((down == mine) & (across == other)) | ((down == other) & (across == mine))
-                table = jnp.where(spot, value, table)
+                here = (spots == mine * parts + other) | (spots == other * parts + mine)
+                table = jnp.where(here, value, table)
     out_ref[...] = table
 
 
@@ -230,7 +230,10 @@
     table = gram_ref[0]
     for member in range(1, gram_ref.shape[0]):
         table = table + gram_ref[member]
-    gram = {(i, j): table[i : i + 1, j : j + 1] for i, j in pair_list(count)}
+    gram = {}
+    for i, j in pair_list(count):
+        down, across = divmod(i * count + j, 128)
+        gram[i, j] = table[down : down + 1, across : across + 1]
     weights = tree_weights(gram, count)
     total = None
     for distance, delta in zip(distances(count), deltas):
@@ -319,7 +322,7 @@
         ],
     )(hold(row_index[0]), hold(token_pool[0]), hold(weights[0]), hold(targets[0, 0]))
     leaves = {first: flipped(out, first)}
-    middle = max(2, parts - 3)
+    middle = max(2, parts - 2)
     for group, after in (
         ([0, *order[2:middle]], []),
         (order[middle:], [leaves[first]]),
@@ -336,22 +339,19 @@
         for d, out in zip(group, made):
             leaves[d] = flipped(out, d) if d else out
 
-    tall = -(-parts // 8) * 8
-    table = jax.ShapeDtypeStruct((tall, 128), F32)
-    late = LATE if parts > LATE + 1 else 0
-    soon = order[: parts - late]
-
-    def first_gram(*refs):
-        gram_kernel(soon, 0, *refs)
-
-    def full_gram(*refs):
-        gram_kernel(order, len(soon), *refs)
-
-    gram = call(first_gram, table, [near] * len(soon))(*(leaves[d] for d in soon))
-    if late:
-        gram = call(full_gram, table, [near] * (parts + 1))(
-            *(leaves[d] for d in order), gram
-        )
+    table = jax.ShapeDtypeStruct((-(-parts * parts // 128), 128), F32)
+    gram, known = [], 0
+    for reached in (parts - 3, parts - 2, parts):
+        if reached <= known:
+            continue
+        taken = order[:reached]
+
+        def products(*refs, taken=taken, known=known):
+            gram_kernel(parts, taken, known, *refs)
+
+        inputs = [leaves[d] for d in taken] + gram
+        gram, known = [call(products, table, [near] * len(inputs))(*inputs)], reached
+    gram = gram[0]
     shards = lax.axis_size("shard")
     groups = [
         [i * shards + j for i in range(parts) for j in range(first, first + cut)]

time: 42.8 us -> 42.3 us (0.988)
  waiting for transfers between devices: 11.3 us -> 13.7 us
  starting transfers between devices: 13.7 us -> 11.8 us
  blocking collectives: 8.82 us -> 7.84 us
    ppermute x14, waiting for transfers between devices: 11.3 us -> 13.7 us  [flipped(): return lax.ppermute(value, ('rep', 'shard'), pairs)]
    ppermute x14, starting transfers between devices: 13.7 us -> 11.8 us  [flipped(): return lax.ppermute(value, ('rep', 'shard'), pairs)]
    all_to_all x1, blocking collectives: 8.82 us -> 7.84 us  [body(): lax.all_to_all(gram, ('rep', 'shard'), 0, 0, axis_index_groups=groups)]
    pallas_call x2 -> x3, Pallas kernels: 1.15 us -> 1.11 us  [body(): call(products, table, [near] * len(inputs))(*inputs)]
  transfers between devices with their start and end apart: 14 -> 14, of which waited for: 9 -> 9; matrix products, arithmetic and copies ran while one was open for 0% -> 0% of each run, Pallas kernels for 3% -> 4%
where the time goes in v3:
time: 42.3 us; the launch traced here: 42.1 us
  waiting for transfers between devices  13.7 us (32%)
  starting transfers between devices  11.8 us (28%)
  Pallas kernels  8.63 us (20%)
  blocking collectives  7.84 us (19%)
    ppermute x14, waiting for transfers between devices, flipped(): return lax.ppermute(value, ('rep', 'shard'), pairs)  13.7 us
    ppermute x14, starting transfers between devices, flipped(): return lax.ppermute(value, ('rep', 'shard'), pairs)  11.8 us
    all_to_all x1, blocking collectives, body(): lax.all_to_all(gram, ('rep', 'shard'), 0, 0, axis_index_groups=groups)  7.84 us
    pallas_call x1, Pallas kernels, body(): call(local, [rows_out, jax.ShapeDtypeStruct((seg, columns), BF16), jax.Sh...  4.79 us
    pallas_call x3, Pallas kernels, body(): call(products, table, [near] * len(inputs))(*inputs)  1.11 us
    pallas_call x1, Pallas kernels, body(): call(place_kernel, jax.ShapeDtypeStruct((width, columns), BF16), [any_pla...  1.02 us
    pallas_call x1, Pallas kernels, body(): call(combine_kernel, jax.ShapeDtypeStruct((seg, columns), BF16), [near] *...  0.87 us
  transfers between devices with their start and end apart: 14, of which 9 were waited for; matrix products, arithmetic and copies ran while one was open for 0% of the time, Pallas kernels for 4%

profile of v3, /device:TPU:0, one launch (start us, length us, event | category | flops | bytes accessed | tf_op | source)
XLA Modules:
  0.0 42.1 jit_solution(5806283974330364342)
XLA Ops:
  0.0 4.8 %shard_map.46 = (bf16[256,256]{1,0:T(8,128)(2,1)S(1)}, bf16[256,256]{1,0:T(8,128)(2,1)S(1)}, bf16[256,512]{1,0:T(8,128)(2,1)S(1)}, bf16[512,2048]{1,0:T(8,128)(2,1)S(1)}) custom-call(s32[2,1,512]{2,1,0:T(1,128)} %bitcast.10, bf16[384,2048]{1,0:T(8,128)(2,1)} %bitcast.7, bf16[2048,256]{1,0:T(8,128)(2,1)} %bitcast.8, bf16[512,256]{1,0:T(8,128)(2,1)} %bitcast.9), custom_call_target="tpu_custom_call" | custom-call | tf_op jit(solution)/shard_map/pallas_call | solution.py:307
  4.8 4.0 %collective-permute-start = (bf16[256,256]{1,0:T(8,128)(2,1)S(1)}, bf16[256,256]{1,0:T(8,128)(2,1)S(1)}, u32[]{:S(2)}, u32[]{:S(2)}) collective-permute-start(bf16[256,256]{1,0:T(8,128)(2,1)S(1)} %get-tuple-element.19), channel_id=1, source_target_pairs={{0,24},{1,25},{2,26},{3,27},{4,28},{5,29},{6,30},{7,31},{8,16},{9,... | collective-permute-start | bytes 393224 | tf_op jit(solution)/shard_map/ppermute | solution.py:286
  8.8 0.5 %shard_map.47 = (bf16[256,256]{1,0:T(8,128)(2,1)S(1)}, bf16[256,256]{1,0:T(8,128)(2,1)S(1)}, bf16[256,256]{1,0:T(8,128)(2,1)S(1)}, bf16[256,256]{1,0:T(8,128)(2,1)S(1)}, bf16[256,256]{1,0:T(8,128)(2,1)S(1)}) custom-call(bf16[256,512]{1,0:T(8,128)(2,1)S(1)} %get-tuple-element.16.refs_0_, bf16[512,2048]{1,0:T(8,128)(2,1)S(1)} %get-tuple-element.17.refs_1_), custom_call_target="tpu_custom_call" | custom-call | tf_op jit(solution)/shard_map/pallas_call | solution.py:336
  9.3 0.6 %collective-permute-start.1 = (bf16[256,256]{1,0:T(8,128)(2,1)S(1)}, bf16[256,256]{1,0:T(8,128)(2,1)S(1)}, u32[]{:S(2)}, u32[]{:S(2)}) collective-permute-start(bf16[256,256]{1,0:T(8,128)(2,1)S(1)} %get-tuple-element.20), channel_id=1, source_target_pairs={{0,8},{1,9},{2,10},{3,11},{4,12},{5,13},{6,14},{7,15},{8,0},{9,1},... | collective-permute-start | bytes 393224 | tf_op jit(solution)/shard_map/ppermute | solution.py:286
  9.9 0.1 collective-permute-start.2
  9.9 1.5 %collective-permute-start.3 = (bf16[256,256]{1,0:T(8,128)(2,1)S(1)}, bf16[256,256]{1,0:T(8,128)(2,1)S(1)}, u32[]{:S(2)}, u32[]{:S(2)}) collective-permute-start(bf16[256,256]{1,0:T(8,128)(2,1)S(1)} %get-tuple-element.22), channel_id=1, source_target_pairs={{0,28},{1,29},{2,30},{3,31},{4,24},{5,25},{6,26},{7,27},{8,20},{9,... | collective-permute-start | bytes 393224 | tf_op jit(solution)/shard_map/ppermute | solution.py:286
  11.4 1.7 %collective-permute-start.4 = (bf16[256,256]{1,0:T(8,128)(2,1)S(1)}, bf16[256,256]{1,0:T(8,128)(2,1)S(1)}, u32[]{:S(2)}, u32[]{:S(2)}) collective-permute-start(bf16[256,256]{1,0:T(8,128)(2,1)S(1)} %get-tuple-element.23), channel_id=1, source_target_pairs={{0,12},{1,13},{2,14},{3,15},{4,8},{5,9},{6,10},{7,11},{8,4},{9,5},... | collective-permute-start | bytes 393224 | tf_op jit(solution)/shard_map/ppermute | solution.py:286
  13.1 0.0 collective-permute-done.refs_2_.refs_1_.rest_1_
  13.1 0.3 shard_map.48
  13.4 0.1 collective-permute-start.5
  13.5 2.7 %collective-permute-done.1.refs_2_.rest_2_ = bf16[256,256]{1,0:T(8,128)(2,1)S(1)} collective-permute-done((bf16[256,256]{1,0:T(8,128)(2,1)S(1)}, bf16[256,256]{1,0:T(8,128)(2,1)S(1)}, u32[]{:S(2)}, u32[]{:S(2)}) %collective-permute-start.1) | collective-permute-done | bytes 131104 | tf_op jit(solution)/shard_map/ppermute | solution.py:286
  16.2 0.0 collective-permute-start.6
  16.2 1.1 %collective-permute-done.2.refs_3_.rest_3_ = bf16[256,256]{1,0:T(8,128)(2,1)S(1)} collective-permute-done((bf16[256,256]{1,0:T(8,128)(2,1)S(1)}, bf16[256,256]{1,0:T(8,128)(2,1)S(1)}, u32[]{:S(2)}, u32[]{:S(2)}) %collective-permute-start.2) | collective-permute-done | bytes 131104 | tf_op jit(solution)/shard_map/ppermute | solution.py:286
  17.3 0.8 %collective-permute-done.3.refs_4_.rest_4_ = bf16[256,256]{1,0:T(8,128)(2,1)S(1)} collective-permute-done((bf16[256,256]{1,0:T(8,128)(2,1)S(1)}, bf16[256,256]{1,0:T(8,128)(2,1)S(1)}, u32[]{:S(2)}, u32[]{:S(2)}) %collective-permute-start.3) | collective-permute-done | bytes 131104 | tf_op jit(solution)/shard_map/ppermute | solution.py:286
  18.1 0.4 shard_map.49.refs_6_
  18.5 1.6 %collective-permute-done.4.refs_5_.rest_5_ = bf16[256,256]{1,0:T(8,128)(2,1)S(1)} collective-permute-done((bf16[256,256]{1,0:T(8,128)(2,1)S(1)}, bf16[256,256]{1,0:T(8,128)(2,1)S(1)}, u32[]{:S(2)}, u32[]{:S(2)}) %collective-permute-start.4) | collective-permute-done | bytes 131104 | tf_op jit(solution)/shard_map/ppermute | solution.py:286
  20.1 0.3 shard_map.50.refs_8_
  20.3 0.5 %collective-permute-done.5.refs_6_.rest_6_ = bf16[256,256]{1,0:T(8,128)(2,1)S(1)} collective-permute-done((bf16[256,256]{1,0:T(8,128)(2,1)S(1)}, bf16[256,256]{1,0:T(8,128)(2,1)S(1)}, u32[]{:S(2)}, u32[]{:S(2)}) %collective-permute-start.5) | collective-permute-done | bytes 131104 | tf_op jit(solution)/shard_map/ppermute | solution.py:286
  20.8 0.0 collective-permute-done.6.refs_7_.rest_7_
  20.8 0.4 %shard_map.51 = f32[1,128]{1,0:T(1,128)S(1)} custom-call(bf16[256,256]{1,0:T(8,128)(2,1)S(1)} %get-tuple-element.18.refs_0_.rest_0_, bf16[256,256]{1,0:T(8,128)(2,1)S(1)} %collective-permute-done.refs_2_.refs_1_.rest_1_, bf16[256,256]{1,0:T(8,128)(2,1)S(1)} %collective-permute-done.1.refs_2_.rest_2_, ...), custom_call_target="tpu_custom_call" | custom-call | tf_op jit(solution)/shard_map/pallas_call | solution.py:353
  21.3 7.8 %all_to_all.5.gram_ref = f32[16,1,128]{2,1,0:T(1,128)S(1)} all-to-all(f32[16,1,128]{2,1,0:T(1,128)S(1)} %broadcast_in_dim.6), channel_id=1, replica_groups={{29,28,25,24,21,20,17,16,13,12,9,8,5,4,1,0},{31,30,27,26,23,22,19,18,15..., dimensions={0} | all-to-all | bytes 16384 | tf_op jit(solution)/shard_map/all_to_all | solution.py:362
  29.1 0.9 %shard_map.52.refs_0_ = bf16[256,256]{1,0:T(8,128)(2,1)S(1)} custom-call(f32[16,1,128]{2,1,0:T(1,128)S(1)} %all_to_all.5.gram_ref, bf16[256,256]{1,0:T(8,128)(2,1)S(1)} %get-tuple-element.26.own_ref, bf16[256,256]{1,0:T(8,128)(2,1)S(1)} %get-tuple-element.18.refs_0_.rest_0_, bf16[256,256]{1,0:T(8,128)(2,1)S(1)} %collective-permute-done.refs_2_.refs_1_.rest_1_, ...), custom_call_target="tpu_custom_call" | custom-call | tf_op jit(solution)/shard_map/pallas_call | solution.py:364
  30.0 1.9 %collective-permute-start.12 = (bf16[256,256]{1,0:T(8,128)(2,1)S(1)}, bf16[256,256]{1,0:T(8,128)(2,1)S(1)}, u32[]{:S(2)}, u32[]{:S(2)}) collective-permute-start(bf16[256,256]{1,0:T(8,128)(2,1)S(1)} %shard_map.52.refs_0_), channel_id=1, source_target_pairs={{0,28},{1,29},{2,30},{3,31},{4,24},{5,25},{6,26},{7,27},{8,20},{9,... | collective-permute-start | bytes 393224 | tf_op jit(solution)/shard_map/ppermute | solution.py:286
  31.9 0.9 %collective-permute-start.10 = (bf16[256,256]{1,0:T(8,128)(2,1)S(1)}, bf16[256,256]{1,0:T(8,128)(2,1)S(1)}, u32[]{:S(2)}, u32[]{:S(2)}) collective-permute-start(bf16[256,256]{1,0:T(8,128)(2,1)S(1)} %shard_map.52.refs_0_), channel_id=1, source_target_pairs={{0,20},{1,21},{2,22},{3,23},{4,16},{5,17},{6,18},{7,19},{8,28},{9,... | collective-permute-start | bytes 393224 | tf_op jit(solution)/shard_map/ppermute | solution.py:286
  32.8 0.1 collective-permute-start.8
  32.8 0.6 %collective-permute-start.7 = (bf16[256,256]{1,0:T(8,128)(2,1)S(1)}, bf16[256,256]{1,0:T(8,128)(2,1)S(1)}, u32[]{:S(2)}, u32[]{:S(2)}) collective-permute-start(bf16[256,256]{1,0:T(8,128)(2,1)S(1)} %shard_map.52.refs_0_), channel_id=1, source_target_pairs={{0,4},{1,5},{2,6},{3,7},{4,0},{5,1},{6,2},{7,3},{8,12},{9,13},{10,... | collective-permute-start | bytes 393224 | tf_op jit(solution)/shard_map/ppermute | solution.py:286
  33.4 3.4 %collective-permute-done.12.refs_7_ = bf16[256,256]{1,0:T(8,128)(2,1)S(1)} collective-permute-done((bf16[256,256]{1,0:T(8,128)(2,1)S(1)}, bf16[256,256]{1,0:T(8,128)(2,1)S(1)}, u32[]{:S(2)}, u32[]{:S(2)}) %collective-permute-start.12) | collective-permute-done | bytes 131104 | tf_op jit(solution)/shard_map/ppermute | solution.py:286
  36.8 0.1 collective-permute-start.13
  36.9 2.6 %collective-permute-done.10.refs_5_ = bf16[256,256]{1,0:T(8,128)(2,1)S(1)} collective-permute-done((bf16[256,256]{1,0:T(8,128)(2,1)S(1)}, bf16[256,256]{1,0:T(8,128)(2,1)S(1)}, u32[]{:S(2)}, u32[]{:S(2)}) %collective-permute-start.10) | collective-permute-done | bytes 131104 | tf_op jit(solution)/shard_map/ppermute | solution.py:286
  39.5 0.2 collective-permute-start.11
  39.7 0.0 collective-permute-done.8.refs_3_
  39.7 0.3 collective-permute-start.9
  40.0 0.0 collective-permute-done.7.refs_1_
  40.0 0.0 collective-permute-done.13.refs_6_
  40.0 0.8 %collective-permute-done.11.refs_4_ = bf16[256,256]{1,0:T(8,128)(2,1)S(1)} collective-permute-done((bf16[256,256]{1,0:T(8,128)(2,1)S(1)}, bf16[256,256]{1,0:T(8,128)(2,1)S(1)}, u32[]{:S(2)}, u32[]{:S(2)}) %collective-permute-start.11) | collective-permute-done | bytes 131104 | tf_op jit(solution)/shard_map/ppermute | solution.py:286
  40.9 0.2 collective-permute-done.9.refs_2_
  41.1 1.0 %shard_map.53 = bf16[2048,256]{1,0:T(8,128)(2,1)} custom-call(bf16[256,256]{1,0:T(8,128)(2,1)S(1)} %shard_map.52.refs_0_, bf16[256,256]{1,0:T(8,128)(2,1)S(1)} %collective-permute-done.7.refs_1_, bf16[256,256]{1,0:T(8,128)(2,1)S(1)} %collective-permute-done.9.refs_2_, bf16[256,256]{1,0:T(8,128)(2,1)S(1)} %collective-permute-done.8.refs_3_, ...), custom_call_target="tpu_custom_call" | custom-call | tf_op jit(solution)/shard_map/pallas_call | solution.py:374
  (1 shorter events, 0.0 us)
Async XLA Ops:
  4.8 8.3 %collective-permute-start = (bf16[256,256]{1,0:T(8,128)(2,1)S(1)}, bf16[256,256]{1,0:T(8,128)(2,1)S(1)}, u32[]{:S(2)}, u32[]{:S(2)}) collective-permute-start(bf16[256,256]{1,0:T(8,128)(2,1)S(1)} %get-tuple-element.19), channel_id=1, source_target_pairs={{0,24},{1,25},{2,26},{3,27},{4,28},{5,29},{6,30},{7,31},{8,16},{9,... | collective-permute-start | bytes 393224 | tf_op jit(solution)/shard_map/ppermute | solution.py:286
  9.3 6.9 %collective-permute-start.1 = (bf16[256,256]{1,0:T(8,128)(2,1)S(1)}, bf16[256,256]{1,0:T(8,128)(2,1)S(1)}, u32[]{:S(2)}, u32[]{:S(2)}) collective-permute-start(bf16[256,256]{1,0:T(8,128)(2,1)S(1)} %get-tuple-element.20), channel_id=1, source_target_pairs={{0,8},{1,9},{2,10},{3,11},{4,12},{5,13},{6,14},{7,15},{8,0},{9,1},... | collective-permute-start | bytes 393224 | tf_op jit(solution)/shard_map/ppermute | solution.py:286
  9.9 7.4 %collective-permute-start.2 = (bf16[256,256]{1,0:T(8,128)(2,1)S(1)}, bf16[256,256]{1,0:T(8,128)(2,1)S(1)}, u32[]{:S(2)}, u32[]{:S(2)}) collective-permute-start(bf16[256,256]{1,0:T(8,128)(2,1)S(1)} %get-tuple-element.21), channel_id=1, source_target_pairs={{0,16},{1,17},{2,18},{3,19},{4,20},{5,21},{6,22},{7,23},{8,24},{9,... | collective-permute-start | bytes 393224 | tf_op jit(solution)/shard_map/ppermute | solution.py:286
  9.9 8.1 %collective-permute-start.3 = (bf16[256,256]{1,0:T(8,128)(2,1)S(1)}, bf16[256,256]{1,0:T(8,128)(2,1)S(1)}, u32[]{:S(2)}, u32[]{:S(2)}) collective-permute-start(bf16[256,256]{1,0:T(8,128)(2,1)S(1)} %get-tuple-element.22), channel_id=1, source_target_pairs={{0,28},{1,29},{2,30},{3,31},{4,24},{5,25},{6,26},{7,27},{8,20},{9,... | collective-permute-start | bytes 393224 | tf_op jit(solution)/shard_map/ppermute | solution.py:286
  11.4 8.6 %collective-permute-start.4 = (bf16[256,256]{1,0:T(8,128)(2,1)S(1)}, bf16[256,256]{1,0:T(8,128)(2,1)S(1)}, u32[]{:S(2)}, u32[]{:S(2)}) collective-permute-start(bf16[256,256]{1,0:T(8,128)(2,1)S(1)} %get-tuple-element.23), channel_id=1, source_target_pairs={{0,12},{1,13},{2,14},{3,15},{4,8},{5,9},{6,10},{7,11},{8,4},{9,5},... | collective-permute-start | bytes 393224 | tf_op jit(solution)/shard_map/ppermute | solution.py:286
  13.4 7.4 %collective-permute-start.5 = (bf16[256,256]{1,0:T(8,128)(2,1)S(1)}, bf16[256,256]{1,0:T(8,128)(2,1)S(1)}, u32[]{:S(2)}, u32[]{:S(2)}) collective-permute-start(bf16[256,256]{1,0:T(8,128)(2,1)S(1)} %get-tuple-element.24), channel_id=1, source_target_pairs={{0,20},{1,21},{2,22},{3,23},{4,16},{5,17},{6,18},{7,19},{8,28},{9,... | collective-permute-start | bytes 393224 | tf_op jit(solution)/shard_map/ppermute | solution.py:286
  16.2 4.6 %collective-permute-start.6 = (bf16[256,256]{1,0:T(8,128)(2,1)S(1)}, bf16[256,256]{1,0:T(8,128)(2,1)S(1)}, u32[]{:S(2)}, u32[]{:S(2)}) collective-permute-start(bf16[256,256]{1,0:T(8,128)(2,1)S(1)} %get-tuple-element.25), channel_id=1, source_target_pairs={{0,4},{1,5},{2,6},{3,7},{4,0},{5,1},{6,2},{7,3},{8,12},{9,13},{10,... | collective-permute-start | bytes 393224 | tf_op jit(solution)/shard_map/ppermute | solution.py:286
  30.0 6.8 %collective-permute-start.12 = (bf16[256,256]{1,0:T(8,128)(2,1)S(1)}, bf16[256,256]{1,0:T(8,128)(2,1)S(1)}, u32[]{:S(2)}, u32[]{:S(2)}) collective-permute-start(bf16[256,256]{1,0:T(8,128)(2,1)S(1)} %shard_map.52.refs_0_), channel_id=1, source_target_pairs={{0,28},{1,29},{2,30},{3,31},{4,24},{5,25},{6,26},{7,27},{8,20},{9,... | collective-permute-start | bytes 393224 | tf_op jit(solution)/shard_map/ppermute | solution.py:286
  31.9 7.6 %collective-permute-start.10 = (bf16[256,256]{1,0:T(8,128)(2,1)S(1)}, bf16[256,256]{1,0:T(8,128)(2,1)S(1)}, u32[]{:S(2)}, u32[]{:S(2)}) collective-permute-start(bf16[256,256]{1,0:T(8,128)(2,1)S(1)} %shard_map.52.refs_0_), channel_id=1, source_target_pairs={{0,20},{1,21},{2,22},{3,23},{4,16},{5,17},{6,18},{7,19},{8,28},{9,... | collective-permute-start | bytes 393224 | tf_op jit(solution)/shard_map/ppermute | solution.py:286
  32.8 6.9 %collective-permute-start.8 = (bf16[256,256]{1,0:T(8,128)(2,1)S(1)}, bf16[256,256]{1,0:T(8,128)(2,1)S(1)}, u32[]{:S(2)}, u32[]{:S(2)}) collective-permute-start(bf16[256,256]{1,0:T(8,128)(2,1)S(1)} %shard_map.52.refs_0_), channel_id=1, source_target_pairs={{0,12},{1,13},{2,14},{3,15},{4,8},{5,9},{6,10},{7,11},{8,4},{9,5},... | collective-permute-start | bytes 393224 | tf_op jit(solution)/shard_map/ppermute | solution.py:286
  32.8 7.2 %collective-permute-start.7 = (bf16[256,256]{1,0:T(8,128)(2,1)S(1)}, bf16[256,256]{1,0:T(8,128)(2,1)S(1)}, u32[]{:S(2)}, u32[]{:S(2)}) collective-permute-start(bf16[256,256]{1,0:T(8,128)(2,1)S(1)} %shard_map.52.refs_0_), channel_id=1, source_target_pairs={{0,4},{1,5},{2,6},{3,7},{4,0},{5,1},{6,2},{7,3},{8,12},{9,13},{10,... | collective-permute-start | bytes 393224 | tf_op jit(solution)/shard_map/ppermute | solution.py:286
  36.8 3.2 %collective-permute-start.13 = (bf16[256,256]{1,0:T(8,128)(2,1)S(1)}, bf16[256,256]{1,0:T(8,128)(2,1)S(1)}, u32[]{:S(2)}, u32[]{:S(2)}) collective-permute-start(bf16[256,256]{1,0:T(8,128)(2,1)S(1)} %collective-permute-done.12.refs_7_), channel_id=1, source_target_pairs={{0,4},{1,5},{2,6},{3,7},{4,0},{5,1},{6,2},{7,3},{8,12},{9,13},{10,... | collective-permute-start | bytes 393224 | tf_op jit(solution)/shard_map/ppermute | solution.py:286
  39.5 1.3 %collective-permute-start.11 = (bf16[256,256]{1,0:T(8,128)(2,1)S(1)}, bf16[256,256]{1,0:T(8,128)(2,1)S(1)}, u32[]{:S(2)}, u32[]{:S(2)}) collective-permute-start(bf16[256,256]{1,0:T(8,128)(2,1)S(1)} %collective-permute-done.10.refs_5_), channel_id=1, source_target_pairs={{0,4},{1,5},{2,6},{3,7},{4,0},{5,1},{6,2},{7,3},{8,12},{9,13},{10,... | collective-permute-start | bytes 393224 | tf_op jit(solution)/shard_map/ppermute | solution.py:286
  39.7 1.3 %collective-permute-start.9 = (bf16[256,256]{1,0:T(8,128)(2,1)S(1)}, bf16[256,256]{1,0:T(8,128)(2,1)S(1)}, u32[]{:S(2)}, u32[]{:S(2)}) collective-permute-start(bf16[256,256]{1,0:T(8,128)(2,1)S(1)} %collective-permute-done.8.refs_3_), channel_id=1, source_target_pairs={{0,4},{1,5},{2,6},{3,7},{4,0},{5,1},{6,2},{7,3},{8,12},{9,13},{10,... | collective-permute-start | bytes 393224 | tf_op jit(solution)/shard_map/ppermute | solution.py:286

commit v4 on v3

--- a/solution.py
+++ b/solution.py
@@ -13,7 +13,6 @@
 MOMENTUM = 0.9
 EPSILON = 1e-06
 LOADS = 4
-LATE = 3
 VMEM_LIMIT = 48 * 1024 * 1024
 
 F32 = jnp.float32
@@ -246,14 +245,15 @@
     out_ref[...] = (own_ref[...].astype(F32) + combined).astype(BF16)
 
 
-def place_kernel(*refs):
+def place_kernel(routes, *refs):
     pieces, (out_ref, sems) = refs[:-2], refs[-2:]
     seg = pieces[0].shape[0]
     me = lax.axis_index("rep")
     moves = []
-    for distance, piece in enumerate(pieces):
+    for n, ((even, odd), piece) in enumerate(zip(routes, pieces)):
+        distance = jnp.where(me % 2 == 1, odd, even)
         at = pl.multiple_of((me ^ distance) * seg, seg)
-        move = pltpu.make_async_copy(piece, out_ref.at[pl.ds(at, seg)], sems.at[distance])
+        move = pltpu.make_async_copy(piece, out_ref.at[pl.ds(at, seg)], sems.at[n])
         move.start()
         moves.append(move)
     for move in moves:
@@ -278,8 +278,9 @@
 
 def flipped(value, replica_bits, shard_bits=0):
     replicas, shards = lax.axis_size("rep"), lax.axis_size("shard")
+    bits = replica_bits if isinstance(replica_bits, tuple) else (replica_bits,) * 2
     pairs = [
-        (i * shards + j, (i ^ replica_bits) * shards + (j ^ shard_bits))
+        (i * shards + j, (i ^ bits[i % 2]) * shards + (j ^ shard_bits))
         for i in range(replicas)
         for j in range(shards)
     ]
@@ -366,18 +367,27 @@
         jax.ShapeDtypeStruct((seg, columns), BF16),
         [near] * (parts + 2),
     )(gram, own_weights, *(leaves[d] for d in order))
-    pieces = [own] + [None] * (parts - 1)
-    pieces[1] = flipped(own, 1)
-    for d in range(2, parts, 2):
-        pieces[d + 1] = flipped(own, d + 1)
-        pieces[d] = flipped(pieces[d + 1], 1)
+    pieces = {(0, 0): own, (1, 1): flipped(own, 1)}
+    bits = parts.bit_length() - 2
+    for chip in range(parts // 2 - 1, 0, -1):
+        mirror = sum((chip >> k & 1) << (bits - 1 - k) for k in range(bits))
+        if mirror == chip:
+            came, passed = (2 * chip + 1, 2 * chip + 1), (2 * chip, 2 * chip)
+        else:
+            came, passed = (2 * chip, 2 * mirror), (2 * mirror + 1, 2 * chip + 1)
+        pieces[came] = flipped(own, came)
+        pieces[passed] = flipped(pieces[came], 1)
+
+    def place(*refs):
+        place_kernel(list(pieces), *refs)
+
     placed = call(
-        place_kernel,
+        place,
         jax.ShapeDtypeStruct((width, columns), BF16),
         [any_place] * parts,
         [pltpu.SemaphoreType.DMA((parts,))],
         far,
-    )(*pieces)
+    )(*pieces.values())
     return placed[None]
 
 

time: 42.3 us -> 41.9 us (level)
  no operation moved by 1% of the time
where the time goes in v4:
time: 41.9 us; the launch traced here: 41.7 us
  waiting for transfers between devices  13.3 us (32%)
  starting transfers between devices  11.9 us (28%)
  Pallas kernels  8.63 us (21%)
  blocking collectives  7.84 us (19%)
    ppermute x14, waiting for transfers between devices, flipped(): return lax.ppermute(value, ('rep', 'shard'), pairs)  13.3 us
    ppermute x14, starting transfers between devices, flipped(): return lax.ppermute(value, ('rep', 'shard'), pairs)  11.9 us
    all_to_all x1, blocking collectives, body(): lax.all_to_all(gram, ('rep', 'shard'), 0, 0, axis_index_groups=groups)  7.84 us
    pallas_call x1, Pallas kernels, body(): call(local, [rows_out, jax.ShapeDtypeStruct((seg, columns), BF16), jax.Sh...  4.79 us
    pallas_call x3, Pallas kernels, body(): call(products, table, [near] * len(inputs))(*inputs)  1.11 us
    pallas_call x1, Pallas kernels, body(): call(place, jax.ShapeDtypeStruct((width, columns), BF16), [any_place] * p...  1.02 us
    pallas_call x1, Pallas kernels, body(): call(combine_kernel, jax.ShapeDtypeStruct((seg, columns), BF16), [near] *...  0.87 us
  transfers between devices with their start and end apart: 14, of which 9 were waited for; matrix products, arithmetic and copies ran while one was open for 0% of the time, Pallas kernels for 4%

profile of v4, /device:TPU:0, one launch (start us, length us, event | category | flops | bytes accessed | tf_op | source)
XLA Modules:
  0.0 41.7 jit_solution(199839595654463525)
XLA Ops:
  0.0 4.8 %shard_map.46 = (bf16[256,256]{1,0:T(8,128)(2,1)S(1)}, bf16[256,256]{1,0:T(8,128)(2,1)S(1)}, bf16[256,512]{1,0:T(8,128)(2,1)S(1)}, bf16[512,2048]{1,0:T(8,128)(2,1)S(1)}) custom-call(s32[2,1,512]{2,1,0:T(1,128)} %bitcast.10, bf16[384,2048]{1,0:T(8,128)(2,1)} %bitcast.7, bf16[2048,256]{1,0:T(8,128)(2,1)} %bitcast.8, bf16[512,256]{1,0:T(8,128)(2,1)} %bitcast.9), custom_call_target="tpu_custom_call" | custom-call | tf_op jit(solution)/shard_map/pallas_call | solution.py:308
  4.8 4.0 %collective-permute-start = (bf16[256,256]{1,0:T(8,128)(2,1)S(1)}, bf16[256,256]{1,0:T(8,128)(2,1)S(1)}, u32[]{:S(2)}, u32[]{:S(2)}) collective-permute-start(bf16[256,256]{1,0:T(8,128)(2,1)S(1)} %get-tuple-element.19), channel_id=1, source_target_pairs={{0,24},{1,25},{2,26},{3,27},{4,28},{5,29},{6,30},{7,31},{8,16},{9,... | collective-permute-start | bytes 393224 | tf_op jit(solution)/shard_map/ppermute | solution.py:287
  8.8 0.5 %shard_map.47 = (bf16[256,256]{1,0:T(8,128)(2,1)S(1)}, bf16[256,256]{1,0:T(8,128)(2,1)S(1)}, bf16[256,256]{1,0:T(8,128)(2,1)S(1)}, bf16[256,256]{1,0:T(8,128)(2,1)S(1)}, bf16[256,256]{1,0:T(8,128)(2,1)S(1)}) custom-call(bf16[256,512]{1,0:T(8,128)(2,1)S(1)} %get-tuple-element.16.refs_0_, bf16[512,2048]{1,0:T(8,128)(2,1)S(1)} %get-tuple-element.17.refs_1_), custom_call_target="tpu_custom_call" | custom-call | tf_op jit(solution)/shard_map/pallas_call | solution.py:337
  9.3 0.6 %collective-permute-start.1 = (bf16[256,256]{1,0:T(8,128)(2,1)S(1)}, bf16[256,256]{1,0:T(8,128)(2,1)S(1)}, u32[]{:S(2)}, u32[]{:S(2)}) collective-permute-start(bf16[256,256]{1,0:T(8,128)(2,1)S(1)} %get-tuple-element.20), channel_id=1, source_target_pairs={{0,8},{1,9},{2,10},{3,11},{4,12},{5,13},{6,14},{7,15},{8,0},{9,1},... | collective-permute-start | bytes 393224 | tf_op jit(solution)/shard_map/ppermute | solution.py:287
  9.9 0.1 collective-permute-start.2
  9.9 1.5 %collective-permute-start.3 = (bf16[256,256]{1,0:T(8,128)(2,1)S(1)}, bf16[256,256]{1,0:T(8,128)(2,1)S(1)}, u32[]{:S(2)}, u32[]{:S(2)}) collective-permute-start(bf16[256,256]{1,0:T(8,128)(2,1)S(1)} %get-tuple-element.22), channel_id=1, source_target_pairs={{0,28},{1,29},{2,30},{3,31},{4,24},{5,25},{6,26},{7,27},{8,20},{9,... | collective-permute-start | bytes 393224 | tf_op jit(solution)/shard_map/ppermute | solution.py:287
  11.4 1.7 %collective-permute-start.4 = (bf16[256,256]{1,0:T(8,128)(2,1)S(1)}, bf16[256,256]{1,0:T(8,128)(2,1)S(1)}, u32[]{:S(2)}, u32[]{:S(2)}) collective-permute-start(bf16[256,256]{1,0:T(8,128)(2,1)S(1)} %get-tuple-element.23), channel_id=1, source_target_pairs={{0,12},{1,13},{2,14},{3,15},{4,8},{5,9},{6,10},{7,11},{8,4},{9,5},... | collective-permute-start | bytes 393224 | tf_op jit(solution)/shard_map/ppermute | solution.py:287
  13.1 0.0 collective-permute-done.refs_2_.refs_1_.rest_1_
  13.1 0.3 shard_map.48
  13.4 0.1 collective-permute-start.5
  13.5 2.7 %collective-permute-done.1.refs_2_.rest_2_ = bf16[256,256]{1,0:T(8,128)(2,1)S(1)} collective-permute-done((bf16[256,256]{1,0:T(8,128)(2,1)S(1)}, bf16[256,256]{1,0:T(8,128)(2,1)S(1)}, u32[]{:S(2)}, u32[]{:S(2)}) %collective-permute-start.1) | collective-permute-done | bytes 131104 | tf_op jit(solution)/shard_map/ppermute | solution.py:287
  16.2 0.0 collective-permute-start.6
  16.2 1.1 %collective-permute-done.2.refs_3_.rest_3_ = bf16[256,256]{1,0:T(8,128)(2,1)S(1)} collective-permute-done((bf16[256,256]{1,0:T(8,128)(2,1)S(1)}, bf16[256,256]{1,0:T(8,128)(2,1)S(1)}, u32[]{:S(2)}, u32[]{:S(2)}) %collective-permute-start.2) | collective-permute-done | bytes 131104 | tf_op jit(solution)/shard_map/ppermute | solution.py:287
  17.3 0.8 %collective-permute-done.3.refs_4_.rest_4_ = bf16[256,256]{1,0:T(8,128)(2,1)S(1)} collective-permute-done((bf16[256,256]{1,0:T(8,128)(2,1)S(1)}, bf16[256,256]{1,0:T(8,128)(2,1)S(1)}, u32[]{:S(2)}, u32[]{:S(2)}) %collective-permute-start.3) | collective-permute-done | bytes 131104 | tf_op jit(solution)/shard_map/ppermute | solution.py:287
  18.1 0.4 shard_map.49.refs_6_
  18.5 1.6 %collective-permute-done.4.refs_5_.rest_5_ = bf16[256,256]{1,0:T(8,128)(2,1)S(1)} collective-permute-done((bf16[256,256]{1,0:T(8,128)(2,1)S(1)}, bf16[256,256]{1,0:T(8,128)(2,1)S(1)}, u32[]{:S(2)}, u32[]{:S(2)}) %collective-permute-start.4) | collective-permute-done | bytes 131104 | tf_op jit(solution)/shard_map/ppermute | solution.py:287
  20.1 0.3 shard_map.50.refs_8_
  20.3 0.5 %collective-permute-done.5.refs_6_.rest_6_ = bf16[256,256]{1,0:T(8,128)(2,1)S(1)} collective-permute-done((bf16[256,256]{1,0:T(8,128)(2,1)S(1)}, bf16[256,256]{1,0:T(8,128)(2,1)S(1)}, u32[]{:S(2)}, u32[]{:S(2)}) %collective-permute-start.5) | collective-permute-done | bytes 131104 | tf_op jit(solution)/shard_map/ppermute | solution.py:287
  20.8 0.0 collective-permute-done.6.refs_7_.rest_7_
  20.8 0.4 %shard_map.51 = f32[1,128]{1,0:T(1,128)S(1)} custom-call(bf16[256,256]{1,0:T(8,128)(2,1)S(1)} %get-tuple-element.18.refs_0_.rest_0_, bf16[256,256]{1,0:T(8,128)(2,1)S(1)} %collective-permute-done.refs_2_.refs_1_.rest_1_, bf16[256,256]{1,0:T(8,128)(2,1)S(1)} %collective-permute-done.1.refs_2_.rest_2_, ...), custom_call_target="tpu_custom_call" | custom-call | tf_op jit(solution)/shard_map/pallas_call | solution.py:354
  21.3 7.8 %all_to_all.5.gram_ref = f32[16,1,128]{2,1,0:T(1,128)S(1)} all-to-all(f32[16,1,128]{2,1,0:T(1,128)S(1)} %broadcast_in_dim.6), channel_id=1, replica_groups={{29,28,25,24,21,20,17,16,13,12,9,8,5,4,1,0},{31,30,27,26,23,22,19,18,15..., dimensions={0} | all-to-all | bytes 16384 | tf_op jit(solution)/shard_map/all_to_all | solution.py:363
  29.1 0.9 %shard_map.52.refs_0_ = bf16[256,256]{1,0:T(8,128)(2,1)S(1)} custom-call(f32[16,1,128]{2,1,0:T(1,128)S(1)} %all_to_all.5.gram_ref, bf16[256,256]{1,0:T(8,128)(2,1)S(1)} %get-tuple-element.26.own_ref, bf16[256,256]{1,0:T(8,128)(2,1)S(1)} %get-tuple-element.18.refs_0_.rest_0_, bf16[256,256]{1,0:T(8,128)(2,1)S(1)} %collective-permute-done.refs_2_.refs_1_.rest_1_, ...), custom_call_target="tpu_custom_call" | custom-call | tf_op jit(solution)/shard_map/pallas_call | solution.py:365
  30.0 1.6 %collective-permute-start.12 = (bf16[256,256]{1,0:T(8,128)(2,1)S(1)}, bf16[256,256]{1,0:T(8,128)(2,1)S(1)}, u32[]{:S(2)}, u32[]{:S(2)}) collective-permute-start(bf16[256,256]{1,0:T(8,128)(2,1)S(1)} %shard_map.52.refs_0_), channel_id=1, source_target_pairs={{0,8},{1,9},{2,10},{3,11},{4,20},{5,21},{6,22},{7,23},{8,0},{9,1},... | collective-permute-start | bytes 393224 | tf_op jit(solution)/shard_map/ppermute | solution.py:287
  31.6 1.4 %collective-permute-start.10 = (bf16[256,256]{1,0:T(8,128)(2,1)S(1)}, bf16[256,256]{1,0:T(8,128)(2,1)S(1)}, u32[]{:S(2)}, u32[]{:S(2)}) collective-permute-start(bf16[256,256]{1,0:T(8,128)(2,1)S(1)} %shard_map.52.refs_0_), channel_id=1, source_target_pairs={{0,16},{1,17},{2,18},{3,19},{4,12},{5,13},{6,14},{7,15},{8,24},{9,... | collective-permute-start | bytes 393224 | tf_op jit(solution)/shard_map/ppermute | solution.py:287
  33.0 0.0 collective-permute-start.8
  33.0 0.7 %collective-permute-start.7 = (bf16[256,256]{1,0:T(8,128)(2,1)S(1)}, bf16[256,256]{1,0:T(8,128)(2,1)S(1)}, u32[]{:S(2)}, u32[]{:S(2)}) collective-permute-start(bf16[256,256]{1,0:T(8,128)(2,1)S(1)} %shard_map.52.refs_0_), channel_id=1, source_target_pairs={{0,4},{1,5},{2,6},{3,7},{4,0},{5,1},{6,2},{7,3},{8,12},{9,13},{10,... | collective-permute-start | bytes 393224 | tf_op jit(solution)/shard_map/ppermute | solution.py:287
  33.7 2.7 %collective-permute-done.12.refs_6_ = bf16[256,256]{1,0:T(8,128)(2,1)S(1)} collective-permute-done((bf16[256,256]{1,0:T(8,128)(2,1)S(1)}, bf16[256,256]{1,0:T(8,128)(2,1)S(1)}, u32[]{:S(2)}, u32[]{:S(2)}) %collective-permute-start.12) | collective-permute-done | bytes 131104 | tf_op jit(solution)/shard_map/ppermute | solution.py:287
  36.4 0.0 collective-permute-start.13
  36.4 0.2 collective-permute-done.10.refs_4_
  36.6 0.3 collective-permute-start.11
  36.9 2.5 %collective-permute-done.8.refs_2_ = bf16[256,256]{1,0:T(8,128)(2,1)S(1)} collective-permute-done((bf16[256,256]{1,0:T(8,128)(2,1)S(1)}, bf16[256,256]{1,0:T(8,128)(2,1)S(1)}, u32[]{:S(2)}, u32[]{:S(2)}) %collective-permute-start.8) | collective-permute-done | bytes 131104 | tf_op jit(solution)/shard_map/ppermute | solution.py:287
  39.4 0.0 collective-permute-start.9
  39.4 0.0 collective-permute-done.7.refs_1_
  39.4 0.0 collective-permute-done.13.refs_7_
  39.4 0.0 collective-permute-done.11.refs_5_
  39.4 1.3 %collective-permute-done.9.refs_3_ = bf16[256,256]{1,0:T(8,128)(2,1)S(1)} collective-permute-done((bf16[256,256]{1,0:T(8,128)(2,1)S(1)}, bf16[256,256]{1,0:T(8,128)(2,1)S(1)}, u32[]{:S(2)}, u32[]{:S(2)}) %collective-permute-start.9) | collective-permute-done | bytes 131104 | tf_op jit(solution)/shard_map/ppermute | solution.py:287
  40.7 1.0 %shard_map.53 = bf16[2048,256]{1,0:T(8,128)(2,1)} custom-call(bf16[256,256]{1,0:T(8,128)(2,1)S(1)} %shard_map.52.refs_0_, bf16[256,256]{1,0:T(8,128)(2,1)S(1)} %collective-permute-done.7.refs_1_, bf16[256,256]{1,0:T(8,128)(2,1)S(1)} %collective-permute-done.8.refs_2_, bf16[256,256]{1,0:T(8,128)(2,1)S(1)} %collective-permute-done.9.refs_3_, ...), custom_call_target="tpu_custom_call" | custom-call | tf_op jit(solution)/shard_map/pallas_call | solution.py:384
  (1 shorter events, 0.0 us)
Async XLA Ops:
  4.8 8.3 %collective-permute-start = (bf16[256,256]{1,0:T(8,128)(2,1)S(1)}, bf16[256,256]{1,0:T(8,128)(2,1)S(1)}, u32[]{:S(2)}, u32[]{:S(2)}) collective-permute-start(bf16[256,256]{1,0:T(8,128)(2,1)S(1)} %get-tuple-element.19), channel_id=1, source_target_pairs={{0,24},{1,25},{2,26},{3,27},{4,28},{5,29},{6,30},{7,31},{8,16},{9,... | collective-permute-start | bytes 393224 | tf_op jit(solution)/shard_map/ppermute | solution.py:287
  9.3 6.9 %collective-permute-start.1 = (bf16[256,256]{1,0:T(8,128)(2,1)S(1)}, bf16[256,256]{1,0:T(8,128)(2,1)S(1)}, u32[]{:S(2)}, u32[]{:S(2)}) collective-permute-start(bf16[256,256]{1,0:T(8,128)(2,1)S(1)} %get-tuple-element.20), channel_id=1, source_target_pairs={{0,8},{1,9},{2,10},{3,11},{4,12},{5,13},{6,14},{7,15},{8,0},{9,1},... | collective-permute-start | bytes 393224 | tf_op jit(solution)/shard_map/ppermute | solution.py:287
  9.9 7.4 %collective-permute-start.2 = (bf16[256,256]{1,0:T(8,128)(2,1)S(1)}, bf16[256,256]{1,0:T(8,128)(2,1)S(1)}, u32[]{:S(2)}, u32[]{:S(2)}) collective-permute-start(bf16[256,256]{1,0:T(8,128)(2,1)S(1)} %get-tuple-element.21), channel_id=1, source_target_pairs={{0,16},{1,17},{2,18},{3,19},{4,20},{5,21},{6,22},{7,23},{8,24},{9,... | collective-permute-start | bytes 393224 | tf_op jit(solution)/shard_map/ppermute | solution.py:287
  9.9 8.1 %collective-permute-start.3 = (bf16[256,256]{1,0:T(8,128)(2,1)S(1)}, bf16[256,256]{1,0:T(8,128)(2,1)S(1)}, u32[]{:S(2)}, u32[]{:S(2)}) collective-permute-start(bf16[256,256]{1,0:T(8,128)(2,1)S(1)} %get-tuple-element.22), channel_id=1, source_target_pairs={{0,28},{1,29},{2,30},{3,31},{4,24},{5,25},{6,26},{7,27},{8,20},{9,... | collective-permute-start | bytes 393224 | tf_op jit(solution)/shard_map/ppermute | solution.py:287
  11.4 8.6 %collective-permute-start.4 = (bf16[256,256]{1,0:T(8,128)(2,1)S(1)}, bf16[256,256]{1,0:T(8,128)(2,1)S(1)}, u32[]{:S(2)}, u32[]{:S(2)}) collective-permute-start(bf16[256,256]{1,0:T(8,128)(2,1)S(1)} %get-tuple-element.23), channel_id=1, source_target_pairs={{0,12},{1,13},{2,14},{3,15},{4,8},{5,9},{6,10},{7,11},{8,4},{9,5},... | collective-permute-start | bytes 393224 | tf_op jit(solution)/shard_map/ppermute | solution.py:287
  13.4 7.4 %collective-permute-start.5 = (bf16[256,256]{1,0:T(8,128)(2,1)S(1)}, bf16[256,256]{1,0:T(8,128)(2,1)S(1)}, u32[]{:S(2)}, u32[]{:S(2)}) collective-permute-start(bf16[256,256]{1,0:T(8,128)(2,1)S(1)} %get-tuple-element.24), channel_id=1, source_target_pairs={{0,20},{1,21},{2,22},{3,23},{4,16},{5,17},{6,18},{7,19},{8,28},{9,... | collective-permute-start | bytes 393224 | tf_op jit(solution)/shard_map/ppermute | solution.py:287
  16.2 4.6 %collective-permute-start.6 = (bf16[256,256]{1,0:T(8,128)(2,1)S(1)}, bf16[256,256]{1,0:T(8,128)(2,1)S(1)}, u32[]{:S(2)}, u32[]{:S(2)}) collective-permute-start(bf16[256,256]{1,0:T(8,128)(2,1)S(1)} %get-tuple-element.25), channel_id=1, source_target_pairs={{0,4},{1,5},{2,6},{3,7},{4,0},{5,1},{6,2},{7,3},{8,12},{9,13},{10,... | collective-permute-start | bytes 393224 | tf_op jit(solution)/shard_map/ppermute | solution.py:287
  30.0 6.4 %collective-permute-start.12 = (bf16[256,256]{1,0:T(8,128)(2,1)S(1)}, bf16[256,256]{1,0:T(8,128)(2,1)S(1)}, u32[]{:S(2)}, u32[]{:S(2)}) collective-permute-start(bf16[256,256]{1,0:T(8,128)(2,1)S(1)} %shard_map.52.refs_0_), channel_id=1, source_target_pairs={{0,8},{1,9},{2,10},{3,11},{4,20},{5,21},{6,22},{7,23},{8,0},{9,1},... | collective-permute-start | bytes 393224 | tf_op jit(solution)/shard_map/ppermute | solution.py:287
  31.6 5.0 %collective-permute-start.10 = (bf16[256,256]{1,0:T(8,128)(2,1)S(1)}, bf16[256,256]{1,0:T(8,128)(2,1)S(1)}, u32[]{:S(2)}, u32[]{:S(2)}) collective-permute-start(bf16[256,256]{1,0:T(8,128)(2,1)S(1)} %shard_map.52.refs_0_), channel_id=1, source_target_pairs={{0,16},{1,17},{2,18},{3,19},{4,12},{5,13},{6,14},{7,15},{8,24},{9,... | collective-permute-start | bytes 393224 | tf_op jit(solution)/shard_map/ppermute | solution.py:287
  33.0 6.3 %collective-permute-start.8 = (bf16[256,256]{1,0:T(8,128)(2,1)S(1)}, bf16[256,256]{1,0:T(8,128)(2,1)S(1)}, u32[]{:S(2)}, u32[]{:S(2)}) collective-permute-start(bf16[256,256]{1,0:T(8,128)(2,1)S(1)} %shard_map.52.refs_0_), channel_id=1, source_target_pairs={{0,28},{1,29},{2,30},{3,31},{4,24},{5,25},{6,26},{7,27},{8,20},{9,... | collective-permute-start | bytes 393224 | tf_op jit(solution)/shard_map/ppermute | solution.py:287
  33.0 6.3 %collective-permute-start.7 = (bf16[256,256]{1,0:T(8,128)(2,1)S(1)}, bf16[256,256]{1,0:T(8,128)(2,1)S(1)}, u32[]{:S(2)}, u32[]{:S(2)}) collective-permute-start(bf16[256,256]{1,0:T(8,128)(2,1)S(1)} %shard_map.52.refs_0_), channel_id=1, source_target_pairs={{0,4},{1,5},{2,6},{3,7},{4,0},{5,1},{6,2},{7,3},{8,12},{9,13},{10,... | collective-permute-start | bytes 393224 | tf_op jit(solution)/shard_map/ppermute | solution.py:287
  36.4 3.0 %collective-permute-start.13 = (bf16[256,256]{1,0:T(8,128)(2,1)S(1)}, bf16[256,256]{1,0:T(8,128)(2,1)S(1)}, u32[]{:S(2)}, u32[]{:S(2)}) collective-permute-start(bf16[256,256]{1,0:T(8,128)(2,1)S(1)} %collective-permute-done.12.refs_6_), channel_id=1, source_target_pairs={{0,4},{1,5},{2,6},{3,7},{4,0},{5,1},{6,2},{7,3},{8,12},{9,13},{10,... | collective-permute-start | bytes 393224 | tf_op jit(solution)/shard_map/ppermute | solution.py:287
  36.6 2.8 %collective-permute-start.11 = (bf16[256,256]{1,0:T(8,128)(2,1)S(1)}, bf16[256,256]{1,0:T(8,128)(2,1)S(1)}, u32[]{:S(2)}, u32[]{:S(2)}) collective-permute-start(bf16[256,256]{1,0:T(8,128)(2,1)S(1)} %collective-permute-done.10.refs_4_), channel_id=1, source_target_pairs={{0,4},{1,5},{2,6},{3,7},{4,0},{5,1},{6,2},{7,3},{8,12},{9,13},{10,... | collective-permute-start | bytes 393224 | tf_op jit(solution)/shard_map/ppermute | solution.py:287
  39.4 1.3 %collective-permute-start.9 = (bf16[256,256]{1,0:T(8,128)(2,1)S(1)}, bf16[256,256]{1,0:T(8,128)(2,1)S(1)}, u32[]{:S(2)}, u32[]{:S(2)}) collective-permute-start(bf16[256,256]{1,0:T(8,128)(2,1)S(1)} %collective-permute-done.8.refs_2_), channel_id=1, source_target_pairs={{0,4},{1,5},{2,6},{3,7},{4,0},{5,1},{6,2},{7,3},{8,12},{9,13},{10,... | collective-permute-start | bytes 393224 | tf_op jit(solution)/shard_map/ppermute | solution.py:287

commit v5 on v4

--- a/solution.py
+++ b/solution.py
@@ -27,9 +27,23 @@
     return lax.dot_general(a, b, (dims, ((), ())), preferred_element_type=F32)
 
 
-def share_rows(turned_ref, x_ref, distance, out_ref):
+def routes(parts):
+    bits = parts.bit_length() - 2
+    ways = {}
+    for distance in range(parts):
+        chip = distance >> 1
+        mirror = sum((chip >> k & 1) << (bits - 1 - k) for k in range(bits))
+        ways[distance] = (distance, distance if distance & 1 else 2 * mirror)
+    return ways
+
+
+def partner(me, way):
+    return me ^ jnp.where(me % 2 == 1, way[1], way[0])
+
+
+def share_rows(turned_ref, x_ref, way, out_ref):
     seg = out_ref.shape[1]
-    target = lax.axis_index("rep") ^ distance
+    target = partner(lax.axis_index("rep"), way)
     held = max(seg, 128)
     at = pl.multiple_of(target * seg // held * held, held)
     moved = jnp.dot(turned_ref[...], x_ref[:, pl.ds(at, held)], preferred_element_type=F32)
@@ -41,11 +55,11 @@
 
 
 def share_kernel(order, turned_ref, x_ref, *rest):
-    for distance, out_ref in zip(order, rest[-len(order) :]):
-        share_rows(turned_ref, x_ref, distance, out_ref)
-
-
-def local_kernel(cut, partner, idx_hbm, pool_hbm, w_hbm, goal_hbm, *rest):
+    for way, out_ref in zip(order, rest[-len(order) :]):
+        share_rows(turned_ref, x_ref, way, out_ref)
+
+
+def local_kernel(cut, way, idx_hbm, pool_hbm, w_hbm, goal_hbm, *rest):
     first_ref, own_ref, turned_ref, x_ref = rest[:4]
     idx_ref, pool_ref, w_ref, goal_ref, sems = rest[4:]
     pool_rows, width = pool_ref.shape
@@ -126,7 +140,7 @@
         final.append((grad * (-reach(STEPS - s) * inv_batch)).T.astype(BF16))
 
     turned_ref[...] = jnp.concatenate(final, axis=1)
-    share_rows(turned_ref, x_ref, partner, first_ref)
+    share_rows(turned_ref, x_ref, way, first_ref)
     start = pl.multiple_of(lax.axis_index("rep") * seg, seg)
     own_ref[...] = w_ref[pl.ds(start, seg), :]
 
@@ -182,7 +196,7 @@
             sums = lax.fori_loop(0, rows // tall, step, zeros, unroll=4 if count <= block else 1)
             for n, (i, j) in enumerate(pairs):
                 value = jnp.sum(jnp.sum(sums[n], axis=0, keepdims=True), axis=1, keepdims=True)
-                mine, other = me ^ order[i], me ^ order[j]
+                mine, other = partner(me, order[i]), partner(me, order[j])
                 here = (spots == mine * parts + other) | (spots == other * parts + mine)
                 table = jnp.where(here, value, table)
     out_ref[...] = table
@@ -235,24 +249,24 @@
         gram[i, j] = table[down : down + 1, across : across + 1]
     weights = tree_weights(gram, count)
     total = None
+    ways = routes(count)
     for distance, delta in zip(distances(count), deltas):
         weight = weights[0]
         for k in range(1, count):
-            weight = jnp.where((me ^ distance) == k, weights[k], weight)
+            weight = jnp.where(partner(me, ways[distance]) == k, weights[k], weight)
         term = weight * delta[...].astype(F32)
         total = term if total is None else total + term
     combined = total.T.astype(BF16).astype(F32)
     out_ref[...] = (own_ref[...].astype(F32) + combined).astype(BF16)
 
 
-def place_kernel(routes, *refs):
+def place_kernel(ways, *refs):
     pieces, (out_ref, sems) = refs[:-2], refs[-2:]
     seg = pieces[0].shape[0]
     me = lax.axis_index("rep")
     moves = []
-    for n, ((even, odd), piece) in enumerate(zip(routes, pieces)):
-        distance = jnp.where(me % 2 == 1, odd, even)
-        at = pl.multiple_of((me ^ distance) * seg, seg)
+    for n, (way, piece) in enumerate(zip(ways, pieces)):
+        at = pl.multiple_of(partner(me, way) * seg, seg)
         move = pltpu.make_async_copy(piece, out_ref.at[pl.ds(at, seg)], sems.at[n])
         move.start()
         moves.append(move)
@@ -276,9 +290,9 @@
     return pltpu.with_memory_space_constraint(value, pltpu.HBM)
 
 
-def flipped(value, replica_bits, shard_bits=0):
+def flipped(value, way, shard_bits=0):
     replicas, shards = lax.axis_size("rep"), lax.axis_size("shard")
-    bits = replica_bits if isinstance(replica_bits, tuple) else (replica_bits,) * 2
+    bits = way if isinstance(way, tuple) else (way, way)
     pairs = [
         (i * shards + j, (i ^ bits[i % 2]) * shards + (j ^ shard_bits))
         for i in range(replicas)
@@ -298,11 +312,11 @@
     far = pl.BlockSpec(memory_space=pltpu.HBM)
     any_place = pl.BlockSpec(memory_space=pl.ANY)
 
-    order = distances(parts)
+    order, ways = distances(parts), routes(parts)
     first = order[1]
 
     def local(*refs):
-        local_kernel(cut, first, *refs)
+        local_kernel(cut, ways[first], *refs)
 
     rows_out = jax.ShapeDtypeStruct((columns, seg), BF16)
     out, own_weights, turned, gathered = call(
@@ -322,7 +336,7 @@
             pltpu.SemaphoreType.DMA((LOADS + 3,)),
         ],
     )(hold(row_index[0]), hold(token_pool[0]), hold(weights[0]), hold(targets[0, 0]))
-    leaves = {first: flipped(out, first)}
+    leaves = {first: flipped(out, ways[first])}
     middle = max(2, parts - 2)
     for group, after in (
         ([0, *order[2:middle]], []),
@@ -332,13 +346,13 @@
             continue
 
         def shares(*refs, group=group):
-            share_kernel(group, *refs)
+            share_kernel([ways[d] for d in group], *refs)
 
         made = call(shares, [rows_out] * len(group), [near] * (2 + len(after)))(
             turned, gathered, *after
         )
         for d, out in zip(group, made):
-            leaves[d] = flipped(out, d) if d else out
+            leaves[d] = flipped(out, ways[d]) if d else out
 
     table = jax.ShapeDtypeStruct((-(-parts * parts // 128), 128), F32)
     gram, known = [], 0
@@ -348,7 +362,7 @@
         taken = order[:reached]
 
         def products(*refs, taken=taken, known=known):
-            gram_kernel(parts, taken, known, *refs)
+            gram_kernel(parts, [ways[d] for d in taken], known, *refs)
 
         inputs = [leaves[d] for d in taken] + gram
         gram, known = [call(products, table, [near] * len(inputs))(*inputs)], reached
@@ -367,14 +381,13 @@
         jax.ShapeDtypeStruct((seg, columns), BF16),
         [near] * (parts + 2),
     )(gram, own_weights, *(leaves[d] for d in order))
-    pieces = {(0, 0): own, (1, 1): flipped(own, 1)}
-    bits = parts.bit_length() - 2
-    for chip in range(parts // 2 - 1, 0, -1):
-        mirror = sum((chip >> k & 1) << (bits - 1 - k) for k in range(bits))
-        if mirror == chip:
-            came, passed = (2 * chip + 1, 2 * chip + 1), (2 * chip, 2 * chip)
-        else:
-            came, passed = (2 * chip, 2 * mirror), (2 * mirror + 1, 2 * chip + 1)
+    pieces = {ways[0]: own, ways[1]: flipped(own, 1)}
+    chips = sorted(range(1, parts // 2), key=lambda chip: (chip & 1, -chip))
+    for chip in [*(c for c in chips if c != 1), 1]:
+        came = ways[2 * chip]
+        if came[0] == came[1]:
+            came = ways[2 * chip + 1]
+        passed = (came[1] ^ 1, came[0] ^ 1)
         pieces[came] = flipped(own, came)
         pieces[passed] = flipped(pieces[came], 1)
 

time: 41.9 us -> 42.1 us (level)
  starting transfers between devices: 11.9 us -> 13 us
  blocking collectives: 7.84 us -> 7.34 us
    ppermute x14, starting transfers between devices: 11.9 us -> 13 us  [flipped(): return lax.ppermute(value, ('rep', 'shard'), pairs)]
    all_to_all x1, blocking collectives: 7.84 us -> 7.34 us  [body(): lax.all_to_all(gram, ('rep', 'shard'), 0, 0, axis_index_groups=groups)]
where the time goes in v5:
time: 42.1 us; the launch traced here: 41.9 us
  starting transfers between devices  13 us (31%)
  waiting for transfers between devices  12.9 us (31%)
  Pallas kernels  8.63 us (20%)
  blocking collectives  7.34 us (17%)
    ppermute x14, starting transfers between devices, flipped(): return lax.ppermute(value, ('rep', 'shard'), pairs)  13 us
    ppermute x14, waiting for transfers between devices, flipped(): return lax.ppermute(value, ('rep', 'shard'), pairs)  12.9 us
    all_to_all x1, blocking collectives, body(): lax.all_to_all(gram, ('rep', 'shard'), 0, 0, axis_index_groups=groups)  7.34 us
    pallas_call x1, Pallas kernels, body(): call(local, [rows_out, jax.ShapeDtypeStruct((seg, columns), BF16), jax.Sh...  4.79 us
    pallas_call x3, Pallas kernels, body(): call(products, table, [near] * len(inputs))(*inputs)  1.11 us
    pallas_call x1, Pallas kernels, body(): call(place, jax.ShapeDtypeStruct((width, columns), BF16), [any_place] * p...  1.02 us
    pallas_call x1, Pallas kernels, body(): call(combine_kernel, jax.ShapeDtypeStruct((seg, columns), BF16), [near] *...  0.87 us
  transfers between devices with their start and end apart: 14, of which 9 were waited for; matrix products, arithmetic and copies ran while one was open for 0% of the time, Pallas kernels for 4%

profile of v5, /device:TPU:0, one launch (start us, length us, event | category | flops | bytes accessed | tf_op | source)
XLA Modules:
  0.0 41.9 jit_solution(13029857578502535978)
XLA Ops:
  0.0 4.8 %shard_map.46 = (bf16[256,256]{1,0:T(8,128)(2,1)S(1)}, bf16[256,256]{1,0:T(8,128)(2,1)S(1)}, bf16[256,512]{1,0:T(8,128)(2,1)S(1)}, bf16[512,2048]{1,0:T(8,128)(2,1)S(1)}) custom-call(s32[2,1,512]{2,1,0:T(1,128)} %bitcast.10, bf16[384,2048]{1,0:T(8,128)(2,1)} %bitcast.7, bf16[2048,256]{1,0:T(8,128)(2,1)} %bitcast.8, bf16[512,256]{1,0:T(8,128)(2,1)} %bitcast.9), custom_call_target="tpu_custom_call" | custom-call | tf_op jit(solution)/shard_map/pallas_call | solution.py:322
  4.8 4.0 %collective-permute-start = (bf16[256,256]{1,0:T(8,128)(2,1)S(1)}, bf16[256,256]{1,0:T(8,128)(2,1)S(1)}, u32[]{:S(2)}, u32[]{:S(2)}) collective-permute-start(bf16[256,256]{1,0:T(8,128)(2,1)S(1)} %get-tuple-element.19), channel_id=1, source_target_pairs={{0,24},{1,25},{2,26},{3,27},{4,28},{5,29},{6,30},{7,31},{8,16},{9,... | collective-permute-start | bytes 393224 | tf_op jit(solution)/shard_map/ppermute | solution.py:301
  8.8 0.5 %shard_map.47 = (bf16[256,256]{1,0:T(8,128)(2,1)S(1)}, bf16[256,256]{1,0:T(8,128)(2,1)S(1)}, bf16[256,256]{1,0:T(8,128)(2,1)S(1)}, bf16[256,256]{1,0:T(8,128)(2,1)S(1)}, bf16[256,256]{1,0:T(8,128)(2,1)S(1)}) custom-call(bf16[256,512]{1,0:T(8,128)(2,1)S(1)} %get-tuple-element.16.refs_0_, bf16[512,2048]{1,0:T(8,128)(2,1)S(1)} %get-tuple-element.17.refs_1_), custom_call_target="tpu_custom_call" | custom-call | tf_op jit(solution)/shard_map/pallas_call | solution.py:351
  9.3 0.6 %collective-permute-start.1 = (bf16[256,256]{1,0:T(8,128)(2,1)S(1)}, bf16[256,256]{1,0:T(8,128)(2,1)S(1)}, u32[]{:S(2)}, u32[]{:S(2)}) collective-permute-start(bf16[256,256]{1,0:T(8,128)(2,1)S(1)} %get-tuple-element.20), channel_id=1, source_target_pairs={{0,8},{1,9},{2,10},{3,11},{4,20},{5,21},{6,22},{7,23},{8,0},{9,1},... | collective-permute-start | bytes 393224 | tf_op jit(solution)/shard_map/ppermute | solution.py:301
  9.9 0.1 collective-permute-start.2
  9.9 1.5 %collective-permute-start.3 = (bf16[256,256]{1,0:T(8,128)(2,1)S(1)}, bf16[256,256]{1,0:T(8,128)(2,1)S(1)}, u32[]{:S(2)}, u32[]{:S(2)}) collective-permute-start(bf16[256,256]{1,0:T(8,128)(2,1)S(1)} %get-tuple-element.22), channel_id=1, source_target_pairs={{0,28},{1,29},{2,30},{3,31},{4,24},{5,25},{6,26},{7,27},{8,20},{9,... | collective-permute-start | bytes 393224 | tf_op jit(solution)/shard_map/ppermute | solution.py:301
  11.4 1.7 %collective-permute-start.4 = (bf16[256,256]{1,0:T(8,128)(2,1)S(1)}, bf16[256,256]{1,0:T(8,128)(2,1)S(1)}, u32[]{:S(2)}, u32[]{:S(2)}) collective-permute-start(bf16[256,256]{1,0:T(8,128)(2,1)S(1)} %get-tuple-element.23), channel_id=1, source_target_pairs={{0,12},{1,13},{2,14},{3,15},{4,8},{5,9},{6,10},{7,11},{8,4},{9,5},... | collective-permute-start | bytes 393224 | tf_op jit(solution)/shard_map/ppermute | solution.py:301
  13.1 0.0 collective-permute-done.refs_2_.refs_1_.rest_1_
  13.1 0.3 shard_map.48
  13.4 0.1 collective-permute-start.5
  13.5 2.6 %collective-permute-done.1.refs_2_.rest_2_ = bf16[256,256]{1,0:T(8,128)(2,1)S(1)} collective-permute-done((bf16[256,256]{1,0:T(8,128)(2,1)S(1)}, bf16[256,256]{1,0:T(8,128)(2,1)S(1)}, u32[]{:S(2)}, u32[]{:S(2)}) %collective-permute-start.1) | collective-permute-done | bytes 131104 | tf_op jit(solution)/shard_map/ppermute | solution.py:301
  16.1 0.0 collective-permute-start.6
  16.1 0.0 collective-permute-done.2.refs_3_.rest_3_
  16.1 2.1 %collective-permute-done.3.refs_4_.rest_4_ = bf16[256,256]{1,0:T(8,128)(2,1)S(1)} collective-permute-done((bf16[256,256]{1,0:T(8,128)(2,1)S(1)}, bf16[256,256]{1,0:T(8,128)(2,1)S(1)}, u32[]{:S(2)}, u32[]{:S(2)}) %collective-permute-start.3) | collective-permute-done | bytes 131104 | tf_op jit(solution)/shard_map/ppermute | solution.py:301
  18.2 0.4 shard_map.49.refs_6_
  18.6 1.5 %collective-permute-done.4.refs_5_.rest_5_ = bf16[256,256]{1,0:T(8,128)(2,1)S(1)} collective-permute-done((bf16[256,256]{1,0:T(8,128)(2,1)S(1)}, bf16[256,256]{1,0:T(8,128)(2,1)S(1)}, u32[]{:S(2)}, u32[]{:S(2)}) %collective-permute-start.4) | collective-permute-done | bytes 131104 | tf_op jit(solution)/shard_map/ppermute | solution.py:301
  20.2 0.3 shard_map.50.refs_8_
  20.4 0.7 %collective-permute-done.5.refs_6_.rest_6_ = bf16[256,256]{1,0:T(8,128)(2,1)S(1)} collective-permute-done((bf16[256,256]{1,0:T(8,128)(2,1)S(1)}, bf16[256,256]{1,0:T(8,128)(2,1)S(1)}, u32[]{:S(2)}, u32[]{:S(2)}) %collective-permute-start.5) | collective-permute-done | bytes 131104 | tf_op jit(solution)/shard_map/ppermute | solution.py:301
  21.1 0.0 collective-permute-done.6.refs_7_.rest_7_
  21.1 0.4 %shard_map.51 = f32[1,128]{1,0:T(1,128)S(1)} custom-call(bf16[256,256]{1,0:T(8,128)(2,1)S(1)} %get-tuple-element.18.refs_0_.rest_0_, bf16[256,256]{1,0:T(8,128)(2,1)S(1)} %collective-permute-done.refs_2_.refs_1_.rest_1_, bf16[256,256]{1,0:T(8,128)(2,1)S(1)} %collective-permute-done.1.refs_2_.rest_2_, ...), custom_call_target="tpu_custom_call" | custom-call | tf_op jit(solution)/shard_map/pallas_call | solution.py:368
  21.6 7.3 %all_to_all.5.gram_ref = f32[16,1,128]{2,1,0:T(1,128)S(1)} all-to-all(f32[16,1,128]{2,1,0:T(1,128)S(1)} %broadcast_in_dim.6), channel_id=1, replica_groups={{29,28,25,24,21,20,17,16,13,12,9,8,5,4,1,0},{31,30,27,26,23,22,19,18,15..., dimensions={0} | all-to-all | bytes 16384 | tf_op jit(solution)/shard_map/all_to_all | solution.py:377
  28.9 0.9 %shard_map.52.refs_0_ = bf16[256,256]{1,0:T(8,128)(2,1)S(1)} custom-call(f32[16,1,128]{2,1,0:T(1,128)S(1)} %all_to_all.5.gram_ref, bf16[256,256]{1,0:T(8,128)(2,1)S(1)} %get-tuple-element.26.own_ref, bf16[256,256]{1,0:T(8,128)(2,1)S(1)} %get-tuple-element.18.refs_0_.rest_0_, bf16[256,256]{1,0:T(8,128)(2,1)S(1)} %collective-permute-done.refs_2_.refs_1_.rest_1_, ...), custom_call_target="tpu_custom_call" | custom-call | tf_op jit(solution)/shard_map/pallas_call | solution.py:379
  29.8 1.5 %collective-permute-start.12 = (bf16[256,256]{1,0:T(8,128)(2,1)S(1)}, bf16[256,256]{1,0:T(8,128)(2,1)S(1)}, u32[]{:S(2)}, u32[]{:S(2)}) collective-permute-start(bf16[256,256]{1,0:T(8,128)(2,1)S(1)} %shard_map.52.refs_0_), channel_id=1, source_target_pairs={{0,8},{1,9},{2,10},{3,11},{4,20},{5,21},{6,22},{7,23},{8,0},{9,1},... | collective-permute-start | bytes 393224 | tf_op jit(solution)/shard_map/ppermute | solution.py:301
  31.3 0.6 %collective-permute-start.10 = (bf16[256,256]{1,0:T(8,128)(2,1)S(1)}, bf16[256,256]{1,0:T(8,128)(2,1)S(1)}, u32[]{:S(2)}, u32[]{:S(2)}) collective-permute-start(bf16[256,256]{1,0:T(8,128)(2,1)S(1)} %shard_map.52.refs_0_), channel_id=1, source_target_pairs={{0,28},{1,29},{2,30},{3,31},{4,24},{5,25},{6,26},{7,27},{8,20},{9,... | collective-permute-start | bytes 393224 | tf_op jit(solution)/shard_map/ppermute | solution.py:301
  31.9 1.5 %collective-permute-start.8 = (bf16[256,256]{1,0:T(8,128)(2,1)S(1)}, bf16[256,256]{1,0:T(8,128)(2,1)S(1)}, u32[]{:S(2)}, u32[]{:S(2)}) collective-permute-start(bf16[256,256]{1,0:T(8,128)(2,1)S(1)} %shard_map.52.refs_0_), channel_id=1, source_target_pairs={{0,16},{1,17},{2,18},{3,19},{4,12},{5,13},{6,14},{7,15},{8,24},{9,... | collective-permute-start | bytes 393224 | tf_op jit(solution)/shard_map/ppermute | solution.py:301
  33.4 0.7 %collective-permute-start.7 = (bf16[256,256]{1,0:T(8,128)(2,1)S(1)}, bf16[256,256]{1,0:T(8,128)(2,1)S(1)}, u32[]{:S(2)}, u32[]{:S(2)}) collective-permute-start(bf16[256,256]{1,0:T(8,128)(2,1)S(1)} %shard_map.52.refs_0_), channel_id=1, source_target_pairs={{0,4},{1,5},{2,6},{3,7},{4,0},{5,1},{6,2},{7,3},{8,12},{9,13},{10,... | collective-permute-start | bytes 393224 | tf_op jit(solution)/shard_map/ppermute | solution.py:301
  34.1 0.8 %collective-permute-done.12.refs_6_ = bf16[256,256]{1,0:T(8,128)(2,1)S(1)} collective-permute-done((bf16[256,256]{1,0:T(8,128)(2,1)S(1)}, bf16[256,256]{1,0:T(8,128)(2,1)S(1)}, u32[]{:S(2)}, u32[]{:S(2)}) %collective-permute-start.12) | collective-permute-done | bytes 131104 | tf_op jit(solution)/shard_map/ppermute | solution.py:301
  34.8 0.0 collective-permute-start.13
  34.8 3.3 %collective-permute-done.10.refs_4_ = bf16[256,256]{1,0:T(8,128)(2,1)S(1)} collective-permute-done((bf16[256,256]{1,0:T(8,128)(2,1)S(1)}, bf16[256,256]{1,0:T(8,128)(2,1)S(1)}, u32[]{:S(2)}, u32[]{:S(2)}) %collective-permute-start.10) | collective-permute-done | bytes 131104 | tf_op jit(solution)/shard_map/ppermute | solution.py:301
  38.1 0.8 %collective-permute-start.11 = (bf16[256,256]{1,0:T(8,128)(2,1)S(1)}, bf16[256,256]{1,0:T(8,128)(2,1)S(1)}, u32[]{:S(2)}, u32[]{:S(2)}) collective-permute-start(bf16[256,256]{1,0:T(8,128)(2,1)S(1)} %collective-permute-done.10.refs_4_), channel_id=1, source_target_pairs={{0,4},{1,5},{2,6},{3,7},{4,0},{5,1},{6,2},{7,3},{8,12},{9,13},{10,... | collective-permute-start | bytes 393224 | tf_op jit(solution)/shard_map/ppermute | solution.py:301
  38.9 0.6 %collective-permute-done.8.refs_2_ = bf16[256,256]{1,0:T(8,128)(2,1)S(1)} collective-permute-done((bf16[256,256]{1,0:T(8,128)(2,1)S(1)}, bf16[256,256]{1,0:T(8,128)(2,1)S(1)}, u32[]{:S(2)}, u32[]{:S(2)}) %collective-permute-start.8) | collective-permute-done | bytes 131104 | tf_op jit(solution)/shard_map/ppermute | solution.py:301
  39.5 0.0 collective-permute-start.9
  39.6 0.0 collective-permute-done.7.refs_1_
  39.6 0.0 collective-permute-done.13.refs_7_
  39.6 0.3 collective-permute-done.11.refs_5_
  39.9 1.0 %collective-permute-done.9.refs_3_ = bf16[256,256]{1,0:T(8,128)(2,1)S(1)} collective-permute-done((bf16[256,256]{1,0:T(8,128)(2,1)S(1)}, bf16[256,256]{1,0:T(8,128)(2,1)S(1)}, u32[]{:S(2)}, u32[]{:S(2)}) %collective-permute-start.9) | collective-permute-done | bytes 131104 | tf_op jit(solution)/shard_map/ppermute | solution.py:301
  40.9 1.0 %shard_map.53 = bf16[2048,256]{1,0:T(8,128)(2,1)} custom-call(bf16[256,256]{1,0:T(8,128)(2,1)S(1)} %shard_map.52.refs_0_, bf16[256,256]{1,0:T(8,128)(2,1)S(1)} %collective-permute-done.7.refs_1_, bf16[256,256]{1,0:T(8,128)(2,1)S(1)} %collective-permute-done.8.refs_2_, bf16[256,256]{1,0:T(8,128)(2,1)S(1)} %collective-permute-done.9.refs_3_, ...), custom_call_target="tpu_custom_call" | custom-call | tf_op jit(solution)/shard_map/pallas_call | solution.py:397
  (1 shorter events, 0.0 us)
Async XLA Ops:
  4.8 8.3 %collective-permute-start = (bf16[256,256]{1,0:T(8,128)(2,1)S(1)}, bf16[256,256]{1,0:T(8,128)(2,1)S(1)}, u32[]{:S(2)}, u32[]{:S(2)}) collective-permute-start(bf16[256,256]{1,0:T(8,128)(2,1)S(1)} %get-tuple-element.19), channel_id=1, source_target_pairs={{0,24},{1,25},{2,26},{3,27},{4,28},{5,29},{6,30},{7,31},{8,16},{9,... | collective-permute-start | bytes 393224 | tf_op jit(solution)/shard_map/ppermute | solution.py:301
  9.3 6.8 %collective-permute-start.1 = (bf16[256,256]{1,0:T(8,128)(2,1)S(1)}, bf16[256,256]{1,0:T(8,128)(2,1)S(1)}, u32[]{:S(2)}, u32[]{:S(2)}) collective-permute-start(bf16[256,256]{1,0:T(8,128)(2,1)S(1)} %get-tuple-element.20), channel_id=1, source_target_pairs={{0,8},{1,9},{2,10},{3,11},{4,20},{5,21},{6,22},{7,23},{8,0},{9,1},... | collective-permute-start | bytes 393224 | tf_op jit(solution)/shard_map/ppermute | solution.py:301
  9.9 6.2 %collective-permute-start.2 = (bf16[256,256]{1,0:T(8,128)(2,1)S(1)}, bf16[256,256]{1,0:T(8,128)(2,1)S(1)}, u32[]{:S(2)}, u32[]{:S(2)}) collective-permute-start(bf16[256,256]{1,0:T(8,128)(2,1)S(1)} %get-tuple-element.21), channel_id=1, source_target_pairs={{0,16},{1,17},{2,18},{3,19},{4,12},{5,13},{6,14},{7,15},{8,24},{9,... | collective-permute-start | bytes 393224 | tf_op jit(solution)/shard_map/ppermute | solution.py:301
  9.9 8.3 %collective-permute-start.3 = (bf16[256,256]{1,0:T(8,128)(2,1)S(1)}, bf16[256,256]{1,0:T(8,128)(2,1)S(1)}, u32[]{:S(2)}, u32[]{:S(2)}) collective-permute-start(bf16[256,256]{1,0:T(8,128)(2,1)S(1)} %get-tuple-element.22), channel_id=1, source_target_pairs={{0,28},{1,29},{2,30},{3,31},{4,24},{5,25},{6,26},{7,27},{8,20},{9,... | collective-permute-start | bytes 393224 | tf_op jit(solution)/shard_map/ppermute | solution.py:301
  11.4 8.7 %collective-permute-start.4 = (bf16[256,256]{1,0:T(8,128)(2,1)S(1)}, bf16[256,256]{1,0:T(8,128)(2,1)S(1)}, u32[]{:S(2)}, u32[]{:S(2)}) collective-permute-start(bf16[256,256]{1,0:T(8,128)(2,1)S(1)} %get-tuple-element.23), channel_id=1, source_target_pairs={{0,12},{1,13},{2,14},{3,15},{4,8},{5,9},{6,10},{7,11},{8,4},{9,5},... | collective-permute-start | bytes 393224 | tf_op jit(solution)/shard_map/ppermute | solution.py:301
  13.4 7.7 %collective-permute-start.5 = (bf16[256,256]{1,0:T(8,128)(2,1)S(1)}, bf16[256,256]{1,0:T(8,128)(2,1)S(1)}, u32[]{:S(2)}, u32[]{:S(2)}) collective-permute-start(bf16[256,256]{1,0:T(8,128)(2,1)S(1)} %get-tuple-element.24), channel_id=1, source_target_pairs={{0,20},{1,21},{2,22},{3,23},{4,16},{5,17},{6,18},{7,19},{8,28},{9,... | collective-permute-start | bytes 393224 | tf_op jit(solution)/shard_map/ppermute | solution.py:301
  16.1 5.0 %collective-permute-start.6 = (bf16[256,256]{1,0:T(8,128)(2,1)S(1)}, bf16[256,256]{1,0:T(8,128)(2,1)S(1)}, u32[]{:S(2)}, u32[]{:S(2)}) collective-permute-start(bf16[256,256]{1,0:T(8,128)(2,1)S(1)} %get-tuple-element.25), channel_id=1, source_target_pairs={{0,4},{1,5},{2,6},{3,7},{4,0},{5,1},{6,2},{7,3},{8,12},{9,13},{10,... | collective-permute-start | bytes 393224 | tf_op jit(solution)/shard_map/ppermute | solution.py:301
  29.8 5.0 %collective-permute-start.12 = (bf16[256,256]{1,0:T(8,128)(2,1)S(1)}, bf16[256,256]{1,0:T(8,128)(2,1)S(1)}, u32[]{:S(2)}, u32[]{:S(2)}) collective-permute-start(bf16[256,256]{1,0:T(8,128)(2,1)S(1)} %shard_map.52.refs_0_), channel_id=1, source_target_pairs={{0,8},{1,9},{2,10},{3,11},{4,20},{5,21},{6,22},{7,23},{8,0},{9,1},... | collective-permute-start | bytes 393224 | tf_op jit(solution)/shard_map/ppermute | solution.py:301
  31.3 6.8 %collective-permute-start.10 = (bf16[256,256]{1,0:T(8,128)(2,1)S(1)}, bf16[256,256]{1,0:T(8,128)(2,1)S(1)}, u32[]{:S(2)}, u32[]{:S(2)}) collective-permute-start(bf16[256,256]{1,0:T(8,128)(2,1)S(1)} %shard_map.52.refs_0_), channel_id=1, source_target_pairs={{0,28},{1,29},{2,30},{3,31},{4,24},{5,25},{6,26},{7,27},{8,20},{9,... | collective-permute-start | bytes 393224 | tf_op jit(solution)/shard_map/ppermute | solution.py:301
  31.9 7.6 %collective-permute-start.8 = (bf16[256,256]{1,0:T(8,128)(2,1)S(1)}, bf16[256,256]{1,0:T(8,128)(2,1)S(1)}, u32[]{:S(2)}, u32[]{:S(2)}) collective-permute-start(bf16[256,256]{1,0:T(8,128)(2,1)S(1)} %shard_map.52.refs_0_), channel_id=1, source_target_pairs={{0,16},{1,17},{2,18},{3,19},{4,12},{5,13},{6,14},{7,15},{8,24},{9,... | collective-permute-start | bytes 393224 | tf_op jit(solution)/shard_map/ppermute | solution.py:301
  33.4 6.2 %collective-permute-start.7 = (bf16[256,256]{1,0:T(8,128)(2,1)S(1)}, bf16[256,256]{1,0:T(8,128)(2,1)S(1)}, u32[]{:S(2)}, u32[]{:S(2)}) collective-permute-start(bf16[256,256]{1,0:T(8,128)(2,1)S(1)} %shard_map.52.refs_0_), channel_id=1, source_target_pairs={{0,4},{1,5},{2,6},{3,7},{4,0},{5,1},{6,2},{7,3},{8,12},{9,13},{10,... | collective-permute-start | bytes 393224 | tf_op jit(solution)/shard_map/ppermute | solution.py:301
  34.8 4.7 %collective-permute-start.13 = (bf16[256,256]{1,0:T(8,128)(2,1)S(1)}, bf16[256,256]{1,0:T(8,128)(2,1)S(1)}, u32[]{:S(2)}, u32[]{:S(2)}) collective-permute-start(bf16[256,256]{1,0:T(8,128)(2,1)S(1)} %collective-permute-done.12.refs_6_), channel_id=1, source_target_pairs={{0,4},{1,5},{2,6},{3,7},{4,0},{5,1},{6,2},{7,3},{8,12},{9,13},{10,... | collective-permute-start | bytes 393224 | tf_op jit(solution)/shard_map/ppermute | solution.py:301
  38.1 1.8 %collective-permute-start.11 = (bf16[256,256]{1,0:T(8,128)(2,1)S(1)}, bf16[256,256]{1,0:T(8,128)(2,1)S(1)}, u32[]{:S(2)}, u32[]{:S(2)}) collective-permute-start(bf16[256,256]{1,0:T(8,128)(2,1)S(1)} %collective-permute-done.10.refs_4_), channel_id=1, source_target_pairs={{0,4},{1,5},{2,6},{3,7},{4,0},{5,1},{6,2},{7,3},{8,12},{9,13},{10,... | collective-permute-start | bytes 393224 | tf_op jit(solution)/shard_map/ppermute | solution.py:301
  39.5 1.3 %collective-permute-start.9 = (bf16[256,256]{1,0:T(8,128)(2,1)S(1)}, bf16[256,256]{1,0:T(8,128)(2,1)S(1)}, u32[]{:S(2)}, u32[]{:S(2)}) collective-permute-start(bf16[256,256]{1,0:T(8,128)(2,1)S(1)} %collective-permute-done.8.refs_2_), channel_id=1, source_target_pairs={{0,4},{1,5},{2,6},{3,7},{4,0},{5,1},{6,2},{7,3},{8,12},{9,13},{10,... | collective-permute-start | bytes 393224 | tf_op jit(solution)/shard_map/ppermute | solution.py:301

commit v6 on v4

--- a/solution.py
+++ b/solution.py
@@ -372,7 +372,7 @@
     for chip in range(parts // 2 - 1, 0, -1):
         mirror = sum((chip >> k & 1) << (bits - 1 - k) for k in range(bits))
         if mirror == chip:
-            came, passed = (2 * chip + 1, 2 * chip + 1), (2 * chip, 2 * chip)
+            came, passed = (2 * chip, 2 * chip), (2 * chip + 1, 2 * chip + 1)
         else:
             came, passed = (2 * chip, 2 * mirror), (2 * mirror + 1, 2 * chip + 1)
         pieces[came] = flipped(own, came)

time: 41.9 us -> 41.9 us (level)
  starting transfers between devices: 11.9 us -> 11.4 us
  waiting for transfers between devices: 13.3 us -> 13.8 us
    ppermute x14, starting transfers between devices: 11.9 us -> 11.4 us  [flipped(): return lax.ppermute(value, ('rep', 'shard'), pairs)]
    ppermute x14, waiting for transfers between devices: 13.3 us -> 13.8 us  [flipped(): return lax.ppermute(value, ('rep', 'shard'), pairs)]
where the time goes in v6:
time: 41.9 us; the launch traced here: 41.7 us
  waiting for transfers between devices  13.8 us (33%)
  starting transfers between devices  11.4 us (27%)
  Pallas kernels  8.63 us (21%)
  blocking collectives  7.84 us (19%)
    ppermute x14, waiting for transfers between devices, flipped(): return lax.ppermute(value, ('rep', 'shard'), pairs)  13.8 us
    ppermute x14, starting transfers between devices, flipped(): return lax.ppermute(value, ('rep', 'shard'), pairs)  11.4 us
    all_to_all x1, blocking collectives, body(): lax.all_to_all(gram, ('rep', 'shard'), 0, 0, axis_index_groups=groups)  7.84 us
    pallas_call x1, Pallas kernels, body(): call(local, [rows_out, jax.ShapeDtypeStruct((seg, columns), BF16), jax.Sh...  4.79 us
    pallas_call x3, Pallas kernels, body(): call(products, table, [near] * len(inputs))(*inputs)  1.11 us
    pallas_call x1, Pallas kernels, body(): call(place, jax.ShapeDtypeStruct((width, columns), BF16), [any_place] * p...  1.02 us
    pallas_call x1, Pallas kernels, body(): call(combine_kernel, jax.ShapeDtypeStruct((seg, columns), BF16), [near] *...  0.87 us
  transfers between devices with their start and end apart: 14, of which 9 were waited for; matrix products, arithmetic and copies ran while one was open for 0% of the time, Pallas kernels for 4%

profile of v6, /device:TPU:0, one launch (start us, length us, event | category | flops | bytes accessed | tf_op | source)
XLA Modules:
  0.0 41.7 jit_solution(12394420291562004849)
XLA Ops:
  0.0 4.8 %shard_map.46 = (bf16[256,256]{1,0:T(8,128)(2,1)S(1)}, bf16[256,256]{1,0:T(8,128)(2,1)S(1)}, bf16[256,512]{1,0:T(8,128)(2,1)S(1)}, bf16[512,2048]{1,0:T(8,128)(2,1)S(1)}) custom-call(s32[2,1,512]{2,1,0:T(1,128)} %bitcast.10, bf16[384,2048]{1,0:T(8,128)(2,1)} %bitcast.7, bf16[2048,256]{1,0:T(8,128)(2,1)} %bitcast.8, bf16[512,256]{1,0:T(8,128)(2,1)} %bitcast.9), custom_call_target="tpu_custom_call" | custom-call | tf_op jit(solution)/shard_map/pallas_call | solution.py:308
  4.8 4.0 %collective-permute-start = (bf16[256,256]{1,0:T(8,128)(2,1)S(1)}, bf16[256,256]{1,0:T(8,128)(2,1)S(1)}, u32[]{:S(2)}, u32[]{:S(2)}) collective-permute-start(bf16[256,256]{1,0:T(8,128)(2,1)S(1)} %get-tuple-element.19), channel_id=1, source_target_pairs={{0,24},{1,25},{2,26},{3,27},{4,28},{5,29},{6,30},{7,31},{8,16},{9,... | collective-permute-start | bytes 393224 | tf_op jit(solution)/shard_map/ppermute | solution.py:287
  8.8 0.5 %shard_map.47 = (bf16[256,256]{1,0:T(8,128)(2,1)S(1)}, bf16[256,256]{1,0:T(8,128)(2,1)S(1)}, bf16[256,256]{1,0:T(8,128)(2,1)S(1)}, bf16[256,256]{1,0:T(8,128)(2,1)S(1)}, bf16[256,256]{1,0:T(8,128)(2,1)S(1)}) custom-call(bf16[256,512]{1,0:T(8,128)(2,1)S(1)} %get-tuple-element.16.refs_0_, bf16[512,2048]{1,0:T(8,128)(2,1)S(1)} %get-tuple-element.17.refs_1_), custom_call_target="tpu_custom_call" | custom-call | tf_op jit(solution)/shard_map/pallas_call | solution.py:337
  9.3 0.6 %collective-permute-start.1 = (bf16[256,256]{1,0:T(8,128)(2,1)S(1)}, bf16[256,256]{1,0:T(8,128)(2,1)S(1)}, u32[]{:S(2)}, u32[]{:S(2)}) collective-permute-start(bf16[256,256]{1,0:T(8,128)(2,1)S(1)} %get-tuple-element.20), channel_id=1, source_target_pairs={{0,8},{1,9},{2,10},{3,11},{4,12},{5,13},{6,14},{7,15},{8,0},{9,1},... | collective-permute-start | bytes 393224 | tf_op jit(solution)/shard_map/ppermute | solution.py:287
  9.9 0.1 collective-permute-start.2
  9.9 1.5 %collective-permute-start.3 = (bf16[256,256]{1,0:T(8,128)(2,1)S(1)}, bf16[256,256]{1,0:T(8,128)(2,1)S(1)}, u32[]{:S(2)}, u32[]{:S(2)}) collective-permute-start(bf16[256,256]{1,0:T(8,128)(2,1)S(1)} %get-tuple-element.22), channel_id=1, source_target_pairs={{0,28},{1,29},{2,30},{3,31},{4,24},{5,25},{6,26},{7,27},{8,20},{9,... | collective-permute-start | bytes 393224 | tf_op jit(solution)/shard_map/ppermute | solution.py:287
  11.4 1.7 %collective-permute-start.4 = (bf16[256,256]{1,0:T(8,128)(2,1)S(1)}, bf16[256,256]{1,0:T(8,128)(2,1)S(1)}, u32[]{:S(2)}, u32[]{:S(2)}) collective-permute-start(bf16[256,256]{1,0:T(8,128)(2,1)S(1)} %get-tuple-element.23), channel_id=1, source_target_pairs={{0,12},{1,13},{2,14},{3,15},{4,8},{5,9},{6,10},{7,11},{8,4},{9,5},... | collective-permute-start | bytes 393224 | tf_op jit(solution)/shard_map/ppermute | solution.py:287
  13.1 0.0 collective-permute-done.refs_2_.refs_1_.rest_1_
  13.1 0.3 shard_map.48
  13.4 0.1 collective-permute-start.5
  13.5 2.7 %collective-permute-done.1.refs_2_.rest_2_ = bf16[256,256]{1,0:T(8,128)(2,1)S(1)} collective-permute-done((bf16[256,256]{1,0:T(8,128)(2,1)S(1)}, bf16[256,256]{1,0:T(8,128)(2,1)S(1)}, u32[]{:S(2)}, u32[]{:S(2)}) %collective-permute-start.1) | collective-permute-done | bytes 131104 | tf_op jit(solution)/shard_map/ppermute | solution.py:287
  16.2 0.0 collective-permute-start.6
  16.2 1.1 %collective-permute-done.2.refs_3_.rest_3_ = bf16[256,256]{1,0:T(8,128)(2,1)S(1)} collective-permute-done((bf16[256,256]{1,0:T(8,128)(2,1)S(1)}, bf16[256,256]{1,0:T(8,128)(2,1)S(1)}, u32[]{:S(2)}, u32[]{:S(2)}) %collective-permute-start.2) | collective-permute-done | bytes 131104 | tf_op jit(solution)/shard_map/ppermute | solution.py:287
  17.3 0.8 %collective-permute-done.3.refs_4_.rest_4_ = bf16[256,256]{1,0:T(8,128)(2,1)S(1)} collective-permute-done((bf16[256,256]{1,0:T(8,128)(2,1)S(1)}, bf16[256,256]{1,0:T(8,128)(2,1)S(1)}, u32[]{:S(2)}, u32[]{:S(2)}) %collective-permute-start.3) | collective-permute-done | bytes 131104 | tf_op jit(solution)/shard_map/ppermute | solution.py:287
  18.1 0.4 shard_map.49.refs_6_
  18.5 1.6 %collective-permute-done.4.refs_5_.rest_5_ = bf16[256,256]{1,0:T(8,128)(2,1)S(1)} collective-permute-done((bf16[256,256]{1,0:T(8,128)(2,1)S(1)}, bf16[256,256]{1,0:T(8,128)(2,1)S(1)}, u32[]{:S(2)}, u32[]{:S(2)}) %collective-permute-start.4) | collective-permute-done | bytes 131104 | tf_op jit(solution)/shard_map/ppermute | solution.py:287
  20.1 0.3 shard_map.50.refs_8_
  20.3 0.5 %collective-permute-done.5.refs_6_.rest_6_ = bf16[256,256]{1,0:T(8,128)(2,1)S(1)} collective-permute-done((bf16[256,256]{1,0:T(8,128)(2,1)S(1)}, bf16[256,256]{1,0:T(8,128)(2,1)S(1)}, u32[]{:S(2)}, u32[]{:S(2)}) %collective-permute-start.5) | collective-permute-done | bytes 131104 | tf_op jit(solution)/shard_map/ppermute | solution.py:287
  20.8 0.0 collective-permute-done.6.refs_7_.rest_7_
  20.8 0.4 %shard_map.51 = f32[1,128]{1,0:T(1,128)S(1)} custom-call(bf16[256,256]{1,0:T(8,128)(2,1)S(1)} %get-tuple-element.18.refs_0_.rest_0_, bf16[256,256]{1,0:T(8,128)(2,1)S(1)} %collective-permute-done.refs_2_.refs_1_.rest_1_, bf16[256,256]{1,0:T(8,128)(2,1)S(1)} %collective-permute-done.1.refs_2_.rest_2_, ...), custom_call_target="tpu_custom_call" | custom-call | tf_op jit(solution)/shard_map/pallas_call | solution.py:354
  21.3 7.8 %all_to_all.5.gram_ref = f32[16,1,128]{2,1,0:T(1,128)S(1)} all-to-all(f32[16,1,128]{2,1,0:T(1,128)S(1)} %broadcast_in_dim.6), channel_id=1, replica_groups={{29,28,25,24,21,20,17,16,13,12,9,8,5,4,1,0},{31,30,27,26,23,22,19,18,15..., dimensions={0} | all-to-all | bytes 16384 | tf_op jit(solution)/shard_map/all_to_all | solution.py:363
  29.1 0.9 %shard_map.52.refs_0_ = bf16[256,256]{1,0:T(8,128)(2,1)S(1)} custom-call(f32[16,1,128]{2,1,0:T(1,128)S(1)} %all_to_all.5.gram_ref, bf16[256,256]{1,0:T(8,128)(2,1)S(1)} %get-tuple-element.26.own_ref, bf16[256,256]{1,0:T(8,128)(2,1)S(1)} %get-tuple-element.18.refs_0_.rest_0_, bf16[256,256]{1,0:T(8,128)(2,1)S(1)} %collective-permute-done.refs_2_.refs_1_.rest_1_, ...), custom_call_target="tpu_custom_call" | custom-call | tf_op jit(solution)/shard_map/pallas_call | solution.py:365
  30.0 1.6 %collective-permute-start.12 = (bf16[256,256]{1,0:T(8,128)(2,1)S(1)}, bf16[256,256]{1,0:T(8,128)(2,1)S(1)}, u32[]{:S(2)}, u32[]{:S(2)}) collective-permute-start(bf16[256,256]{1,0:T(8,128)(2,1)S(1)} %shard_map.52.refs_0_), channel_id=1, source_target_pairs={{0,8},{1,9},{2,10},{3,11},{4,20},{5,21},{6,22},{7,23},{8,0},{9,1},... | collective-permute-start | bytes 393224 | tf_op jit(solution)/shard_map/ppermute | solution.py:287
  31.6 1.4 %collective-permute-start.10 = (bf16[256,256]{1,0:T(8,128)(2,1)S(1)}, bf16[256,256]{1,0:T(8,128)(2,1)S(1)}, u32[]{:S(2)}, u32[]{:S(2)}) collective-permute-start(bf16[256,256]{1,0:T(8,128)(2,1)S(1)} %shard_map.52.refs_0_), channel_id=1, source_target_pairs={{0,16},{1,17},{2,18},{3,19},{4,12},{5,13},{6,14},{7,15},{8,24},{9,... | collective-permute-start | bytes 393224 | tf_op jit(solution)/shard_map/ppermute | solution.py:287
  33.0 0.5 %collective-permute-start.8 = (bf16[256,256]{1,0:T(8,128)(2,1)S(1)}, bf16[256,256]{1,0:T(8,128)(2,1)S(1)}, u32[]{:S(2)}, u32[]{:S(2)}) collective-permute-start(bf16[256,256]{1,0:T(8,128)(2,1)S(1)} %shard_map.52.refs_0_), channel_id=1, source_target_pairs={{0,24},{1,25},{2,26},{3,27},{4,28},{5,29},{6,30},{7,31},{8,16},{9,... | collective-permute-start | bytes 393224 | tf_op jit(solution)/shard_map/ppermute | solution.py:287
  33.6 0.0 collective-permute-start.7
  33.6 2.8 %collective-permute-done.12.refs_6_ = bf16[256,256]{1,0:T(8,128)(2,1)S(1)} collective-permute-done((bf16[256,256]{1,0:T(8,128)(2,1)S(1)}, bf16[256,256]{1,0:T(8,128)(2,1)S(1)}, u32[]{:S(2)}, u32[]{:S(2)}) %collective-permute-start.12) | collective-permute-done | bytes 131104 | tf_op jit(solution)/shard_map/ppermute | solution.py:287
  36.4 0.0 collective-permute-start.13
  36.4 0.9 %collective-permute-done.10.refs_4_ = bf16[256,256]{1,0:T(8,128)(2,1)S(1)} collective-permute-done((bf16[256,256]{1,0:T(8,128)(2,1)S(1)}, bf16[256,256]{1,0:T(8,128)(2,1)S(1)}, u32[]{:S(2)}, u32[]{:S(2)}) %collective-permute-start.10) | collective-permute-done | bytes 131104 | tf_op jit(solution)/shard_map/ppermute | solution.py:287
  37.3 0.0 collective-permute-start.11
  37.3 2.1 %collective-permute-done.8.refs_2_ = bf16[256,256]{1,0:T(8,128)(2,1)S(1)} collective-permute-done((bf16[256,256]{1,0:T(8,128)(2,1)S(1)}, bf16[256,256]{1,0:T(8,128)(2,1)S(1)}, u32[]{:S(2)}, u32[]{:S(2)}) %collective-permute-start.8) | collective-permute-done | bytes 131104 | tf_op jit(solution)/shard_map/ppermute | solution.py:287
  39.4 0.0 collective-permute-start.9
  39.4 0.0 collective-permute-done.7.refs_1_
  39.4 0.0 collective-permute-done.13.refs_7_
  39.4 0.0 collective-permute-done.11.refs_5_
  39.4 1.3 %collective-permute-done.9.refs_3_ = bf16[256,256]{1,0:T(8,128)(2,1)S(1)} collective-permute-done((bf16[256,256]{1,0:T(8,128)(2,1)S(1)}, bf16[256,256]{1,0:T(8,128)(2,1)S(1)}, u32[]{:S(2)}, u32[]{:S(2)}) %collective-permute-start.9) | collective-permute-done | bytes 131104 | tf_op jit(solution)/shard_map/ppermute | solution.py:287
  40.7 1.0 %shard_map.53 = bf16[2048,256]{1,0:T(8,128)(2,1)} custom-call(bf16[256,256]{1,0:T(8,128)(2,1)S(1)} %shard_map.52.refs_0_, bf16[256,256]{1,0:T(8,128)(2,1)S(1)} %collective-permute-done.7.refs_1_, bf16[256,256]{1,0:T(8,128)(2,1)S(1)} %collective-permute-done.8.refs_2_, bf16[256,256]{1,0:T(8,128)(2,1)S(1)} %collective-permute-done.9.refs_3_, ...), custom_call_target="tpu_custom_call" | custom-call | tf_op jit(solution)/shard_map/pallas_call | solution.py:384
  (1 shorter events, 0.0 us)
Async XLA Ops:
  4.8 8.3 %collective-permute-start = (bf16[256,256]{1,0:T(8,128)(2,1)S(1)}, bf16[256,256]{1,0:T(8,128)(2,1)S(1)}, u32[]{:S(2)}, u32[]{:S(2)}) collective-permute-start(bf16[256,256]{1,0:T(8,128)(2,1)S(1)} %get-tuple-element.19), channel_id=1, source_target_pairs={{0,24},{1,25},{2,26},{3,27},{4,28},{5,29},{6,30},{7,31},{8,16},{9,... | collective-permute-start | bytes 393224 | tf_op jit(solution)/shard_map/ppermute | solution.py:287
  9.3 6.9 %collective-permute-start.1 = (bf16[256,256]{1,0:T(8,128)(2,1)S(1)}, bf16[256,256]{1,0:T(8,128)(2,1)S(1)}, u32[]{:S(2)}, u32[]{:S(2)}) collective-permute-start(bf16[256,256]{1,0:T(8,128)(2,1)S(1)} %get-tuple-element.20), channel_id=1, source_target_pairs={{0,8},{1,9},{2,10},{3,11},{4,12},{5,13},{6,14},{7,15},{8,0},{9,1},... | collective-permute-start | bytes 393224 | tf_op jit(solution)/shard_map/ppermute | solution.py:287
  9.9 7.4 %collective-permute-start.2 = (bf16[256,256]{1,0:T(8,128)(2,1)S(1)}, bf16[256,256]{1,0:T(8,128)(2,1)S(1)}, u32[]{:S(2)}, u32[]{:S(2)}) collective-permute-start(bf16[256,256]{1,0:T(8,128)(2,1)S(1)} %get-tuple-element.21), channel_id=1, source_target_pairs={{0,16},{1,17},{2,18},{3,19},{4,20},{5,21},{6,22},{7,23},{8,24},{9,... | collective-permute-start | bytes 393224 | tf_op jit(solution)/shard_map/ppermute | solution.py:287
  9.9 8.1 %collective-permute-start.3 = (bf16[256,256]{1,0:T(8,128)(2,1)S(1)}, bf16[256,256]{1,0:T(8,128)(2,1)S(1)}, u32[]{:S(2)}, u32[]{:S(2)}) collective-permute-start(bf16[256,256]{1,0:T(8,128)(2,1)S(1)} %get-tuple-element.22), channel_id=1, source_target_pairs={{0,28},{1,29},{2,30},{3,31},{4,24},{5,25},{6,26},{7,27},{8,20},{9,... | collective-permute-start | bytes 393224 | tf_op jit(solution)/shard_map/ppermute | solution.py:287
  11.4 8.6 %collective-permute-start.4 = (bf16[256,256]{1,0:T(8,128)(2,1)S(1)}, bf16[256,256]{1,0:T(8,128)(2,1)S(1)}, u32[]{:S(2)}, u32[]{:S(2)}) collective-permute-start(bf16[256,256]{1,0:T(8,128)(2,1)S(1)} %get-tuple-element.23), channel_id=1, source_target_pairs={{0,12},{1,13},{2,14},{3,15},{4,8},{5,9},{6,10},{7,11},{8,4},{9,5},... | collective-permute-start | bytes 393224 | tf_op jit(solution)/shard_map/ppermute | solution.py:287
  13.4 7.4 %collective-permute-start.5 = (bf16[256,256]{1,0:T(8,128)(2,1)S(1)}, bf16[256,256]{1,0:T(8,128)(2,1)S(1)}, u32[]{:S(2)}, u32[]{:S(2)}) collective-permute-start(bf16[256,256]{1,0:T(8,128)(2,1)S(1)} %get-tuple-element.24), channel_id=1, source_target_pairs={{0,20},{1,21},{2,22},{3,23},{4,16},{5,17},{6,18},{7,19},{8,28},{9,... | collective-permute-start | bytes 393224 | tf_op jit(solution)/shard_map/ppermute | solution.py:287
  16.2 4.6 %collective-permute-start.6 = (bf16[256,256]{1,0:T(8,128)(2,1)S(1)}, bf16[256,256]{1,0:T(8,128)(2,1)S(1)}, u32[]{:S(2)}, u32[]{:S(2)}) collective-permute-start(bf16[256,256]{1,0:T(8,128)(2,1)S(1)} %get-tuple-element.25), channel_id=1, source_target_pairs={{0,4},{1,5},{2,6},{3,7},{4,0},{5,1},{6,2},{7,3},{8,12},{9,13},{10,... | collective-permute-start | bytes 393224 | tf_op jit(solution)/shard_map/ppermute | solution.py:287
  30.0 6.4 %collective-permute-start.12 = (bf16[256,256]{1,0:T(8,128)(2,1)S(1)}, bf16[256,256]{1,0:T(8,128)(2,1)S(1)}, u32[]{:S(2)}, u32[]{:S(2)}) collective-permute-start(bf16[256,256]{1,0:T(8,128)(2,1)S(1)} %shard_map.52.refs_0_), channel_id=1, source_target_pairs={{0,8},{1,9},{2,10},{3,11},{4,20},{5,21},{6,22},{7,23},{8,0},{9,1},... | collective-permute-start | bytes 393224 | tf_op jit(solution)/shard_map/ppermute | solution.py:287
  31.6 5.7 %collective-permute-start.10 = (bf16[256,256]{1,0:T(8,128)(2,1)S(1)}, bf16[256,256]{1,0:T(8,128)(2,1)S(1)}, u32[]{:S(2)}, u32[]{:S(2)}) collective-permute-start(bf16[256,256]{1,0:T(8,128)(2,1)S(1)} %shard_map.52.refs_0_), channel_id=1, source_target_pairs={{0,16},{1,17},{2,18},{3,19},{4,12},{5,13},{6,14},{7,15},{8,24},{9,... | collective-permute-start | bytes 393224 | tf_op jit(solution)/shard_map/ppermute | solution.py:287
  33.0 6.3 %collective-permute-start.8 = (bf16[256,256]{1,0:T(8,128)(2,1)S(1)}, bf16[256,256]{1,0:T(8,128)(2,1)S(1)}, u32[]{:S(2)}, u32[]{:S(2)}) collective-permute-start(bf16[256,256]{1,0:T(8,128)(2,1)S(1)} %shard_map.52.refs_0_), channel_id=1, source_target_pairs={{0,24},{1,25},{2,26},{3,27},{4,28},{5,29},{6,30},{7,31},{8,16},{9,... | collective-permute-start | bytes 393224 | tf_op jit(solution)/shard_map/ppermute | solution.py:287
  33.6 5.8 %collective-permute-start.7 = (bf16[256,256]{1,0:T(8,128)(2,1)S(1)}, bf16[256,256]{1,0:T(8,128)(2,1)S(1)}, u32[]{:S(2)}, u32[]{:S(2)}) collective-permute-start(bf16[256,256]{1,0:T(8,128)(2,1)S(1)} %shard_map.52.refs_0_), channel_id=1, source_target_pairs={{0,4},{1,5},{2,6},{3,7},{4,0},{5,1},{6,2},{7,3},{8,12},{9,13},{10,... | collective-permute-start | bytes 393224 | tf_op jit(solution)/shard_map/ppermute | solution.py:287
  36.4 3.0 %collective-permute-start.13 = (bf16[256,256]{1,0:T(8,128)(2,1)S(1)}, bf16[256,256]{1,0:T(8,128)(2,1)S(1)}, u32[]{:S(2)}, u32[]{:S(2)}) collective-permute-start(bf16[256,256]{1,0:T(8,128)(2,1)S(1)} %collective-permute-done.12.refs_6_), channel_id=1, source_target_pairs={{0,4},{1,5},{2,6},{3,7},{4,0},{5,1},{6,2},{7,3},{8,12},{9,13},{10,... | collective-permute-start | bytes 393224 | tf_op jit(solution)/shard_map/ppermute | solution.py:287
  37.3 2.1 %collective-permute-start.11 = (bf16[256,256]{1,0:T(8,128)(2,1)S(1)}, bf16[256,256]{1,0:T(8,128)(2,1)S(1)}, u32[]{:S(2)}, u32[]{:S(2)}) collective-permute-start(bf16[256,256]{1,0:T(8,128)(2,1)S(1)} %collective-permute-done.10.refs_4_), channel_id=1, source_target_pairs={{0,4},{1,5},{2,6},{3,7},{4,0},{5,1},{6,2},{7,3},{8,12},{9,13},{10,... | collective-permute-start | bytes 393224 | tf_op jit(solution)/shard_map/ppermute | solution.py:287
  39.4 1.3 %collective-permute-start.9 = (bf16[256,256]{1,0:T(8,128)(2,1)S(1)}, bf16[256,256]{1,0:T(8,128)(2,1)S(1)}, u32[]{:S(2)}, u32[]{:S(2)}) collective-permute-start(bf16[256,256]{1,0:T(8,128)(2,1)S(1)} %collective-permute-done.8.refs_2_), channel_id=1, source_target_pairs={{0,4},{1,5},{2,6},{3,7},{4,0},{5,1},{6,2},{7,3},{8,12},{9,13},{10,... | collective-permute-start | bytes 393224 | tf_op jit(solution)/shard_map/ppermute | solution.py:287

commit v7 on v4

--- a/solution.py
+++ b/solution.py
@@ -133,7 +133,7 @@
 
 def distances(parts):
     def far(distance):
-        return (distance == 1, distance & 1, -(distance >> 1).bit_count(), distance)
+        return (distance == 1, -(distance >> 1).bit_count(), distance & 1, distance)
 
     return [0, *sorted(range(1, parts), key=far)]
 

time: 41.9 us -> 42.1 us (level)
  waiting for transfers between devices: 13.3 us -> 13.9 us
    ppermute x14, waiting for transfers between devices: 13.3 us -> 13.9 us  [flipped(): return lax.ppermute(value, ('rep', 'shard'), pairs)]
  transfers between devices with their start and end apart: 14 -> 14, of which waited for: 9 -> 10; matrix products, arithmetic and copies ran while one was open for 0% -> 0% of each run, Pallas kernels for 4% -> 4%
where the time goes in v7:
time: 42.1 us; the launch traced here: 41.9 us
  waiting for transfers between devices  13.9 us (33%)
  starting transfers between devices  11.8 us (28%)
  Pallas kernels  8.62 us (20%)
  blocking collectives  7.44 us (18%)
    ppermute x14, waiting for transfers between devices, flipped(): return lax.ppermute(value, ('rep', 'shard'), pairs)  13.9 us
    ppermute x14, starting transfers between devices, flipped(): return lax.ppermute(value, ('rep', 'shard'), pairs)  11.8 us
    all_to_all x1, blocking collectives, body(): lax.all_to_all(gram, ('rep', 'shard'), 0, 0, axis_index_groups=groups)  7.44 us
    pallas_call x1, Pallas kernels, body(): call(local, [rows_out, jax.ShapeDtypeStruct((seg, columns), BF16), jax.Sh...  4.79 us
    pallas_call x3, Pallas kernels, body(): call(products, table, [near] * len(inputs))(*inputs)  1.11 us
    pallas_call x1, Pallas kernels, body(): call(place, jax.ShapeDtypeStruct((width, columns), BF16), [any_place] * p...  1.02 us
    pallas_call x1, Pallas kernels, body(): call(combine_kernel, jax.ShapeDtypeStruct((seg, columns), BF16), [near] *...  0.87 us
  transfers between devices with their start and end apart: 14, of which 10 were waited for; matrix products, arithmetic and copies ran while one was open for 0% of the time, Pallas kernels for 4%

profile of v7, /device:TPU:0, one launch (start us, length us, event | category | flops | bytes accessed | tf_op | source)
XLA Modules:
  0.0 41.9 jit_solution(8507232014994983950)
XLA Ops:
  0.0 4.8 %shard_map.46 = (bf16[256,256]{1,0:T(8,128)(2,1)S(1)}, bf16[256,256]{1,0:T(8,128)(2,1)S(1)}, bf16[256,512]{1,0:T(8,128)(2,1)S(1)}, bf16[512,2048]{1,0:T(8,128)(2,1)S(1)}) custom-call(s32[2,1,512]{2,1,0:T(1,128)} %bitcast.10, bf16[384,2048]{1,0:T(8,128)(2,1)} %bitcast.7, bf16[2048,256]{1,0:T(8,128)(2,1)} %bitcast.8, bf16[512,256]{1,0:T(8,128)(2,1)} %bitcast.9), custom_call_target="tpu_custom_call" | custom-call | tf_op jit(solution)/shard_map/pallas_call | solution.py:308
  4.8 4.0 %collective-permute-start = (bf16[256,256]{1,0:T(8,128)(2,1)S(1)}, bf16[256,256]{1,0:T(8,128)(2,1)S(1)}, u32[]{:S(2)}, u32[]{:S(2)}) collective-permute-start(bf16[256,256]{1,0:T(8,128)(2,1)S(1)} %get-tuple-element.19), channel_id=1, source_target_pairs={{0,24},{1,25},{2,26},{3,27},{4,28},{5,29},{6,30},{7,31},{8,16},{9,... | collective-permute-start | bytes 393224 | tf_op jit(solution)/shard_map/ppermute | solution.py:287
  8.8 0.5 %shard_map.47 = (bf16[256,256]{1,0:T(8,128)(2,1)S(1)}, bf16[256,256]{1,0:T(8,128)(2,1)S(1)}, bf16[256,256]{1,0:T(8,128)(2,1)S(1)}, bf16[256,256]{1,0:T(8,128)(2,1)S(1)}, bf16[256,256]{1,0:T(8,128)(2,1)S(1)}) custom-call(bf16[256,512]{1,0:T(8,128)(2,1)S(1)} %get-tuple-element.16.refs_0_, bf16[512,2048]{1,0:T(8,128)(2,1)S(1)} %get-tuple-element.17.refs_1_), custom_call_target="tpu_custom_call" | custom-call | tf_op jit(solution)/shard_map/pallas_call | solution.py:337
  9.3 0.1 collective-permute-start.1
  9.4 1.1 %collective-permute-start.2 = (bf16[256,256]{1,0:T(8,128)(2,1)S(1)}, bf16[256,256]{1,0:T(8,128)(2,1)S(1)}, u32[]{:S(2)}, u32[]{:S(2)}) collective-permute-start(bf16[256,256]{1,0:T(8,128)(2,1)S(1)} %get-tuple-element.21), channel_id=1, source_target_pairs={{0,8},{1,9},{2,10},{3,11},{4,12},{5,13},{6,14},{7,15},{8,0},{9,1},... | collective-permute-start | bytes 393224 | tf_op jit(solution)/shard_map/ppermute | solution.py:287
  10.5 1.5 %collective-permute-start.3 = (bf16[256,256]{1,0:T(8,128)(2,1)S(1)}, bf16[256,256]{1,0:T(8,128)(2,1)S(1)}, u32[]{:S(2)}, u32[]{:S(2)}) collective-permute-start(bf16[256,256]{1,0:T(8,128)(2,1)S(1)} %get-tuple-element.22), channel_id=1, source_target_pairs={{0,16},{1,17},{2,18},{3,19},{4,20},{5,21},{6,22},{7,23},{8,24},{9,... | collective-permute-start | bytes 393224 | tf_op jit(solution)/shard_map/ppermute | solution.py:287
  12.0 0.5 %collective-permute-start.4 = (bf16[256,256]{1,0:T(8,128)(2,1)S(1)}, bf16[256,256]{1,0:T(8,128)(2,1)S(1)}, u32[]{:S(2)}, u32[]{:S(2)}) collective-permute-start(bf16[256,256]{1,0:T(8,128)(2,1)S(1)} %get-tuple-element.23), channel_id=1, source_target_pairs={{0,12},{1,13},{2,14},{3,15},{4,8},{5,9},{6,10},{7,11},{8,4},{9,5},... | collective-permute-start | bytes 393224 | tf_op jit(solution)/shard_map/ppermute | solution.py:287
  12.5 0.1 collective-permute-done.refs_2_.refs_1_.rest_1_
  12.7 0.3 shard_map.48
  13.0 0.6 %collective-permute-start.5 = (bf16[256,256]{1,0:T(8,128)(2,1)S(1)}, bf16[256,256]{1,0:T(8,128)(2,1)S(1)}, u32[]{:S(2)}, u32[]{:S(2)}) collective-permute-start(bf16[256,256]{1,0:T(8,128)(2,1)S(1)} %get-tuple-element.24), channel_id=1, source_target_pairs={{0,20},{1,21},{2,22},{3,23},{4,16},{5,17},{6,18},{7,19},{8,28},{9,... | collective-permute-start | bytes 393224 | tf_op jit(solution)/shard_map/ppermute | solution.py:287
  13.6 2.5 %collective-permute-done.1.refs_2_.rest_2_ = bf16[256,256]{1,0:T(8,128)(2,1)S(1)} collective-permute-done((bf16[256,256]{1,0:T(8,128)(2,1)S(1)}, bf16[256,256]{1,0:T(8,128)(2,1)S(1)}, u32[]{:S(2)}, u32[]{:S(2)}) %collective-permute-start.1) | collective-permute-done | bytes 131104 | tf_op jit(solution)/shard_map/ppermute | solution.py:287
  16.1 0.0 collective-permute-start.6
  16.1 2.2 %collective-permute-done.2.refs_3_.rest_3_ = bf16[256,256]{1,0:T(8,128)(2,1)S(1)} collective-permute-done((bf16[256,256]{1,0:T(8,128)(2,1)S(1)}, bf16[256,256]{1,0:T(8,128)(2,1)S(1)}, u32[]{:S(2)}, u32[]{:S(2)}) %collective-permute-start.2) | collective-permute-done | bytes 131104 | tf_op jit(solution)/shard_map/ppermute | solution.py:287
  18.3 0.3 collective-permute-done.3.refs_4_.rest_4_
  18.6 0.4 shard_map.49.refs_6_
  19.0 1.7 %collective-permute-done.4.refs_5_.rest_5_ = bf16[256,256]{1,0:T(8,128)(2,1)S(1)} collective-permute-done((bf16[256,256]{1,0:T(8,128)(2,1)S(1)}, bf16[256,256]{1,0:T(8,128)(2,1)S(1)}, u32[]{:S(2)}, u32[]{:S(2)}) %collective-permute-start.4) | collective-permute-done | bytes 131104 | tf_op jit(solution)/shard_map/ppermute | solution.py:287
  20.8 0.3 shard_map.50.refs_8_
  21.0 0.4 collective-permute-done.5.refs_6_.rest_6_
  21.4 0.0 collective-permute-done.6.refs_7_.rest_7_
  21.4 0.4 %shard_map.51 = f32[1,128]{1,0:T(1,128)S(1)} custom-call(bf16[256,256]{1,0:T(8,128)(2,1)S(1)} %get-tuple-element.18.refs_0_.rest_0_, bf16[256,256]{1,0:T(8,128)(2,1)S(1)} %collective-permute-done.refs_2_.refs_1_.rest_1_, bf16[256,256]{1,0:T(8,128)(2,1)S(1)} %collective-permute-done.1.refs_2_.rest_2_, ...), custom_call_target="tpu_custom_call" | custom-call | tf_op jit(solution)/shard_map/pallas_call | solution.py:354
  21.8 7.4 %all_to_all.5.gram_ref = f32[16,1,128]{2,1,0:T(1,128)S(1)} all-to-all(f32[16,1,128]{2,1,0:T(1,128)S(1)} %broadcast_in_dim.6), channel_id=1, replica_groups={{29,28,25,24,21,20,17,16,13,12,9,8,5,4,1,0},{31,30,27,26,23,22,19,18,15..., dimensions={0} | all-to-all | bytes 16384 | tf_op jit(solution)/shard_map/all_to_all | solution.py:363
  29.3 0.9 %shard_map.52.refs_0_ = bf16[256,256]{1,0:T(8,128)(2,1)S(1)} custom-call(f32[16,1,128]{2,1,0:T(1,128)S(1)} %all_to_all.5.gram_ref, bf16[256,256]{1,0:T(8,128)(2,1)S(1)} %get-tuple-element.26.own_ref, bf16[256,256]{1,0:T(8,128)(2,1)S(1)} %get-tuple-element.18.refs_0_.rest_0_, bf16[256,256]{1,0:T(8,128)(2,1)S(1)} %collective-permute-done.refs_2_.refs_1_.rest_1_, ...), custom_call_target="tpu_custom_call" | custom-call | tf_op jit(solution)/shard_map/pallas_call | solution.py:365
  30.2 1.6 %collective-permute-start.12 = (bf16[256,256]{1,0:T(8,128)(2,1)S(1)}, bf16[256,256]{1,0:T(8,128)(2,1)S(1)}, u32[]{:S(2)}, u32[]{:S(2)}) collective-permute-start(bf16[256,256]{1,0:T(8,128)(2,1)S(1)} %shard_map.52.refs_0_), channel_id=1, source_target_pairs={{0,8},{1,9},{2,10},{3,11},{4,20},{5,21},{6,22},{7,23},{8,0},{9,1},... | collective-permute-start | bytes 393224 | tf_op jit(solution)/shard_map/ppermute | solution.py:287
  31.7 1.4 %collective-permute-start.10 = (bf16[256,256]{1,0:T(8,128)(2,1)S(1)}, bf16[256,256]{1,0:T(8,128)(2,1)S(1)}, u32[]{:S(2)}, u32[]{:S(2)}) collective-permute-start(bf16[256,256]{1,0:T(8,128)(2,1)S(1)} %shard_map.52.refs_0_), channel_id=1, source_target_pairs={{0,16},{1,17},{2,18},{3,19},{4,12},{5,13},{6,14},{7,15},{8,24},{9,... | collective-permute-start | bytes 393224 | tf_op jit(solution)/shard_map/ppermute | solution.py:287
  33.2 0.0 collective-permute-start.8
  33.2 0.7 %collective-permute-start.7 = (bf16[256,256]{1,0:T(8,128)(2,1)S(1)}, bf16[256,256]{1,0:T(8,128)(2,1)S(1)}, u32[]{:S(2)}, u32[]{:S(2)}) collective-permute-start(bf16[256,256]{1,0:T(8,128)(2,1)S(1)} %shard_map.52.refs_0_), channel_id=1, source_target_pairs={{0,4},{1,5},{2,6},{3,7},{4,0},{5,1},{6,2},{7,3},{8,12},{9,13},{10,... | collective-permute-start | bytes 393224 | tf_op jit(solution)/shard_map/ppermute | solution.py:287
  33.8 2.7 %collective-permute-done.12.refs_6_ = bf16[256,256]{1,0:T(8,128)(2,1)S(1)} collective-permute-done((bf16[256,256]{1,0:T(8,128)(2,1)S(1)}, bf16[256,256]{1,0:T(8,128)(2,1)S(1)}, u32[]{:S(2)}, u32[]{:S(2)}) %collective-permute-start.12) | collective-permute-done | bytes 131104 | tf_op jit(solution)/shard_map/ppermute | solution.py:287
  36.5 0.0 collective-permute-start.13
  36.5 0.2 collective-permute-done.10.refs_4_
  36.7 0.3 collective-permute-start.11
  37.0 2.5 %collective-permute-done.8.refs_2_ = bf16[256,256]{1,0:T(8,128)(2,1)S(1)} collective-permute-done((bf16[256,256]{1,0:T(8,128)(2,1)S(1)}, bf16[256,256]{1,0:T(8,128)(2,1)S(1)}, u32[]{:S(2)}, u32[]{:S(2)}) %collective-permute-start.8) | collective-permute-done | bytes 131104 | tf_op jit(solution)/shard_map/ppermute | solution.py:287
  39.5 0.0 collective-permute-start.9
  39.5 0.0 collective-permute-done.7.refs_1_
  39.5 0.0 collective-permute-done.13.refs_7_
  39.5 0.0 collective-permute-done.11.refs_5_
  39.5 1.3 %collective-permute-done.9.refs_3_ = bf16[256,256]{1,0:T(8,128)(2,1)S(1)} collective-permute-done((bf16[256,256]{1,0:T(8,128)(2,1)S(1)}, bf16[256,256]{1,0:T(8,128)(2,1)S(1)}, u32[]{:S(2)}, u32[]{:S(2)}) %collective-permute-start.9) | collective-permute-done | bytes 131104 | tf_op jit(solution)/shard_map/ppermute | solution.py:287
  40.9 1.0 %shard_map.53 = bf16[2048,256]{1,0:T(8,128)(2,1)} custom-call(bf16[256,256]{1,0:T(8,128)(2,1)S(1)} %shard_map.52.refs_0_, bf16[256,256]{1,0:T(8,128)(2,1)S(1)} %collective-permute-done.7.refs_1_, bf16[256,256]{1,0:T(8,128)(2,1)S(1)} %collective-permute-done.8.refs_2_, bf16[256,256]{1,0:T(8,128)(2,1)S(1)} %collective-permute-done.9.refs_3_, ...), custom_call_target="tpu_custom_call" | custom-call | tf_op jit(solution)/shard_map/pallas_call | solution.py:384
  (1 shorter events, 0.0 us)
Async XLA Ops:
  4.8 7.9 %collective-permute-start = (bf16[256,256]{1,0:T(8,128)(2,1)S(1)}, bf16[256,256]{1,0:T(8,128)(2,1)S(1)}, u32[]{:S(2)}, u32[]{:S(2)}) collective-permute-start(bf16[256,256]{1,0:T(8,128)(2,1)S(1)} %get-tuple-element.19), channel_id=1, source_target_pairs={{0,24},{1,25},{2,26},{3,27},{4,28},{5,29},{6,30},{7,31},{8,16},{9,... | collective-permute-start | bytes 393224 | tf_op jit(solution)/shard_map/ppermute | solution.py:287
  9.3 6.8 %collective-permute-start.1 = (bf16[256,256]{1,0:T(8,128)(2,1)S(1)}, bf16[256,256]{1,0:T(8,128)(2,1)S(1)}, u32[]{:S(2)}, u32[]{:S(2)}) collective-permute-start(bf16[256,256]{1,0:T(8,128)(2,1)S(1)} %get-tuple-element.20), channel_id=1, source_target_pairs={{0,28},{1,29},{2,30},{3,31},{4,24},{5,25},{6,26},{7,27},{8,20},{9,... | collective-permute-start | bytes 393224 | tf_op jit(solution)/shard_map/ppermute | solution.py:287
  9.4 8.9 %collective-permute-start.2 = (bf16[256,256]{1,0:T(8,128)(2,1)S(1)}, bf16[256,256]{1,0:T(8,128)(2,1)S(1)}, u32[]{:S(2)}, u32[]{:S(2)}) collective-permute-start(bf16[256,256]{1,0:T(8,128)(2,1)S(1)} %get-tuple-element.21), channel_id=1, source_target_pairs={{0,8},{1,9},{2,10},{3,11},{4,12},{5,13},{6,14},{7,15},{8,0},{9,1},... | collective-permute-start | bytes 393224 | tf_op jit(solution)/shard_map/ppermute | solution.py:287
  10.5 8.1 %collective-permute-start.3 = (bf16[256,256]{1,0:T(8,128)(2,1)S(1)}, bf16[256,256]{1,0:T(8,128)(2,1)S(1)}, u32[]{:S(2)}, u32[]{:S(2)}) collective-permute-start(bf16[256,256]{1,0:T(8,128)(2,1)S(1)} %get-tuple-element.22), channel_id=1, source_target_pairs={{0,16},{1,17},{2,18},{3,19},{4,20},{5,21},{6,22},{7,23},{8,24},{9,... | collective-permute-start | bytes 393224 | tf_op jit(solution)/shard_map/ppermute | solution.py:287
  12.0 8.8 %collective-permute-start.4 = (bf16[256,256]{1,0:T(8,128)(2,1)S(1)}, bf16[256,256]{1,0:T(8,128)(2,1)S(1)}, u32[]{:S(2)}, u32[]{:S(2)}) collective-permute-start(bf16[256,256]{1,0:T(8,128)(2,1)S(1)} %get-tuple-element.23), channel_id=1, source_target_pairs={{0,12},{1,13},{2,14},{3,15},{4,8},{5,9},{6,10},{7,11},{8,4},{9,5},... | collective-permute-start | bytes 393224 | tf_op jit(solution)/shard_map/ppermute | solution.py:287
  13.0 8.4 %collective-permute-start.5 = (bf16[256,256]{1,0:T(8,128)(2,1)S(1)}, bf16[256,256]{1,0:T(8,128)(2,1)S(1)}, u32[]{:S(2)}, u32[]{:S(2)}) collective-permute-start(bf16[256,256]{1,0:T(8,128)(2,1)S(1)} %get-tuple-element.24), channel_id=1, source_target_pairs={{0,20},{1,21},{2,22},{3,23},{4,16},{5,17},{6,18},{7,19},{8,28},{9,... | collective-permute-start | bytes 393224 | tf_op jit(solution)/shard_map/ppermute | solution.py:287
  16.1 5.3 %collective-permute-start.6 = (bf16[256,256]{1,0:T(8,128)(2,1)S(1)}, bf16[256,256]{1,0:T(8,128)(2,1)S(1)}, u32[]{:S(2)}, u32[]{:S(2)}) collective-permute-start(bf16[256,256]{1,0:T(8,128)(2,1)S(1)} %get-tuple-element.25), channel_id=1, source_target_pairs={{0,4},{1,5},{2,6},{3,7},{4,0},{5,1},{6,2},{7,3},{8,12},{9,13},{10,... | collective-permute-start | bytes 393224 | tf_op jit(solution)/shard_map/ppermute | solution.py:287
  30.2 6.4 %collective-permute-start.12 = (bf16[256,256]{1,0:T(8,128)(2,1)S(1)}, bf16[256,256]{1,0:T(8,128)(2,1)S(1)}, u32[]{:S(2)}, u32[]{:S(2)}) collective-permute-start(bf16[256,256]{1,0:T(8,128)(2,1)S(1)} %shard_map.52.refs_0_), channel_id=1, source_target_pairs={{0,8},{1,9},{2,10},{3,11},{4,20},{5,21},{6,22},{7,23},{8,0},{9,1},... | collective-permute-start | bytes 393224 | tf_op jit(solution)/shard_map/ppermute | solution.py:287
  31.7 5.0 %collective-permute-start.10 = (bf16[256,256]{1,0:T(8,128)(2,1)S(1)}, bf16[256,256]{1,0:T(8,128)(2,1)S(1)}, u32[]{:S(2)}, u32[]{:S(2)}) collective-permute-start(bf16[256,256]{1,0:T(8,128)(2,1)S(1)} %shard_map.52.refs_0_), channel_id=1, source_target_pairs={{0,16},{1,17},{2,18},{3,19},{4,12},{5,13},{6,14},{7,15},{8,24},{9,... | collective-permute-start | bytes 393224 | tf_op jit(solution)/shard_map/ppermute | solution.py:287
  33.2 6.3 %collective-permute-start.8 = (bf16[256,256]{1,0:T(8,128)(2,1)S(1)}, bf16[256,256]{1,0:T(8,128)(2,1)S(1)}, u32[]{:S(2)}, u32[]{:S(2)}) collective-permute-start(bf16[256,256]{1,0:T(8,128)(2,1)S(1)} %shard_map.52.refs_0_), channel_id=1, source_target_pairs={{0,28},{1,29},{2,30},{3,31},{4,24},{5,25},{6,26},{7,27},{8,20},{9,... | collective-permute-start | bytes 393224 | tf_op jit(solution)/shard_map/ppermute | solution.py:287
  33.2 6.3 %collective-permute-start.7 = (bf16[256,256]{1,0:T(8,128)(2,1)S(1)}, bf16[256,256]{1,0:T(8,128)(2,1)S(1)}, u32[]{:S(2)}, u32[]{:S(2)}) collective-permute-start(bf16[256,256]{1,0:T(8,128)(2,1)S(1)} %shard_map.52.refs_0_), channel_id=1, source_target_pairs={{0,4},{1,5},{2,6},{3,7},{4,0},{5,1},{6,2},{7,3},{8,12},{9,13},{10,... | collective-permute-start | bytes 393224 | tf_op jit(solution)/shard_map/ppermute | solution.py:287
  36.5 3.0 %collective-permute-start.13 = (bf16[256,256]{1,0:T(8,128)(2,1)S(1)}, bf16[256,256]{1,0:T(8,128)(2,1)S(1)}, u32[]{:S(2)}, u32[]{:S(2)}) collective-permute-start(bf16[256,256]{1,0:T(8,128)(2,1)S(1)} %collective-permute-done.12.refs_6_), channel_id=1, source_target_pairs={{0,4},{1,5},{2,6},{3,7},{4,0},{5,1},{6,2},{7,3},{8,12},{9,13},{10,... | collective-permute-start | bytes 393224 | tf_op jit(solution)/shard_map/ppermute | solution.py:287
  36.7 2.8 %collective-permute-start.11 = (bf16[256,256]{1,0:T(8,128)(2,1)S(1)}, bf16[256,256]{1,0:T(8,128)(2,1)S(1)}, u32[]{:S(2)}, u32[]{:S(2)}) collective-permute-start(bf16[256,256]{1,0:T(8,128)(2,1)S(1)} %collective-permute-done.10.refs_4_), channel_id=1, source_target_pairs={{0,4},{1,5},{2,6},{3,7},{4,0},{5,1},{6,2},{7,3},{8,12},{9,13},{10,... | collective-permute-start | bytes 393224 | tf_op jit(solution)/shard_map/ppermute | solution.py:287
  39.5 1.3 %collective-permute-start.9 = (bf16[256,256]{1,0:T(8,128)(2,1)S(1)}, bf16[256,256]{1,0:T(8,128)(2,1)S(1)}, u32[]{:S(2)}, u32[]{:S(2)}) collective-permute-start(bf16[256,256]{1,0:T(8,128)(2,1)S(1)} %collective-permute-done.8.refs_2_), channel_id=1, source_target_pairs={{0,4},{1,5},{2,6},{3,7},{4,0},{5,1},{6,2},{7,3},{8,12},{9,13},{10,... | collective-permute-start | bytes 393224 | tf_op jit(solution)/shard_map/ppermute | solution.py:287

commit v8 on v4

--- a/solution.py
+++ b/solution.py
@@ -355,7 +355,7 @@
     gram = gram[0]
     shards = lax.axis_size("shard")
     groups = [
-        [i * shards + j for i in range(parts) for j in range(first, first + cut)]
+        [i * shards + j for j in range(first, first + cut) for i in range(parts)]
         for first in range(0, shards, cut)
     ]
     groups = [group[::-1] for group in groups]

time: 41.9 us -> 41.9 us (level)
  no operation moved by 1% of the time
where the time goes in v8:
time: 41.9 us; the launch traced here: 41.7 us
  waiting for transfers between devices  13.2 us (32%)
  starting transfers between devices  11.9 us (28%)
  Pallas kernels  8.63 us (21%)
  blocking collectives  7.86 us (19%)
    ppermute x14, waiting for transfers between devices, flipped(): return lax.ppermute(value, ('rep', 'shard'), pairs)  13.2 us
    ppermute x14, starting transfers between devices, flipped(): return lax.ppermute(value, ('rep', 'shard'), pairs)  11.9 us
    all_to_all x1, blocking collectives, body(): lax.all_to_all(gram, ('rep', 'shard'), 0, 0, axis_index_groups=groups)  7.86 us
    pallas_call x1, Pallas kernels, body(): call(local, [rows_out, jax.ShapeDtypeStruct((seg, columns), BF16), jax.Sh...  4.79 us
    pallas_call x3, Pallas kernels, body(): call(products, table, [near] * len(inputs))(*inputs)  1.11 us
    pallas_call x1, Pallas kernels, body(): call(place, jax.ShapeDtypeStruct((width, columns), BF16), [any_place] * p...  1.02 us
    pallas_call x1, Pallas kernels, body(): call(combine_kernel, jax.ShapeDtypeStruct((seg, columns), BF16), [near] *...  0.87 us
  transfers between devices with their start and end apart: 14, of which 9 were waited for; matrix products, arithmetic and copies ran while one was open for 0% of the time, Pallas kernels for 4%

profile of v8, /device:TPU:0, one launch (start us, length us, event | category | flops | bytes accessed | tf_op | source)
XLA Modules:
  0.0 41.7 jit_solution(7019434399596451551)
XLA Ops:
  0.0 4.8 %shard_map.46 = (bf16[256,256]{1,0:T(8,128)(2,1)S(1)}, bf16[256,256]{1,0:T(8,128)(2,1)S(1)}, bf16[256,512]{1,0:T(8,128)(2,1)S(1)}, bf16[512,2048]{1,0:T(8,128)(2,1)S(1)}) custom-call(s32[2,1,512]{2,1,0:T(1,128)} %bitcast.10, bf16[384,2048]{1,0:T(8,128)(2,1)} %bitcast.7, bf16[2048,256]{1,0:T(8,128)(2,1)} %bitcast.8, bf16[512,256]{1,0:T(8,128)(2,1)} %bitcast.9), custom_call_target="tpu_custom_call" | custom-call | tf_op jit(solution)/shard_map/pallas_call | solution.py:308
  4.8 4.0 %collective-permute-start = (bf16[256,256]{1,0:T(8,128)(2,1)S(1)}, bf16[256,256]{1,0:T(8,128)(2,1)S(1)}, u32[]{:S(2)}, u32[]{:S(2)}) collective-permute-start(bf16[256,256]{1,0:T(8,128)(2,1)S(1)} %get-tuple-element.19), channel_id=1, source_target_pairs={{0,24},{1,25},{2,26},{3,27},{4,28},{5,29},{6,30},{7,31},{8,16},{9,... | collective-permute-start | bytes 393224 | tf_op jit(solution)/shard_map/ppermute | solution.py:287
  8.8 0.5 %shard_map.47 = (bf16[256,256]{1,0:T(8,128)(2,1)S(1)}, bf16[256,256]{1,0:T(8,128)(2,1)S(1)}, bf16[256,256]{1,0:T(8,128)(2,1)S(1)}, bf16[256,256]{1,0:T(8,128)(2,1)S(1)}, bf16[256,256]{1,0:T(8,128)(2,1)S(1)}) custom-call(bf16[256,512]{1,0:T(8,128)(2,1)S(1)} %get-tuple-element.16.refs_0_, bf16[512,2048]{1,0:T(8,128)(2,1)S(1)} %get-tuple-element.17.refs_1_), custom_call_target="tpu_custom_call" | custom-call | tf_op jit(solution)/shard_map/pallas_call | solution.py:337
  9.3 0.6 %collective-permute-start.1 = (bf16[256,256]{1,0:T(8,128)(2,1)S(1)}, bf16[256,256]{1,0:T(8,128)(2,1)S(1)}, u32[]{:S(2)}, u32[]{:S(2)}) collective-permute-start(bf16[256,256]{1,0:T(8,128)(2,1)S(1)} %get-tuple-element.20), channel_id=1, source_target_pairs={{0,8},{1,9},{2,10},{3,11},{4,12},{5,13},{6,14},{7,15},{8,0},{9,1},... | collective-permute-start | bytes 393224 | tf_op jit(solution)/shard_map/ppermute | solution.py:287
  9.9 0.1 collective-permute-start.2
  9.9 1.5 %collective-permute-start.3 = (bf16[256,256]{1,0:T(8,128)(2,1)S(1)}, bf16[256,256]{1,0:T(8,128)(2,1)S(1)}, u32[]{:S(2)}, u32[]{:S(2)}) collective-permute-start(bf16[256,256]{1,0:T(8,128)(2,1)S(1)} %get-tuple-element.22), channel_id=1, source_target_pairs={{0,28},{1,29},{2,30},{3,31},{4,24},{5,25},{6,26},{7,27},{8,20},{9,... | collective-permute-start | bytes 393224 | tf_op jit(solution)/shard_map/ppermute | solution.py:287
  11.4 1.7 %collective-permute-start.4 = (bf16[256,256]{1,0:T(8,128)(2,1)S(1)}, bf16[256,256]{1,0:T(8,128)(2,1)S(1)}, u32[]{:S(2)}, u32[]{:S(2)}) collective-permute-start(bf16[256,256]{1,0:T(8,128)(2,1)S(1)} %get-tuple-element.23), channel_id=1, source_target_pairs={{0,12},{1,13},{2,14},{3,15},{4,8},{5,9},{6,10},{7,11},{8,4},{9,5},... | collective-permute-start | bytes 393224 | tf_op jit(solution)/shard_map/ppermute | solution.py:287
  13.1 0.0 collective-permute-done.refs_2_.refs_1_.rest_1_
  13.1 0.3 shard_map.48
  13.4 0.1 collective-permute-start.5
  13.5 2.7 %collective-permute-done.1.refs_2_.rest_2_ = bf16[256,256]{1,0:T(8,128)(2,1)S(1)} collective-permute-done((bf16[256,256]{1,0:T(8,128)(2,1)S(1)}, bf16[256,256]{1,0:T(8,128)(2,1)S(1)}, u32[]{:S(2)}, u32[]{:S(2)}) %collective-permute-start.1) | collective-permute-done | bytes 131104 | tf_op jit(solution)/shard_map/ppermute | solution.py:287
  16.2 0.0 collective-permute-start.6
  16.2 1.1 %collective-permute-done.2.refs_3_.rest_3_ = bf16[256,256]{1,0:T(8,128)(2,1)S(1)} collective-permute-done((bf16[256,256]{1,0:T(8,128)(2,1)S(1)}, bf16[256,256]{1,0:T(8,128)(2,1)S(1)}, u32[]{:S(2)}, u32[]{:S(2)}) %collective-permute-start.2) | collective-permute-done | bytes 131104 | tf_op jit(solution)/shard_map/ppermute | solution.py:287
  17.3 0.8 %collective-permute-done.3.refs_4_.rest_4_ = bf16[256,256]{1,0:T(8,128)(2,1)S(1)} collective-permute-done((bf16[256,256]{1,0:T(8,128)(2,1)S(1)}, bf16[256,256]{1,0:T(8,128)(2,1)S(1)}, u32[]{:S(2)}, u32[]{:S(2)}) %collective-permute-start.3) | collective-permute-done | bytes 131104 | tf_op jit(solution)/shard_map/ppermute | solution.py:287
  18.1 0.4 shard_map.49.refs_6_
  18.5 1.6 %collective-permute-done.4.refs_5_.rest_5_ = bf16[256,256]{1,0:T(8,128)(2,1)S(1)} collective-permute-done((bf16[256,256]{1,0:T(8,128)(2,1)S(1)}, bf16[256,256]{1,0:T(8,128)(2,1)S(1)}, u32[]{:S(2)}, u32[]{:S(2)}) %collective-permute-start.4) | collective-permute-done | bytes 131104 | tf_op jit(solution)/shard_map/ppermute | solution.py:287
  20.1 0.3 shard_map.50.refs_8_
  20.3 0.5 %collective-permute-done.5.refs_6_.rest_6_ = bf16[256,256]{1,0:T(8,128)(2,1)S(1)} collective-permute-done((bf16[256,256]{1,0:T(8,128)(2,1)S(1)}, bf16[256,256]{1,0:T(8,128)(2,1)S(1)}, u32[]{:S(2)}, u32[]{:S(2)}) %collective-permute-start.5) | collective-permute-done | bytes 131104 | tf_op jit(solution)/shard_map/ppermute | solution.py:287
  20.8 0.0 collective-permute-done.6.refs_7_.rest_7_
  20.8 0.4 %shard_map.51 = f32[1,128]{1,0:T(1,128)S(1)} custom-call(bf16[256,256]{1,0:T(8,128)(2,1)S(1)} %get-tuple-element.18.refs_0_.rest_0_, bf16[256,256]{1,0:T(8,128)(2,1)S(1)} %collective-permute-done.refs_2_.refs_1_.rest_1_, bf16[256,256]{1,0:T(8,128)(2,1)S(1)} %collective-permute-done.1.refs_2_.rest_2_, ...), custom_call_target="tpu_custom_call" | custom-call | tf_op jit(solution)/shard_map/pallas_call | solution.py:354
  21.3 7.9 %all_to_all.5.gram_ref = f32[16,1,128]{2,1,0:T(1,128)S(1)} all-to-all(f32[16,1,128]{2,1,0:T(1,128)S(1)} %broadcast_in_dim.6), channel_id=1, replica_groups={{29,25,21,17,13,9,5,1,28,24,20,16,12,8,4,0},{31,27,23,19,15,11,7,3,30,2..., dimensions={0} | all-to-all | bytes 16384 | tf_op jit(solution)/shard_map/all_to_all | solution.py:363
  29.2 0.9 %shard_map.52.refs_0_ = bf16[256,256]{1,0:T(8,128)(2,1)S(1)} custom-call(f32[16,1,128]{2,1,0:T(1,128)S(1)} %all_to_all.5.gram_ref, bf16[256,256]{1,0:T(8,128)(2,1)S(1)} %get-tuple-element.26.own_ref, bf16[256,256]{1,0:T(8,128)(2,1)S(1)} %get-tuple-element.18.refs_0_.rest_0_, bf16[256,256]{1,0:T(8,128)(2,1)S(1)} %collective-permute-done.refs_2_.refs_1_.rest_1_, ...), custom_call_target="tpu_custom_call" | custom-call | tf_op jit(solution)/shard_map/pallas_call | solution.py:365
  30.0 1.5 %collective-permute-start.12 = (bf16[256,256]{1,0:T(8,128)(2,1)S(1)}, bf16[256,256]{1,0:T(8,128)(2,1)S(1)}, u32[]{:S(2)}, u32[]{:S(2)}) collective-permute-start(bf16[256,256]{1,0:T(8,128)(2,1)S(1)} %shard_map.52.refs_0_), channel_id=1, source_target_pairs={{0,8},{1,9},{2,10},{3,11},{4,20},{5,21},{6,22},{7,23},{8,0},{9,1},... | collective-permute-start | bytes 393224 | tf_op jit(solution)/shard_map/ppermute | solution.py:287
  31.6 1.5 %collective-permute-start.10 = (bf16[256,256]{1,0:T(8,128)(2,1)S(1)}, bf16[256,256]{1,0:T(8,128)(2,1)S(1)}, u32[]{:S(2)}, u32[]{:S(2)}) collective-permute-start(bf16[256,256]{1,0:T(8,128)(2,1)S(1)} %shard_map.52.refs_0_), channel_id=1, source_target_pairs={{0,16},{1,17},{2,18},{3,19},{4,12},{5,13},{6,14},{7,15},{8,24},{9,... | collective-permute-start | bytes 393224 | tf_op jit(solution)/shard_map/ppermute | solution.py:287
  33.0 0.0 collective-permute-start.8
  33.0 0.7 %collective-permute-start.7 = (bf16[256,256]{1,0:T(8,128)(2,1)S(1)}, bf16[256,256]{1,0:T(8,128)(2,1)S(1)}, u32[]{:S(2)}, u32[]{:S(2)}) collective-permute-start(bf16[256,256]{1,0:T(8,128)(2,1)S(1)} %shard_map.52.refs_0_), channel_id=1, source_target_pairs={{0,4},{1,5},{2,6},{3,7},{4,0},{5,1},{6,2},{7,3},{8,12},{9,13},{10,... | collective-permute-start | bytes 393224 | tf_op jit(solution)/shard_map/ppermute | solution.py:287
  33.7 2.7 %collective-permute-done.12.refs_6_ = bf16[256,256]{1,0:T(8,128)(2,1)S(1)} collective-permute-done((bf16[256,256]{1,0:T(8,128)(2,1)S(1)}, bf16[256,256]{1,0:T(8,128)(2,1)S(1)}, u32[]{:S(2)}, u32[]{:S(2)}) %collective-permute-start.12) | collective-permute-done | bytes 131104 | tf_op jit(solution)/shard_map/ppermute | solution.py:287
  36.4 0.0 collective-permute-start.13
  36.4 0.1 collective-permute-done.10.refs_4_
  36.5 0.4 collective-permute-start.11
  36.9 2.4 %collective-permute-done.8.refs_2_ = bf16[256,256]{1,0:T(8,128)(2,1)S(1)} collective-permute-done((bf16[256,256]{1,0:T(8,128)(2,1)S(1)}, bf16[256,256]{1,0:T(8,128)(2,1)S(1)}, u32[]{:S(2)}, u32[]{:S(2)}) %collective-permute-start.8) | collective-permute-done | bytes 131104 | tf_op jit(solution)/shard_map/ppermute | solution.py:287
  39.3 0.0 collective-permute-start.9
  39.3 0.0 collective-permute-done.7.refs_1_
  39.3 0.0 collective-permute-done.13.refs_7_
  39.4 0.0 collective-permute-done.11.refs_5_
  39.4 1.3 %collective-permute-done.9.refs_3_ = bf16[256,256]{1,0:T(8,128)(2,1)S(1)} collective-permute-done((bf16[256,256]{1,0:T(8,128)(2,1)S(1)}, bf16[256,256]{1,0:T(8,128)(2,1)S(1)}, u32[]{:S(2)}, u32[]{:S(2)}) %collective-permute-start.9) | collective-permute-done | bytes 131104 | tf_op jit(solution)/shard_map/ppermute | solution.py:287
  40.7 1.0 %shard_map.53 = bf16[2048,256]{1,0:T(8,128)(2,1)} custom-call(bf16[256,256]{1,0:T(8,128)(2,1)S(1)} %shard_map.52.refs_0_, bf16[256,256]{1,0:T(8,128)(2,1)S(1)} %collective-permute-done.7.refs_1_, bf16[256,256]{1,0:T(8,128)(2,1)S(1)} %collective-permute-done.8.refs_2_, bf16[256,256]{1,0:T(8,128)(2,1)S(1)} %collective-permute-done.9.refs_3_, ...), custom_call_target="tpu_custom_call" | custom-call | tf_op jit(solution)/shard_map/pallas_call | solution.py:384
  (1 shorter events, 0.0 us)
Async XLA Ops:
  4.8 8.3 %collective-permute-start = (bf16[256,256]{1,0:T(8,128)(2,1)S(1)}, bf16[256,256]{1,0:T(8,128)(2,1)S(1)}, u32[]{:S(2)}, u32[]{:S(2)}) collective-permute-start(bf16[256,256]{1,0:T(8,128)(2,1)S(1)} %get-tuple-element.19), channel_id=1, source_target_pairs={{0,24},{1,25},{2,26},{3,27},{4,28},{5,29},{6,30},{7,31},{8,16},{9,... | collective-permute-start | bytes 393224 | tf_op jit(solution)/shard_map/ppermute | solution.py:287
  9.3 6.9 %collective-permute-start.1 = (bf16[256,256]{1,0:T(8,128)(2,1)S(1)}, bf16[256,256]{1,0:T(8,128)(2,1)S(1)}, u32[]{:S(2)}, u32[]{:S(2)}) collective-permute-start(bf16[256,256]{1,0:T(8,128)(2,1)S(1)} %get-tuple-element.20), channel_id=1, source_target_pairs={{0,8},{1,9},{2,10},{3,11},{4,12},{5,13},{6,14},{7,15},{8,0},{9,1},... | collective-permute-start | bytes 393224 | tf_op jit(solution)/shard_map/ppermute | solution.py:287
  9.9 7.4 %collective-permute-start.2 = (bf16[256,256]{1,0:T(8,128)(2,1)S(1)}, bf16[256,256]{1,0:T(8,128)(2,1)S(1)}, u32[]{:S(2)}, u32[]{:S(2)}) collective-permute-start(bf16[256,256]{1,0:T(8,128)(2,1)S(1)} %get-tuple-element.21), channel_id=1, source_target_pairs={{0,16},{1,17},{2,18},{3,19},{4,20},{5,21},{6,22},{7,23},{8,24},{9,... | collective-permute-start | bytes 393224 | tf_op jit(solution)/shard_map/ppermute | solution.py:287
  9.9 8.1 %collective-permute-start.3 = (bf16[256,256]{1,0:T(8,128)(2,1)S(1)}, bf16[256,256]{1,0:T(8,128)(2,1)S(1)}, u32[]{:S(2)}, u32[]{:S(2)}) collective-permute-start(bf16[256,256]{1,0:T(8,128)(2,1)S(1)} %get-tuple-element.22), channel_id=1, source_target_pairs={{0,28},{1,29},{2,30},{3,31},{4,24},{5,25},{6,26},{7,27},{8,20},{9,... | collective-permute-start | bytes 393224 | tf_op jit(solution)/shard_map/ppermute | solution.py:287
  11.4 8.6 %collective-permute-start.4 = (bf16[256,256]{1,0:T(8,128)(2,1)S(1)}, bf16[256,256]{1,0:T(8,128)(2,1)S(1)}, u32[]{:S(2)}, u32[]{:S(2)}) collective-permute-start(bf16[256,256]{1,0:T(8,128)(2,1)S(1)} %get-tuple-element.23), channel_id=1, source_target_pairs={{0,12},{1,13},{2,14},{3,15},{4,8},{5,9},{6,10},{7,11},{8,4},{9,5},... | collective-permute-start | bytes 393224 | tf_op jit(solution)/shard_map/ppermute | solution.py:287
  13.4 7.4 %collective-permute-start.5 = (bf16[256,256]{1,0:T(8,128)(2,1)S(1)}, bf16[256,256]{1,0:T(8,128)(2,1)S(1)}, u32[]{:S(2)}, u32[]{:S(2)}) collective-permute-start(bf16[256,256]{1,0:T(8,128)(2,1)S(1)} %get-tuple-element.24), channel_id=1, source_target_pairs={{0,20},{1,21},{2,22},{3,23},{4,16},{5,17},{6,18},{7,19},{8,28},{9,... | collective-permute-start | bytes 393224 | tf_op jit(solution)/shard_map/ppermute | solution.py:287
  16.2 4.6 %collective-permute-start.6 = (bf16[256,256]{1,0:T(8,128)(2,1)S(1)}, bf16[256,256]{1,0:T(8,128)(2,1)S(1)}, u32[]{:S(2)}, u32[]{:S(2)}) collective-permute-start(bf16[256,256]{1,0:T(8,128)(2,1)S(1)} %get-tuple-element.25), channel_id=1, source_target_pairs={{0,4},{1,5},{2,6},{3,7},{4,0},{5,1},{6,2},{7,3},{8,12},{9,13},{10,... | collective-permute-start | bytes 393224 | tf_op jit(solution)/shard_map/ppermute | solution.py:287
  30.0 6.4 %collective-permute-start.12 = (bf16[256,256]{1,0:T(8,128)(2,1)S(1)}, bf16[256,256]{1,0:T(8,128)(2,1)S(1)}, u32[]{:S(2)}, u32[]{:S(2)}) collective-permute-start(bf16[256,256]{1,0:T(8,128)(2,1)S(1)} %shard_map.52.refs_0_), channel_id=1, source_target_pairs={{0,8},{1,9},{2,10},{3,11},{4,20},{5,21},{6,22},{7,23},{8,0},{9,1},... | collective-permute-start | bytes 393224 | tf_op jit(solution)/shard_map/ppermute | solution.py:287
  31.6 5.0 %collective-permute-start.10 = (bf16[256,256]{1,0:T(8,128)(2,1)S(1)}, bf16[256,256]{1,0:T(8,128)(2,1)S(1)}, u32[]{:S(2)}, u32[]{:S(2)}) collective-permute-start(bf16[256,256]{1,0:T(8,128)(2,1)S(1)} %shard_map.52.refs_0_), channel_id=1, source_target_pairs={{0,16},{1,17},{2,18},{3,19},{4,12},{5,13},{6,14},{7,15},{8,24},{9,... | collective-permute-start | bytes 393224 | tf_op jit(solution)/shard_map/ppermute | solution.py:287
  33.0 6.3 %collective-permute-start.8 = (bf16[256,256]{1,0:T(8,128)(2,1)S(1)}, bf16[256,256]{1,0:T(8,128)(2,1)S(1)}, u32[]{:S(2)}, u32[]{:S(2)}) collective-permute-start(bf16[256,256]{1,0:T(8,128)(2,1)S(1)} %shard_map.52.refs_0_), channel_id=1, source_target_pairs={{0,28},{1,29},{2,30},{3,31},{4,24},{5,25},{6,26},{7,27},{8,20},{9,... | collective-permute-start | bytes 393224 | tf_op jit(solution)/shard_map/ppermute | solution.py:287
  33.0 6.3 %collective-permute-start.7 = (bf16[256,256]{1,0:T(8,128)(2,1)S(1)}, bf16[256,256]{1,0:T(8,128)(2,1)S(1)}, u32[]{:S(2)}, u32[]{:S(2)}) collective-permute-start(bf16[256,256]{1,0:T(8,128)(2,1)S(1)} %shard_map.52.refs_0_), channel_id=1, source_target_pairs={{0,4},{1,5},{2,6},{3,7},{4,0},{5,1},{6,2},{7,3},{8,12},{9,13},{10,... | collective-permute-start | bytes 393224 | tf_op jit(solution)/shard_map/ppermute | solution.py:287
  36.4 2.9 %collective-permute-start.13 = (bf16[256,256]{1,0:T(8,128)(2,1)S(1)}, bf16[256,256]{1,0:T(8,128)(2,1)S(1)}, u32[]{:S(2)}, u32[]{:S(2)}) collective-permute-start(bf16[256,256]{1,0:T(8,128)(2,1)S(1)} %collective-permute-done.12.refs_6_), channel_id=1, source_target_pairs={{0,4},{1,5},{2,6},{3,7},{4,0},{5,1},{6,2},{7,3},{8,12},{9,13},{10,... | collective-permute-start | bytes 393224 | tf_op jit(solution)/shard_map/ppermute | solution.py:287
  36.5 2.8 %collective-permute-start.11 = (bf16[256,256]{1,0:T(8,128)(2,1)S(1)}, bf16[256,256]{1,0:T(8,128)(2,1)S(1)}, u32[]{:S(2)}, u32[]{:S(2)}) collective-permute-start(bf16[256,256]{1,0:T(8,128)(2,1)S(1)} %collective-permute-done.10.refs_4_), channel_id=1, source_target_pairs={{0,4},{1,5},{2,6},{3,7},{4,0},{5,1},{6,2},{7,3},{8,12},{9,13},{10,... | collective-permute-start | bytes 393224 | tf_op jit(solution)/shard_map/ppermute | solution.py:287
  39.3 1.3 %collective-permute-start.9 = (bf16[256,256]{1,0:T(8,128)(2,1)S(1)}, bf16[256,256]{1,0:T(8,128)(2,1)S(1)}, u32[]{:S(2)}, u32[]{:S(2)}) collective-permute-start(bf16[256,256]{1,0:T(8,128)(2,1)S(1)} %collective-permute-done.8.refs_2_), channel_id=1, source_target_pairs={{0,4},{1,5},{2,6},{3,7},{4,0},{5,1},{6,2},{7,3},{8,12},{9,13},{10,... | collective-permute-start | bytes 393224 | tf_op jit(solution)/shard_map/ppermute | solution.py:287

commit v9 on v4

--- a/solution.py
+++ b/solution.py
@@ -342,7 +342,7 @@
 
     table = jax.ShapeDtypeStruct((-(-parts * parts // 128), 128), F32)
     gram, known = [], 0
-    for reached in (parts - 3, parts - 2, parts):
+    for reached in (parts - 3, parts):
         if reached <= known:
             continue
         taken = order[:reached]

time: 41.9 us -> 42 us (level)
    pallas_call x3 -> x2, Pallas kernels: 1.11 us -> 0.98 us  [body(): call(products, table, [near] * len(inputs))(*inputs)]
  transfers between devices with their start and end apart: 14 -> 14, of which waited for: 9 -> 9; matrix products, arithmetic and copies ran while one was open for 0% -> 0% of each run, Pallas kernels for 4% -> 3%
where the time goes in v9:
time: 42 us; the launch traced here: 41.9 us
  waiting for transfers between devices  13.6 us (32%)
  starting transfers between devices  11.9 us (28%)
  Pallas kernels  8.49 us (20%)
  blocking collectives  7.84 us (19%)
    ppermute x14, waiting for transfers between devices, flipped(): return lax.ppermute(value, ('rep', 'shard'), pairs)  13.6 us
    ppermute x14, starting transfers between devices, flipped(): return lax.ppermute(value, ('rep', 'shard'), pairs)  11.9 us
    all_to_all x1, blocking collectives, body(): lax.all_to_all(gram, ('rep', 'shard'), 0, 0, axis_index_groups=groups)  7.84 us
    pallas_call x1, Pallas kernels, body(): call(local, [rows_out, jax.ShapeDtypeStruct((seg, columns), BF16), jax.Sh...  4.79 us
    pallas_call x1, Pallas kernels, body(): call(place, jax.ShapeDtypeStruct((width, columns), BF16), [any_place] * p...  1.02 us
    pallas_call x2, Pallas kernels, body(): call(products, table, [near] * len(inputs))(*inputs)  0.98 us
    pallas_call x1, Pallas kernels, body(): call(combine_kernel, jax.ShapeDtypeStruct((seg, columns), BF16), [near] *...  0.87 us
  transfers between devices with their start and end apart: 14, of which 9 were waited for; matrix products, arithmetic and copies ran while one was open for 0% of the time, Pallas kernels for 3%

profile of v9, /device:TPU:0, one launch (start us, length us, event | category | flops | bytes accessed | tf_op | source)
XLA Modules:
  0.0 41.9 jit_solution(12000953071205091318)
XLA Ops:
  0.0 4.8 %shard_map.46 = (bf16[256,256]{1,0:T(8,128)(2,1)S(1)}, bf16[256,256]{1,0:T(8,128)(2,1)S(1)}, bf16[256,512]{1,0:T(8,128)(2,1)S(1)}, bf16[512,2048]{1,0:T(8,128)(2,1)S(1)}) custom-call(s32[2,1,512]{2,1,0:T(1,128)} %bitcast.10, bf16[384,2048]{1,0:T(8,128)(2,1)} %bitcast.7, bf16[2048,256]{1,0:T(8,128)(2,1)} %bitcast.8, bf16[512,256]{1,0:T(8,128)(2,1)} %bitcast.9), custom_call_target="tpu_custom_call" | custom-call | tf_op jit(solution)/shard_map/pallas_call | solution.py:308
  4.8 4.0 %collective-permute-start = (bf16[256,256]{1,0:T(8,128)(2,1)S(1)}, bf16[256,256]{1,0:T(8,128)(2,1)S(1)}, u32[]{:S(2)}, u32[]{:S(2)}) collective-permute-start(bf16[256,256]{1,0:T(8,128)(2,1)S(1)} %get-tuple-element.19), channel_id=1, source_target_pairs={{0,24},{1,25},{2,26},{3,27},{4,28},{5,29},{6,30},{7,31},{8,16},{9,... | collective-permute-start | bytes 393224 | tf_op jit(solution)/shard_map/ppermute | solution.py:287
  8.8 0.5 %shard_map.47 = (bf16[256,256]{1,0:T(8,128)(2,1)S(1)}, bf16[256,256]{1,0:T(8,128)(2,1)S(1)}, bf16[256,256]{1,0:T(8,128)(2,1)S(1)}, bf16[256,256]{1,0:T(8,128)(2,1)S(1)}, bf16[256,256]{1,0:T(8,128)(2,1)S(1)}) custom-call(bf16[256,512]{1,0:T(8,128)(2,1)S(1)} %get-tuple-element.16.refs_0_, bf16[512,2048]{1,0:T(8,128)(2,1)S(1)} %get-tuple-element.17.refs_1_), custom_call_target="tpu_custom_call" | custom-call | tf_op jit(solution)/shard_map/pallas_call | solution.py:337
  9.3 0.6 %collective-permute-start.1 = (bf16[256,256]{1,0:T(8,128)(2,1)S(1)}, bf16[256,256]{1,0:T(8,128)(2,1)S(1)}, u32[]{:S(2)}, u32[]{:S(2)}) collective-permute-start(bf16[256,256]{1,0:T(8,128)(2,1)S(1)} %get-tuple-element.20), channel_id=1, source_target_pairs={{0,8},{1,9},{2,10},{3,11},{4,12},{5,13},{6,14},{7,15},{8,0},{9,1},... | collective-permute-start | bytes 393224 | tf_op jit(solution)/shard_map/ppermute | solution.py:287
  9.9 0.1 collective-permute-start.2
  9.9 1.5 %collective-permute-start.3 = (bf16[256,256]{1,0:T(8,128)(2,1)S(1)}, bf16[256,256]{1,0:T(8,128)(2,1)S(1)}, u32[]{:S(2)}, u32[]{:S(2)}) collective-permute-start(bf16[256,256]{1,0:T(8,128)(2,1)S(1)} %get-tuple-element.22), channel_id=1, source_target_pairs={{0,28},{1,29},{2,30},{3,31},{4,24},{5,25},{6,26},{7,27},{8,20},{9,... | collective-permute-start | bytes 393224 | tf_op jit(solution)/shard_map/ppermute | solution.py:287
  11.4 1.7 %collective-permute-start.4 = (bf16[256,256]{1,0:T(8,128)(2,1)S(1)}, bf16[256,256]{1,0:T(8,128)(2,1)S(1)}, u32[]{:S(2)}, u32[]{:S(2)}) collective-permute-start(bf16[256,256]{1,0:T(8,128)(2,1)S(1)} %get-tuple-element.23), channel_id=1, source_target_pairs={{0,12},{1,13},{2,14},{3,15},{4,8},{5,9},{6,10},{7,11},{8,4},{9,5},... | collective-permute-start | bytes 393224 | tf_op jit(solution)/shard_map/ppermute | solution.py:287
  13.1 0.0 collective-permute-done.refs_2_.refs_1_.rest_1_
  13.1 0.3 shard_map.48
  13.4 0.1 collective-permute-start.5
  13.5 2.7 %collective-permute-done.1.refs_2_.rest_2_ = bf16[256,256]{1,0:T(8,128)(2,1)S(1)} collective-permute-done((bf16[256,256]{1,0:T(8,128)(2,1)S(1)}, bf16[256,256]{1,0:T(8,128)(2,1)S(1)}, u32[]{:S(2)}, u32[]{:S(2)}) %collective-permute-start.1) | collective-permute-done | bytes 131104 | tf_op jit(solution)/shard_map/ppermute | solution.py:287
  16.2 0.0 collective-permute-start.6
  16.2 1.1 %collective-permute-done.2.refs_3_.rest_3_ = bf16[256,256]{1,0:T(8,128)(2,1)S(1)} collective-permute-done((bf16[256,256]{1,0:T(8,128)(2,1)S(1)}, bf16[256,256]{1,0:T(8,128)(2,1)S(1)}, u32[]{:S(2)}, u32[]{:S(2)}) %collective-permute-start.2) | collective-permute-done | bytes 131104 | tf_op jit(solution)/shard_map/ppermute | solution.py:287
  17.3 0.8 %collective-permute-done.3.refs_4_.rest_4_ = bf16[256,256]{1,0:T(8,128)(2,1)S(1)} collective-permute-done((bf16[256,256]{1,0:T(8,128)(2,1)S(1)}, bf16[256,256]{1,0:T(8,128)(2,1)S(1)}, u32[]{:S(2)}, u32[]{:S(2)}) %collective-permute-start.3) | collective-permute-done | bytes 131104 | tf_op jit(solution)/shard_map/ppermute | solution.py:287
  18.1 0.4 shard_map.49.refs_8_
  18.5 1.6 %collective-permute-done.4.refs_5_.rest_5_ = bf16[256,256]{1,0:T(8,128)(2,1)S(1)} collective-permute-done((bf16[256,256]{1,0:T(8,128)(2,1)S(1)}, bf16[256,256]{1,0:T(8,128)(2,1)S(1)}, u32[]{:S(2)}, u32[]{:S(2)}) %collective-permute-start.4) | collective-permute-done | bytes 131104 | tf_op jit(solution)/shard_map/ppermute | solution.py:287
  20.1 0.8 %collective-permute-done.5.refs_6_.rest_6_ = bf16[256,256]{1,0:T(8,128)(2,1)S(1)} collective-permute-done((bf16[256,256]{1,0:T(8,128)(2,1)S(1)}, bf16[256,256]{1,0:T(8,128)(2,1)S(1)}, u32[]{:S(2)}, u32[]{:S(2)}) %collective-permute-start.5) | collective-permute-done | bytes 131104 | tf_op jit(solution)/shard_map/ppermute | solution.py:287
  20.8 0.0 collective-permute-done.6.refs_7_.rest_7_
  20.8 0.6 %shard_map.50 = f32[1,128]{1,0:T(1,128)S(1)} custom-call(bf16[256,256]{1,0:T(8,128)(2,1)S(1)} %get-tuple-element.18.refs_0_.rest_0_, bf16[256,256]{1,0:T(8,128)(2,1)S(1)} %collective-permute-done.refs_2_.refs_1_.rest_1_, bf16[256,256]{1,0:T(8,128)(2,1)S(1)} %collective-permute-done.1.refs_2_.rest_2_, ...), custom_call_target="tpu_custom_call" | custom-call | tf_op jit(solution)/shard_map/pallas_call | solution.py:354
  21.4 7.8 %all_to_all.5.gram_ref = f32[16,1,128]{2,1,0:T(1,128)S(1)} all-to-all(f32[16,1,128]{2,1,0:T(1,128)S(1)} %broadcast_in_dim.6), channel_id=1, replica_groups={{29,28,25,24,21,20,17,16,13,12,9,8,5,4,1,0},{31,30,27,26,23,22,19,18,15..., dimensions={0} | all-to-all | bytes 16384 | tf_op jit(solution)/shard_map/all_to_all | solution.py:363
  29.3 0.9 %shard_map.51.refs_0_ = bf16[256,256]{1,0:T(8,128)(2,1)S(1)} custom-call(f32[16,1,128]{2,1,0:T(1,128)S(1)} %all_to_all.5.gram_ref, bf16[256,256]{1,0:T(8,128)(2,1)S(1)} %get-tuple-element.26.own_ref, bf16[256,256]{1,0:T(8,128)(2,1)S(1)} %get-tuple-element.18.refs_0_.rest_0_, bf16[256,256]{1,0:T(8,128)(2,1)S(1)} %collective-permute-done.refs_2_.refs_1_.rest_1_, ...), custom_call_target="tpu_custom_call" | custom-call | tf_op jit(solution)/shard_map/pallas_call | solution.py:365
  30.1 1.6 %collective-permute-start.12 = (bf16[256,256]{1,0:T(8,128)(2,1)S(1)}, bf16[256,256]{1,0:T(8,128)(2,1)S(1)}, u32[]{:S(2)}, u32[]{:S(2)}) collective-permute-start(bf16[256,256]{1,0:T(8,128)(2,1)S(1)} %shard_map.51.refs_0_), channel_id=1, source_target_pairs={{0,8},{1,9},{2,10},{3,11},{4,20},{5,21},{6,22},{7,23},{8,0},{9,1},... | collective-permute-start | bytes 393224 | tf_op jit(solution)/shard_map/ppermute | solution.py:287
  31.7 1.4 %collective-permute-start.10 = (bf16[256,256]{1,0:T(8,128)(2,1)S(1)}, bf16[256,256]{1,0:T(8,128)(2,1)S(1)}, u32[]{:S(2)}, u32[]{:S(2)}) collective-permute-start(bf16[256,256]{1,0:T(8,128)(2,1)S(1)} %shard_map.51.refs_0_), channel_id=1, source_target_pairs={{0,16},{1,17},{2,18},{3,19},{4,12},{5,13},{6,14},{7,15},{8,24},{9,... | collective-permute-start | bytes 393224 | tf_op jit(solution)/shard_map/ppermute | solution.py:287
  33.1 0.0 collective-permute-start.8
  33.1 0.7 %collective-permute-start.7 = (bf16[256,256]{1,0:T(8,128)(2,1)S(1)}, bf16[256,256]{1,0:T(8,128)(2,1)S(1)}, u32[]{:S(2)}, u32[]{:S(2)}) collective-permute-start(bf16[256,256]{1,0:T(8,128)(2,1)S(1)} %shard_map.51.refs_0_), channel_id=1, source_target_pairs={{0,4},{1,5},{2,6},{3,7},{4,0},{5,1},{6,2},{7,3},{8,12},{9,13},{10,... | collective-permute-start | bytes 393224 | tf_op jit(solution)/shard_map/ppermute | solution.py:287
  33.8 2.7 %collective-permute-done.12.refs_6_ = bf16[256,256]{1,0:T(8,128)(2,1)S(1)} collective-permute-done((bf16[256,256]{1,0:T(8,128)(2,1)S(1)}, bf16[256,256]{1,0:T(8,128)(2,1)S(1)}, u32[]{:S(2)}, u32[]{:S(2)}) %collective-permute-start.12) | collective-permute-done | bytes 131104 | tf_op jit(solution)/shard_map/ppermute | solution.py:287
  36.5 0.0 collective-permute-start.13
  36.5 0.2 collective-permute-done.10.refs_4_
  36.7 0.3 collective-permute-start.11
  37.0 2.5 %collective-permute-done.8.refs_2_ = bf16[256,256]{1,0:T(8,128)(2,1)S(1)} collective-permute-done((bf16[256,256]{1,0:T(8,128)(2,1)S(1)}, bf16[256,256]{1,0:T(8,128)(2,1)S(1)}, u32[]{:S(2)}, u32[]{:S(2)}) %collective-permute-start.8) | collective-permute-done | bytes 131104 | tf_op jit(solution)/shard_map/ppermute | solution.py:287
  39.5 0.0 collective-permute-start.9
  39.5 0.0 collective-permute-done.7.refs_1_
  39.5 0.0 collective-permute-done.13.refs_7_
  39.5 0.0 collective-permute-done.11.refs_5_
  39.5 1.3 %collective-permute-done.9.refs_3_ = bf16[256,256]{1,0:T(8,128)(2,1)S(1)} collective-permute-done((bf16[256,256]{1,0:T(8,128)(2,1)S(1)}, bf16[256,256]{1,0:T(8,128)(2,1)S(1)}, u32[]{:S(2)}, u32[]{:S(2)}) %collective-permute-start.9) | collective-permute-done | bytes 131104 | tf_op jit(solution)/shard_map/ppermute | solution.py:287
  40.8 1.0 %shard_map.52 = bf16[2048,256]{1,0:T(8,128)(2,1)} custom-call(bf16[256,256]{1,0:T(8,128)(2,1)S(1)} %shard_map.51.refs_0_, bf16[256,256]{1,0:T(8,128)(2,1)S(1)} %collective-permute-done.7.refs_1_, bf16[256,256]{1,0:T(8,128)(2,1)S(1)} %collective-permute-done.8.refs_2_, bf16[256,256]{1,0:T(8,128)(2,1)S(1)} %collective-permute-done.9.refs_3_, ...), custom_call_target="tpu_custom_call" | custom-call | tf_op jit(solution)/shard_map/pallas_call | solution.py:384
  (1 shorter events, 0.0 us)
Async XLA Ops:
  4.8 8.3 %collective-permute-start = (bf16[256,256]{1,0:T(8,128)(2,1)S(1)}, bf16[256,256]{1,0:T(8,128)(2,1)S(1)}, u32[]{:S(2)}, u32[]{:S(2)}) collective-permute-start(bf16[256,256]{1,0:T(8,128)(2,1)S(1)} %get-tuple-element.19), channel_id=1, source_target_pairs={{0,24},{1,25},{2,26},{3,27},{4,28},{5,29},{6,30},{7,31},{8,16},{9,... | collective-permute-start | bytes 393224 | tf_op jit(solution)/shard_map/ppermute | solution.py:287
  9.3 6.9 %collective-permute-start.1 = (bf16[256,256]{1,0:T(8,128)(2,1)S(1)}, bf16[256,256]{1,0:T(8,128)(2,1)S(1)}, u32[]{:S(2)}, u32[]{:S(2)}) collective-permute-start(bf16[256,256]{1,0:T(8,128)(2,1)S(1)} %get-tuple-element.20), channel_id=1, source_target_pairs={{0,8},{1,9},{2,10},{3,11},{4,12},{5,13},{6,14},{7,15},{8,0},{9,1},... | collective-permute-start | bytes 393224 | tf_op jit(solution)/shard_map/ppermute | solution.py:287
  9.9 7.4 %collective-permute-start.2 = (bf16[256,256]{1,0:T(8,128)(2,1)S(1)}, bf16[256,256]{1,0:T(8,128)(2,1)S(1)}, u32[]{:S(2)}, u32[]{:S(2)}) collective-permute-start(bf16[256,256]{1,0:T(8,128)(2,1)S(1)} %get-tuple-element.21), channel_id=1, source_target_pairs={{0,16},{1,17},{2,18},{3,19},{4,20},{5,21},{6,22},{7,23},{8,24},{9,... | collective-permute-start | bytes 393224 | tf_op jit(solution)/shard_map/ppermute | solution.py:287
  9.9 8.1 %collective-permute-start.3 = (bf16[256,256]{1,0:T(8,128)(2,1)S(1)}, bf16[256,256]{1,0:T(8,128)(2,1)S(1)}, u32[]{:S(2)}, u32[]{:S(2)}) collective-permute-start(bf16[256,256]{1,0:T(8,128)(2,1)S(1)} %get-tuple-element.22), channel_id=1, source_target_pairs={{0,28},{1,29},{2,30},{3,31},{4,24},{5,25},{6,26},{7,27},{8,20},{9,... | collective-permute-start | bytes 393224 | tf_op jit(solution)/shard_map/ppermute | solution.py:287
  11.4 8.6 %collective-permute-start.4 = (bf16[256,256]{1,0:T(8,128)(2,1)S(1)}, bf16[256,256]{1,0:T(8,128)(2,1)S(1)}, u32[]{:S(2)}, u32[]{:S(2)}) collective-permute-start(bf16[256,256]{1,0:T(8,128)(2,1)S(1)} %get-tuple-element.23), channel_id=1, source_target_pairs={{0,12},{1,13},{2,14},{3,15},{4,8},{5,9},{6,10},{7,11},{8,4},{9,5},... | collective-permute-start | bytes 393224 | tf_op jit(solution)/shard_map/ppermute | solution.py:287
  13.4 7.4 %collective-permute-start.5 = (bf16[256,256]{1,0:T(8,128)(2,1)S(1)}, bf16[256,256]{1,0:T(8,128)(2,1)S(1)}, u32[]{:S(2)}, u32[]{:S(2)}) collective-permute-start(bf16[256,256]{1,0:T(8,128)(2,1)S(1)} %get-tuple-element.24), channel_id=1, source_target_pairs={{0,20},{1,21},{2,22},{3,23},{4,16},{5,17},{6,18},{7,19},{8,28},{9,... | collective-permute-start | bytes 393224 | tf_op jit(solution)/shard_map/ppermute | solution.py:287
  16.2 4.6 %collective-permute-start.6 = (bf16[256,256]{1,0:T(8,128)(2,1)S(1)}, bf16[256,256]{1,0:T(8,128)(2,1)S(1)}, u32[]{:S(2)}, u32[]{:S(2)}) collective-permute-start(bf16[256,256]{1,0:T(8,128)(2,1)S(1)} %get-tuple-element.25), channel_id=1, source_target_pairs={{0,4},{1,5},{2,6},{3,7},{4,0},{5,1},{6,2},{7,3},{8,12},{9,13},{10,... | collective-permute-start | bytes 393224 | tf_op jit(solution)/shard_map/ppermute | solution.py:287
  30.1 6.4 %collective-permute-start.12 = (bf16[256,256]{1,0:T(8,128)(2,1)S(1)}, bf16[256,256]{1,0:T(8,128)(2,1)S(1)}, u32[]{:S(2)}, u32[]{:S(2)}) collective-permute-start(bf16[256,256]{1,0:T(8,128)(2,1)S(1)} %shard_map.51.refs_0_), channel_id=1, source_target_pairs={{0,8},{1,9},{2,10},{3,11},{4,20},{5,21},{6,22},{7,23},{8,0},{9,1},... | collective-permute-start | bytes 393224 | tf_op jit(solution)/shard_map/ppermute | solution.py:287
  31.7 5.0 %collective-permute-start.10 = (bf16[256,256]{1,0:T(8,128)(2,1)S(1)}, bf16[256,256]{1,0:T(8,128)(2,1)S(1)}, u32[]{:S(2)}, u32[]{:S(2)}) collective-permute-start(bf16[256,256]{1,0:T(8,128)(2,1)S(1)} %shard_map.51.refs_0_), channel_id=1, source_target_pairs={{0,16},{1,17},{2,18},{3,19},{4,12},{5,13},{6,14},{7,15},{8,24},{9,... | collective-permute-start | bytes 393224 | tf_op jit(solution)/shard_map/ppermute | solution.py:287
  33.1 6.3 %collective-permute-start.8 = (bf16[256,256]{1,0:T(8,128)(2,1)S(1)}, bf16[256,256]{1,0:T(8,128)(2,1)S(1)}, u32[]{:S(2)}, u32[]{:S(2)}) collective-permute-start(bf16[256,256]{1,0:T(8,128)(2,1)S(1)} %shard_map.51.refs_0_), channel_id=1, source_target_pairs={{0,28},{1,29},{2,30},{3,31},{4,24},{5,25},{6,26},{7,27},{8,20},{9,... | collective-permute-start | bytes 393224 | tf_op jit(solution)/shard_map/ppermute | solution.py:287
  33.1 6.3 %collective-permute-start.7 = (bf16[256,256]{1,0:T(8,128)(2,1)S(1)}, bf16[256,256]{1,0:T(8,128)(2,1)S(1)}, u32[]{:S(2)}, u32[]{:S(2)}) collective-permute-start(bf16[256,256]{1,0:T(8,128)(2,1)S(1)} %shard_map.51.refs_0_), channel_id=1, source_target_pairs={{0,4},{1,5},{2,6},{3,7},{4,0},{5,1},{6,2},{7,3},{8,12},{9,13},{10,... | collective-permute-start | bytes 393224 | tf_op jit(solution)/shard_map/ppermute | solution.py:287
  36.5 3.0 %collective-permute-start.13 = (bf16[256,256]{1,0:T(8,128)(2,1)S(1)}, bf16[256,256]{1,0:T(8,128)(2,1)S(1)}, u32[]{:S(2)}, u32[]{:S(2)}) collective-permute-start(bf16[256,256]{1,0:T(8,128)(2,1)S(1)} %collective-permute-done.12.refs_6_), channel_id=1, source_target_pairs={{0,4},{1,5},{2,6},{3,7},{4,0},{5,1},{6,2},{7,3},{8,12},{9,13},{10,... | collective-permute-start | bytes 393224 | tf_op jit(solution)/shard_map/ppermute | solution.py:287
  36.7 2.8 %collective-permute-start.11 = (bf16[256,256]{1,0:T(8,128)(2,1)S(1)}, bf16[256,256]{1,0:T(8,128)(2,1)S(1)}, u32[]{:S(2)}, u32[]{:S(2)}) collective-permute-start(bf16[256,256]{1,0:T(8,128)(2,1)S(1)} %collective-permute-done.10.refs_4_), channel_id=1, source_target_pairs={{0,4},{1,5},{2,6},{3,7},{4,0},{5,1},{6,2},{7,3},{8,12},{9,13},{10,... | collective-permute-start | bytes 393224 | tf_op jit(solution)/shard_map/ppermute | solution.py:287
  39.5 1.3 %collective-permute-start.9 = (bf16[256,256]{1,0:T(8,128)(2,1)S(1)}, bf16[256,256]{1,0:T(8,128)(2,1)S(1)}, u32[]{:S(2)}, u32[]{:S(2)}) collective-permute-start(bf16[256,256]{1,0:T(8,128)(2,1)S(1)} %collective-permute-done.8.refs_2_), channel_id=1, source_target_pairs={{0,4},{1,5},{2,6},{3,7},{4,0},{5,1},{6,2},{7,3},{8,12},{9,13},{10,... | collective-permute-start | bytes 393224 | tf_op jit(solution)/shard_map/ppermute | solution.py:287

commit v10 on v4

--- a/solution.py
+++ b/solution.py
@@ -323,7 +323,7 @@
         ],
     )(hold(row_index[0]), hold(token_pool[0]), hold(weights[0]), hold(targets[0, 0]))
     leaves = {first: flipped(out, first)}
-    middle = max(2, parts - 2)
+    middle = max(2, parts - 1)
     for group, after in (
         ([0, *order[2:middle]], []),
         (order[middle:], [leaves[first]]),

time: 41.9 us -> 41.9 us (level)
  no operation moved by 1% of the time
where the time goes in v10:
time: 41.9 us; the launch traced here: 41.7 us
  waiting for transfers between devices  13.4 us (32%)
  starting transfers between devices  11.8 us (28%)
  Pallas kernels  8.63 us (21%)
  blocking collectives  7.85 us (19%)
    ppermute x14, waiting for transfers between devices, flipped(): return lax.ppermute(value, ('rep', 'shard'), pairs)  13.4 us
    ppermute x14, starting transfers between devices, flipped(): return lax.ppermute(value, ('rep', 'shard'), pairs)  11.8 us
    all_to_all x1, blocking collectives, body(): lax.all_to_all(gram, ('rep', 'shard'), 0, 0, axis_index_groups=groups)  7.85 us
    pallas_call x1, Pallas kernels, body(): call(local, [rows_out, jax.ShapeDtypeStruct((seg, columns), BF16), jax.Sh...  4.79 us
    pallas_call x3, Pallas kernels, body(): call(products, table, [near] * len(inputs))(*inputs)  1.11 us
    pallas_call x1, Pallas kernels, body(): call(place, jax.ShapeDtypeStruct((width, columns), BF16), [any_place] * p...  1.02 us
    pallas_call x1, Pallas kernels, body(): call(combine_kernel, jax.ShapeDtypeStruct((seg, columns), BF16), [near] *...  0.87 us
  transfers between devices with their start and end apart: 14, of which 9 were waited for; matrix products, arithmetic and copies ran while one was open for 0% of the time, Pallas kernels for 4%

profile of v10, /device:TPU:0, one launch (start us, length us, event | category | flops | bytes accessed | tf_op | source)
XLA Modules:
  0.0 41.7 jit_solution(1863391173272697478)
XLA Ops:
  0.0 4.8 %shard_map.46 = (bf16[256,256]{1,0:T(8,128)(2,1)S(1)}, bf16[256,256]{1,0:T(8,128)(2,1)S(1)}, bf16[256,512]{1,0:T(8,128)(2,1)S(1)}, bf16[512,2048]{1,0:T(8,128)(2,1)S(1)}) custom-call(s32[2,1,512]{2,1,0:T(1,128)} %bitcast.10, bf16[384,2048]{1,0:T(8,128)(2,1)} %bitcast.7, bf16[2048,256]{1,0:T(8,128)(2,1)} %bitcast.8, bf16[512,256]{1,0:T(8,128)(2,1)} %bitcast.9), custom_call_target="tpu_custom_call" | custom-call | tf_op jit(solution)/shard_map/pallas_call | solution.py:308
  4.8 4.0 %collective-permute-start = (bf16[256,256]{1,0:T(8,128)(2,1)S(1)}, bf16[256,256]{1,0:T(8,128)(2,1)S(1)}, u32[]{:S(2)}, u32[]{:S(2)}) collective-permute-start(bf16[256,256]{1,0:T(8,128)(2,1)S(1)} %get-tuple-element.18), channel_id=1, source_target_pairs={{0,24},{1,25},{2,26},{3,27},{4,28},{5,29},{6,30},{7,31},{8,16},{9,... | collective-permute-start | bytes 393224 | tf_op jit(solution)/shard_map/ppermute | solution.py:287
  8.8 0.6 %shard_map.47 = (bf16[256,256]{1,0:T(8,128)(2,1)S(1)}, bf16[256,256]{1,0:T(8,128)(2,1)S(1)}, bf16[256,256]{1,0:T(8,128)(2,1)S(1)}, bf16[256,256]{1,0:T(8,128)(2,...) custom-call(bf16[256,512]{1,0:T(8,128)(2,1)S(1)} %get-tuple-element.15.refs_0_, ...), custom_call_target="tpu_custom_call" | custom-call | tf_op jit(solution)/shard_map/pallas_call | solution.py:337
  9.4 0.6 %collective-permute-start.1 = (bf16[256,256]{1,0:T(8,128)(2,1)S(1)}, bf16[256,256]{1,0:T(8,128)(2,1)S(1)}, u32[]{:S(2)}, u32[]{:S(2)}) collective-permute-start(bf16[256,256]{1,0:T(8,128)(2,1)S(1)} %get-tuple-element.19), channel_id=1, source_target_pairs={{0,8},{1,9},{2,10},{3,11},{4,12},{5,13},{6,14},{7,15},{8,0},{9,1},... | collective-permute-start | bytes 393224 | tf_op jit(solution)/shard_map/ppermute | solution.py:287
  10.0 0.1 collective-permute-start.2
  10.0 1.5 %collective-permute-start.3 = (bf16[256,256]{1,0:T(8,128)(2,1)S(1)}, bf16[256,256]{1,0:T(8,128)(2,1)S(1)}, u32[]{:S(2)}, u32[]{:S(2)}) collective-permute-start(bf16[256,256]{1,0:T(8,128)(2,1)S(1)} %get-tuple-element.21), channel_id=1, source_target_pairs={{0,28},{1,29},{2,30},{3,31},{4,24},{5,25},{6,26},{7,27},{8,20},{9,... | collective-permute-start | bytes 393224 | tf_op jit(solution)/shard_map/ppermute | solution.py:287
  11.5 1.7 %collective-permute-start.4 = (bf16[256,256]{1,0:T(8,128)(2,1)S(1)}, bf16[256,256]{1,0:T(8,128)(2,1)S(1)}, u32[]{:S(2)}, u32[]{:S(2)}) collective-permute-start(bf16[256,256]{1,0:T(8,128)(2,1)S(1)} %get-tuple-element.22), channel_id=1, source_target_pairs={{0,12},{1,13},{2,14},{3,15},{4,8},{5,9},{6,10},{7,11},{8,4},{9,5},... | collective-permute-start | bytes 393224 | tf_op jit(solution)/shard_map/ppermute | solution.py:287
  13.2 0.0 collective-permute-done.refs_2_.refs_1_.rest_1_
  13.2 0.0 collective-permute-start.5
  13.2 0.2 shard_map.48
  13.5 2.7 %collective-permute-done.1.refs_2_.rest_2_ = bf16[256,256]{1,0:T(8,128)(2,1)S(1)} collective-permute-done((bf16[256,256]{1,0:T(8,128)(2,1)S(1)}, bf16[256,256]{1,0:T(8,128)(2,1)S(1)}, u32[]{:S(2)}, u32[]{:S(2)}) %collective-permute-start.1) | collective-permute-done | bytes 131104 | tf_op jit(solution)/shard_map/ppermute | solution.py:287
  16.1 0.0 collective-permute-start.6
  16.2 1.2 %collective-permute-done.2.refs_3_.rest_3_ = bf16[256,256]{1,0:T(8,128)(2,1)S(1)} collective-permute-done((bf16[256,256]{1,0:T(8,128)(2,1)S(1)}, bf16[256,256]{1,0:T(8,128)(2,1)S(1)}, u32[]{:S(2)}, u32[]{:S(2)}) %collective-permute-start.2) | collective-permute-done | bytes 131104 | tf_op jit(solution)/shard_map/ppermute | solution.py:287
  17.4 0.6 %collective-permute-done.3.refs_4_.rest_4_ = bf16[256,256]{1,0:T(8,128)(2,1)S(1)} collective-permute-done((bf16[256,256]{1,0:T(8,128)(2,1)S(1)}, bf16[256,256]{1,0:T(8,128)(2,1)S(1)}, u32[]{:S(2)}, u32[]{:S(2)}) %collective-permute-start.3) | collective-permute-done | bytes 131104 | tf_op jit(solution)/shard_map/ppermute | solution.py:287
  18.0 0.4 shard_map.49.refs_6_
  18.4 1.7 %collective-permute-done.4.refs_5_.rest_5_ = bf16[256,256]{1,0:T(8,128)(2,1)S(1)} collective-permute-done((bf16[256,256]{1,0:T(8,128)(2,1)S(1)}, bf16[256,256]{1,0:T(8,128)(2,1)S(1)}, u32[]{:S(2)}, u32[]{:S(2)}) %collective-permute-start.4) | collective-permute-done | bytes 131104 | tf_op jit(solution)/shard_map/ppermute | solution.py:287
  20.1 0.3 shard_map.50.refs_8_
  20.4 0.4 %collective-permute-done.5.refs_6_.rest_6_ = bf16[256,256]{1,0:T(8,128)(2,1)S(1)} collective-permute-done((bf16[256,256]{1,0:T(8,128)(2,1)S(1)}, bf16[256,256]{1,0:T(8,128)(2,1)S(1)}, u32[]{:S(2)}, u32[]{:S(2)}) %collective-permute-start.5) | collective-permute-done | bytes 131104 | tf_op jit(solution)/shard_map/ppermute | solution.py:287
  20.8 0.0 collective-permute-done.6.refs_7_.rest_7_
  20.8 0.4 %shard_map.51 = f32[1,128]{1,0:T(1,128)S(1)} custom-call(bf16[256,256]{1,0:T(8,128)(2,1)S(1)} %get-tuple-element.17.refs_0_.rest_0_, bf16[256,256]{1,0:T(8,128)(2,1)S(1)} %collective-permute-done.refs_2_.refs_1_.rest_1_, bf16[256,256]{1,0:T(8,128)(2,1)S(1)} %collective-permute-done.1.refs_2_.rest_2_, ...), custom_call_target="tpu_custom_call" | custom-call | tf_op jit(solution)/shard_map/pallas_call | solution.py:354
  21.3 7.8 %all_to_all.5.gram_ref = f32[16,1,128]{2,1,0:T(1,128)S(1)} all-to-all(f32[16,1,128]{2,1,0:T(1,128)S(1)} %broadcast_in_dim.6), channel_id=1, replica_groups={{29,28,25,24,21,20,17,16,13,12,9,8,5,4,1,0},{31,30,27,26,23,22,19,18,15..., dimensions={0} | all-to-all | bytes 16384 | tf_op jit(solution)/shard_map/all_to_all | solution.py:363
  29.1 0.9 %shard_map.52.refs_0_ = bf16[256,256]{1,0:T(8,128)(2,1)S(1)} custom-call(f32[16,1,128]{2,1,0:T(1,128)S(1)} %all_to_all.5.gram_ref, bf16[256,256]{1,0:T(8,128)(2,1)S(1)} %get-tuple-element.24.own_ref, bf16[256,256]{1,0:T(8,128)(2,1)S(1)} %get-tuple-element.17.refs_0_.rest_0_, bf16[256,256]{1,0:T(8,128)(2,1)S(1)} %collective-permute-done.refs_2_.refs_1_.rest_1_, ...), custom_call_target="tpu_custom_call" | custom-call | tf_op jit(solution)/shard_map/pallas_call | solution.py:365
  30.0 1.6 %collective-permute-start.12 = (bf16[256,256]{1,0:T(8,128)(2,1)S(1)}, bf16[256,256]{1,0:T(8,128)(2,1)S(1)}, u32[]{:S(2)}, u32[]{:S(2)}) collective-permute-start(bf16[256,256]{1,0:T(8,128)(2,1)S(1)} %shard_map.52.refs_0_), channel_id=1, source_target_pairs={{0,8},{1,9},{2,10},{3,11},{4,20},{5,21},{6,22},{7,23},{8,0},{9,1},... | collective-permute-start | bytes 393224 | tf_op jit(solution)/shard_map/ppermute | solution.py:287
  31.6 1.4 %collective-permute-start.10 = (bf16[256,256]{1,0:T(8,128)(2,1)S(1)}, bf16[256,256]{1,0:T(8,128)(2,1)S(1)}, u32[]{:S(2)}, u32[]{:S(2)}) collective-permute-start(bf16[256,256]{1,0:T(8,128)(2,1)S(1)} %shard_map.52.refs_0_), channel_id=1, source_target_pairs={{0,16},{1,17},{2,18},{3,19},{4,12},{5,13},{6,14},{7,15},{8,24},{9,... | collective-permute-start | bytes 393224 | tf_op jit(solution)/shard_map/ppermute | solution.py:287
  33.0 0.0 collective-permute-start.8
  33.0 0.7 %collective-permute-start.7 = (bf16[256,256]{1,0:T(8,128)(2,1)S(1)}, bf16[256,256]{1,0:T(8,128)(2,1)S(1)}, u32[]{:S(2)}, u32[]{:S(2)}) collective-permute-start(bf16[256,256]{1,0:T(8,128)(2,1)S(1)} %shard_map.52.refs_0_), channel_id=1, source_target_pairs={{0,4},{1,5},{2,6},{3,7},{4,0},{5,1},{6,2},{7,3},{8,12},{9,13},{10,... | collective-permute-start | bytes 393224 | tf_op jit(solution)/shard_map/ppermute | solution.py:287
  33.7 2.7 %collective-permute-done.12.refs_6_ = bf16[256,256]{1,0:T(8,128)(2,1)S(1)} collective-permute-done((bf16[256,256]{1,0:T(8,128)(2,1)S(1)}, bf16[256,256]{1,0:T(8,128)(2,1)S(1)}, u32[]{:S(2)}, u32[]{:S(2)}) %collective-permute-start.12) | collective-permute-done | bytes 131104 | tf_op jit(solution)/shard_map/ppermute | solution.py:287
  36.4 0.0 collective-permute-start.13
  36.4 0.2 collective-permute-done.10.refs_4_
  36.6 0.3 collective-permute-start.11
  36.9 2.5 %collective-permute-done.8.refs_2_ = bf16[256,256]{1,0:T(8,128)(2,1)S(1)} collective-permute-done((bf16[256,256]{1,0:T(8,128)(2,1)S(1)}, bf16[256,256]{1,0:T(8,128)(2,1)S(1)}, u32[]{:S(2)}, u32[]{:S(2)}) %collective-permute-start.8) | collective-permute-done | bytes 131104 | tf_op jit(solution)/shard_map/ppermute | solution.py:287
  39.4 0.0 collective-permute-start.9
  39.4 0.0 collective-permute-done.7.refs_1_
  39.4 0.0 collective-permute-done.13.refs_7_
  39.4 0.0 collective-permute-done.11.refs_5_
  39.4 1.3 %collective-permute-done.9.refs_3_ = bf16[256,256]{1,0:T(8,128)(2,1)S(1)} collective-permute-done((bf16[256,256]{1,0:T(8,128)(2,1)S(1)}, bf16[256,256]{1,0:T(8,128)(2,1)S(1)}, u32[]{:S(2)}, u32[]{:S(2)}) %collective-permute-start.9) | collective-permute-done | bytes 131104 | tf_op jit(solution)/shard_map/ppermute | solution.py:287
  40.7 1.0 %shard_map.53 = bf16[2048,256]{1,0:T(8,128)(2,1)} custom-call(bf16[256,256]{1,0:T(8,128)(2,1)S(1)} %shard_map.52.refs_0_, bf16[256,256]{1,0:T(8,128)(2,1)S(1)} %collective-permute-done.7.refs_1_, bf16[256,256]{1,0:T(8,128)(2,1)S(1)} %collective-permute-done.8.refs_2_, bf16[256,256]{1,0:T(8,128)(2,1)S(1)} %collective-permute-done.9.refs_3_, ...), custom_call_target="tpu_custom_call" | custom-call | tf_op jit(solution)/shard_map/pallas_call | solution.py:384
  (1 shorter events, 0.0 us)
Async XLA Ops:
  4.8 8.4 %collective-permute-start = (bf16[256,256]{1,0:T(8,128)(2,1)S(1)}, bf16[256,256]{1,0:T(8,128)(2,1)S(1)}, u32[]{:S(2)}, u32[]{:S(2)}) collective-permute-start(bf16[256,256]{1,0:T(8,128)(2,1)S(1)} %get-tuple-element.18), channel_id=1, source_target_pairs={{0,24},{1,25},{2,26},{3,27},{4,28},{5,29},{6,30},{7,31},{8,16},{9,... | collective-permute-start | bytes 393224 | tf_op jit(solution)/shard_map/ppermute | solution.py:287
  9.4 6.8 %collective-permute-start.1 = (bf16[256,256]{1,0:T(8,128)(2,1)S(1)}, bf16[256,256]{1,0:T(8,128)(2,1)S(1)}, u32[]{:S(2)}, u32[]{:S(2)}) collective-permute-start(bf16[256,256]{1,0:T(8,128)(2,1)S(1)} %get-tuple-element.19), channel_id=1, source_target_pairs={{0,8},{1,9},{2,10},{3,11},{4,12},{5,13},{6,14},{7,15},{8,0},{9,1},... | collective-permute-start | bytes 393224 | tf_op jit(solution)/shard_map/ppermute | solution.py:287
  10.0 7.4 %collective-permute-start.2 = (bf16[256,256]{1,0:T(8,128)(2,1)S(1)}, bf16[256,256]{1,0:T(8,128)(2,1)S(1)}, u32[]{:S(2)}, u32[]{:S(2)}) collective-permute-start(bf16[256,256]{1,0:T(8,128)(2,1)S(1)} %get-tuple-element.20), channel_id=1, source_target_pairs={{0,16},{1,17},{2,18},{3,19},{4,20},{5,21},{6,22},{7,23},{8,24},{9,... | collective-permute-start | bytes 393224 | tf_op jit(solution)/shard_map/ppermute | solution.py:287
  10.0 8.0 %collective-permute-start.3 = (bf16[256,256]{1,0:T(8,128)(2,1)S(1)}, bf16[256,256]{1,0:T(8,128)(2,1)S(1)}, u32[]{:S(2)}, u32[]{:S(2)}) collective-permute-start(bf16[256,256]{1,0:T(8,128)(2,1)S(1)} %get-tuple-element.21), channel_id=1, source_target_pairs={{0,28},{1,29},{2,30},{3,31},{4,24},{5,25},{6,26},{7,27},{8,20},{9,... | collective-permute-start | bytes 393224 | tf_op jit(solution)/shard_map/ppermute | solution.py:287
  11.5 8.6 %collective-permute-start.4 = (bf16[256,256]{1,0:T(8,128)(2,1)S(1)}, bf16[256,256]{1,0:T(8,128)(2,1)S(1)}, u32[]{:S(2)}, u32[]{:S(2)}) collective-permute-start(bf16[256,256]{1,0:T(8,128)(2,1)S(1)} %get-tuple-element.22), channel_id=1, source_target_pairs={{0,12},{1,13},{2,14},{3,15},{4,8},{5,9},{6,10},{7,11},{8,4},{9,5},... | collective-permute-start | bytes 393224 | tf_op jit(solution)/shard_map/ppermute | solution.py:287
  13.2 7.6 %collective-permute-start.5 = (bf16[256,256]{1,0:T(8,128)(2,1)S(1)}, bf16[256,256]{1,0:T(8,128)(2,1)S(1)}, u32[]{:S(2)}, u32[]{:S(2)}) collective-permute-start(bf16[256,256]{1,0:T(8,128)(2,1)S(1)} %get-tuple-element.23), channel_id=1, source_target_pairs={{0,20},{1,21},{2,22},{3,23},{4,16},{5,17},{6,18},{7,19},{8,28},{9,... | collective-permute-start | bytes 393224 | tf_op jit(solution)/shard_map/ppermute | solution.py:287
  16.1 4.7 %collective-permute-start.6 = (bf16[256,256]{1,0:T(8,128)(2,1)S(1)}, bf16[256,256]{1,0:T(8,128)(2,1)S(1)}, u32[]{:S(2)}, u32[]{:S(2)}) collective-permute-start(bf16[256,256]{1,0:T(8,128)(2,1)S(1)} %shard_map.48), channel_id=1, source_target_pairs={{0,4},{1,5},{2,6},{3,7},{4,0},{5,1},{6,2},{7,3},{8,12},{9,13},{10,... | collective-permute-start | bytes 393224 | tf_op jit(solution)/shard_map/ppermute | solution.py:287
  30.0 6.4 %collective-permute-start.12 = (bf16[256,256]{1,0:T(8,128)(2,1)S(1)}, bf16[256,256]{1,0:T(8,128)(2,1)S(1)}, u32[]{:S(2)}, u32[]{:S(2)}) collective-permute-start(bf16[256,256]{1,0:T(8,128)(2,1)S(1)} %shard_map.52.refs_0_), channel_id=1, source_target_pairs={{0,8},{1,9},{2,10},{3,11},{4,20},{5,21},{6,22},{7,23},{8,0},{9,1},... | collective-permute-start | bytes 393224 | tf_op jit(solution)/shard_map/ppermute | solution.py:287
  31.6 5.0 %collective-permute-start.10 = (bf16[256,256]{1,0:T(8,128)(2,1)S(1)}, bf16[256,256]{1,0:T(8,128)(2,1)S(1)}, u32[]{:S(2)}, u32[]{:S(2)}) collective-permute-start(bf16[256,256]{1,0:T(8,128)(2,1)S(1)} %shard_map.52.refs_0_), channel_id=1, source_target_pairs={{0,16},{1,17},{2,18},{3,19},{4,12},{5,13},{6,14},{7,15},{8,24},{9,... | collective-permute-start | bytes 393224 | tf_op jit(solution)/shard_map/ppermute | solution.py:287
  33.0 6.3 %collective-permute-start.8 = (bf16[256,256]{1,0:T(8,128)(2,1)S(1)}, bf16[256,256]{1,0:T(8,128)(2,1)S(1)}, u32[]{:S(2)}, u32[]{:S(2)}) collective-permute-start(bf16[256,256]{1,0:T(8,128)(2,1)S(1)} %shard_map.52.refs_0_), channel_id=1, source_target_pairs={{0,28},{1,29},{2,30},{3,31},{4,24},{5,25},{6,26},{7,27},{8,20},{9,... | collective-permute-start | bytes 393224 | tf_op jit(solution)/shard_map/ppermute | solution.py:287
  33.0 6.3 %collective-permute-start.7 = (bf16[256,256]{1,0:T(8,128)(2,1)S(1)}, bf16[256,256]{1,0:T(8,128)(2,1)S(1)}, u32[]{:S(2)}, u32[]{:S(2)}) collective-permute-start(bf16[256,256]{1,0:T(8,128)(2,1)S(1)} %shard_map.52.refs_0_), channel_id=1, source_target_pairs={{0,4},{1,5},{2,6},{3,7},{4,0},{5,1},{6,2},{7,3},{8,12},{9,13},{10,... | collective-permute-start | bytes 393224 | tf_op jit(solution)/shard_map/ppermute | solution.py:287
  36.4 3.0 %collective-permute-start.13 = (bf16[256,256]{1,0:T(8,128)(2,1)S(1)}, bf16[256,256]{1,0:T(8,128)(2,1)S(1)}, u32[]{:S(2)}, u32[]{:S(2)}) collective-permute-start(bf16[256,256]{1,0:T(8,128)(2,1)S(1)} %collective-permute-done.12.refs_6_), channel_id=1, source_target_pairs={{0,4},{1,5},{2,6},{3,7},{4,0},{5,1},{6,2},{7,3},{8,12},{9,13},{10,... | collective-permute-start | bytes 393224 | tf_op jit(solution)/shard_map/ppermute | solution.py:287
  36.6 2.8 %collective-permute-start.11 = (bf16[256,256]{1,0:T(8,128)(2,1)S(1)}, bf16[256,256]{1,0:T(8,128)(2,1)S(1)}, u32[]{:S(2)}, u32[]{:S(2)}) collective-permute-start(bf16[256,256]{1,0:T(8,128)(2,1)S(1)} %collective-permute-done.10.refs_4_), channel_id=1, source_target_pairs={{0,4},{1,5},{2,6},{3,7},{4,0},{5,1},{6,2},{7,3},{8,12},{9,13},{10,... | collective-permute-start | bytes 393224 | tf_op jit(solution)/shard_map/ppermute | solution.py:287
  39.4 1.3 %collective-permute-start.9 = (bf16[256,256]{1,0:T(8,128)(2,1)S(1)}, bf16[256,256]{1,0:T(8,128)(2,1)S(1)}, u32[]{:S(2)}, u32[]{:S(2)}) collective-permute-start(bf16[256,256]{1,0:T(8,128)(2,1)S(1)} %collective-permute-done.8.refs_2_), channel_id=1, source_target_pairs={{0,4},{1,5},{2,6},{3,7},{4,0},{5,1},{6,2},{7,3},{8,12},{9,13},{10,... | collective-permute-start | bytes 393224 | tf_op jit(solution)/shard_map/ppermute | solution.py:287

commit v11 on v10

--- a/solution.py
+++ b/solution.py
@@ -241,7 +241,7 @@
             weight = jnp.where((me ^ distance) == k, weights[k], weight)
         term = weight * delta[...].astype(F32)
         total = term if total is None else total + term
-    combined = total.T.astype(BF16).astype(F32)
+    combined = total.astype(BF16).T.astype(F32)
     out_ref[...] = (own_ref[...].astype(F32) + combined).astype(BF16)
 
 
@@ -342,7 +342,7 @@
 
     table = jax.ShapeDtypeStruct((-(-parts * parts // 128), 128), F32)
     gram, known = [], 0
-    for reached in (parts - 3, parts - 2, parts):
+    for reached in (parts - 3, parts):
         if reached <= known:
             continue
         taken = order[:reached]

time: 41.9 us -> 42 us (level)
    pallas_call x3 -> x2, Pallas kernels: 1.11 us -> 0.97 us  [body(): call(products, table, [near] * len(inputs))(*inputs)]
  transfers between devices with their start and end apart: 14 -> 14, of which waited for: 9 -> 9; matrix products, arithmetic and copies ran while one was open for 0% -> 0% of each run, Pallas kernels for 4% -> 3%
where the time goes in v11:
time: 42 us; the launch traced here: 41.8 us
  waiting for transfers between devices  13.6 us (32%)
  starting transfers between devices  11.8 us (28%)
  Pallas kernels  8.47 us (20%)
  blocking collectives  7.85 us (19%)
    ppermute x14, waiting for transfers between devices, flipped(): return lax.ppermute(value, ('rep', 'shard'), pairs)  13.6 us
    ppermute x14, starting transfers between devices, flipped(): return lax.ppermute(value, ('rep', 'shard'), pairs)  11.8 us
    all_to_all x1, blocking collectives, body(): lax.all_to_all(gram, ('rep', 'shard'), 0, 0, axis_index_groups=groups)  7.85 us
    pallas_call x1, Pallas kernels, body(): call(local, [rows_out, jax.ShapeDtypeStruct((seg, columns), BF16), jax.Sh...  4.79 us
    pallas_call x1, Pallas kernels, body(): call(place, jax.ShapeDtypeStruct((width, columns), BF16), [any_place] * p...  1.02 us
    pallas_call x2, Pallas kernels, body(): call(products, table, [near] * len(inputs))(*inputs)  0.97 us
    pallas_call x1, Pallas kernels, body(): call(combine_kernel, jax.ShapeDtypeStruct((seg, columns), BF16), [near] *...  0.85 us
  transfers between devices with their start and end apart: 14, of which 9 were waited for; matrix products, arithmetic and copies ran while one was open for 0% of the time, Pallas kernels for 3%

profile of v11, /device:TPU:0, one launch (start us, length us, event | category | flops | bytes accessed | tf_op | source)
XLA Modules:
  0.0 41.8 jit_solution(9259326261866251549)
XLA Ops:
  0.0 4.8 %shard_map.46 = (bf16[256,256]{1,0:T(8,128)(2,1)S(1)}, bf16[256,256]{1,0:T(8,128)(2,1)S(1)}, bf16[256,512]{1,0:T(8,128)(2,1)S(1)}, bf16[512,2048]{1,0:T(8,128)(2,1)S(1)}) custom-call(s32[2,1,512]{2,1,0:T(1,128)} %bitcast.10, bf16[384,2048]{1,0:T(8,128)(2,1)} %bitcast.7, bf16[2048,256]{1,0:T(8,128)(2,1)} %bitcast.8, bf16[512,256]{1,0:T(8,128)(2,1)} %bitcast.9), custom_call_target="tpu_custom_call" | custom-call | tf_op jit(solution)/shard_map/pallas_call | solution.py:308
  4.8 4.0 %collective-permute-start = (bf16[256,256]{1,0:T(8,128)(2,1)S(1)}, bf16[256,256]{1,0:T(8,128)(2,1)S(1)}, u32[]{:S(2)}, u32[]{:S(2)}) collective-permute-start(bf16[256,256]{1,0:T(8,128)(2,1)S(1)} %get-tuple-element.18), channel_id=1, source_target_pairs={{0,24},{1,25},{2,26},{3,27},{4,28},{5,29},{6,30},{7,31},{8,16},{9,... | collective-permute-start | bytes 393224 | tf_op jit(solution)/shard_map/ppermute | solution.py:287
  8.8 0.6 %shard_map.47 = (bf16[256,256]{1,0:T(8,128)(2,1)S(1)}, bf16[256,256]{1,0:T(8,128)(2,1)S(1)}, bf16[256,256]{1,0:T(8,128)(2,1)S(1)}, bf16[256,256]{1,0:T(8,128)(2,...) custom-call(bf16[256,512]{1,0:T(8,128)(2,1)S(1)} %get-tuple-element.15.refs_0_, ...), custom_call_target="tpu_custom_call" | custom-call | tf_op jit(solution)/shard_map/pallas_call | solution.py:337
  9.4 0.6 %collective-permute-start.1 = (bf16[256,256]{1,0:T(8,128)(2,1)S(1)}, bf16[256,256]{1,0:T(8,128)(2,1)S(1)}, u32[]{:S(2)}, u32[]{:S(2)}) collective-permute-start(bf16[256,256]{1,0:T(8,128)(2,1)S(1)} %get-tuple-element.19), channel_id=1, source_target_pairs={{0,8},{1,9},{2,10},{3,11},{4,12},{5,13},{6,14},{7,15},{8,0},{9,1},... | collective-permute-start | bytes 393224 | tf_op jit(solution)/shard_map/ppermute | solution.py:287
  10.0 0.1 collective-permute-start.2
  10.0 1.5 %collective-permute-start.3 = (bf16[256,256]{1,0:T(8,128)(2,1)S(1)}, bf16[256,256]{1,0:T(8,128)(2,1)S(1)}, u32[]{:S(2)}, u32[]{:S(2)}) collective-permute-start(bf16[256,256]{1,0:T(8,128)(2,1)S(1)} %get-tuple-element.21), channel_id=1, source_target_pairs={{0,28},{1,29},{2,30},{3,31},{4,24},{5,25},{6,26},{7,27},{8,20},{9,... | collective-permute-start | bytes 393224 | tf_op jit(solution)/shard_map/ppermute | solution.py:287
  11.5 1.7 %collective-permute-start.4 = (bf16[256,256]{1,0:T(8,128)(2,1)S(1)}, bf16[256,256]{1,0:T(8,128)(2,1)S(1)}, u32[]{:S(2)}, u32[]{:S(2)}) collective-permute-start(bf16[256,256]{1,0:T(8,128)(2,1)S(1)} %get-tuple-element.22), channel_id=1, source_target_pairs={{0,12},{1,13},{2,14},{3,15},{4,8},{5,9},{6,10},{7,11},{8,4},{9,5},... | collective-permute-start | bytes 393224 | tf_op jit(solution)/shard_map/ppermute | solution.py:287
  13.2 0.0 collective-permute-done.refs_2_.refs_1_.rest_1_
  13.2 0.0 collective-permute-start.5
  13.2 0.2 shard_map.48
  13.5 2.7 %collective-permute-done.1.refs_2_.rest_2_ = bf16[256,256]{1,0:T(8,128)(2,1)S(1)} collective-permute-done((bf16[256,256]{1,0:T(8,128)(2,1)S(1)}, bf16[256,256]{1,0:T(8,128)(2,1)S(1)}, u32[]{:S(2)}, u32[]{:S(2)}) %collective-permute-start.1) | collective-permute-done | bytes 131104 | tf_op jit(solution)/shard_map/ppermute | solution.py:287
  16.1 0.0 collective-permute-start.6
  16.2 1.2 %collective-permute-done.2.refs_3_.rest_3_ = bf16[256,256]{1,0:T(8,128)(2,1)S(1)} collective-permute-done((bf16[256,256]{1,0:T(8,128)(2,1)S(1)}, bf16[256,256]{1,0:T(8,128)(2,1)S(1)}, u32[]{:S(2)}, u32[]{:S(2)}) %collective-permute-start.2) | collective-permute-done | bytes 131104 | tf_op jit(solution)/shard_map/ppermute | solution.py:287
  17.4 0.6 %collective-permute-done.3.refs_4_.rest_4_ = bf16[256,256]{1,0:T(8,128)(2,1)S(1)} collective-permute-done((bf16[256,256]{1,0:T(8,128)(2,1)S(1)}, bf16[256,256]{1,0:T(8,128)(2,1)S(1)}, u32[]{:S(2)}, u32[]{:S(2)}) %collective-permute-start.3) | collective-permute-done | bytes 131104 | tf_op jit(solution)/shard_map/ppermute | solution.py:287
  18.0 0.4 shard_map.49.refs_8_
  18.4 1.7 %collective-permute-done.4.refs_5_.rest_5_ = bf16[256,256]{1,0:T(8,128)(2,1)S(1)} collective-permute-done((bf16[256,256]{1,0:T(8,128)(2,1)S(1)}, bf16[256,256]{1,0:T(8,128)(2,1)S(1)}, u32[]{:S(2)}, u32[]{:S(2)}) %collective-permute-start.4) | collective-permute-done | bytes 131104 | tf_op jit(solution)/shard_map/ppermute | solution.py:287
  20.1 0.7 %collective-permute-done.5.refs_6_.rest_6_ = bf16[256,256]{1,0:T(8,128)(2,1)S(1)} collective-permute-done((bf16[256,256]{1,0:T(8,128)(2,1)S(1)}, bf16[256,256]{1,0:T(8,128)(2,1)S(1)}, u32[]{:S(2)}, u32[]{:S(2)}) %collective-permute-start.5) | collective-permute-done | bytes 131104 | tf_op jit(solution)/shard_map/ppermute | solution.py:287
  20.8 0.0 collective-permute-done.6.refs_7_.rest_7_
  20.8 0.6 %shard_map.50 = f32[1,128]{1,0:T(1,128)S(1)} custom-call(bf16[256,256]{1,0:T(8,128)(2,1)S(1)} %get-tuple-element.17.refs_0_.rest_0_, bf16[256,256]{1,0:T(8,128)(2,1)S(1)} %collective-permute-done.refs_2_.refs_1_.rest_1_, bf16[256,256]{1,0:T(8,128)(2,1)S(1)} %collective-permute-done.1.refs_2_.rest_2_, ...), custom_call_target="tpu_custom_call" | custom-call | tf_op jit(solution)/shard_map/pallas_call | solution.py:354
  21.4 7.8 %all_to_all.5.gram_ref = f32[16,1,128]{2,1,0:T(1,128)S(1)} all-to-all(f32[16,1,128]{2,1,0:T(1,128)S(1)} %broadcast_in_dim.6), channel_id=1, replica_groups={{29,28,25,24,21,20,17,16,13,12,9,8,5,4,1,0},{31,30,27,26,23,22,19,18,15..., dimensions={0} | all-to-all | bytes 16384 | tf_op jit(solution)/shard_map/all_to_all | solution.py:363
  29.3 0.9 %shard_map.51.refs_0_ = bf16[256,256]{1,0:T(8,128)(2,1)S(1)} custom-call(f32[16,1,128]{2,1,0:T(1,128)S(1)} %all_to_all.5.gram_ref, bf16[256,256]{1,0:T(8,128)(2,1)S(1)} %get-tuple-element.24.own_ref, bf16[256,256]{1,0:T(8,128)(2,1)S(1)} %get-tuple-element.17.refs_0_.rest_0_, bf16[256,256]{1,0:T(8,128)(2,1)S(1)} %collective-permute-done.refs_2_.refs_1_.rest_1_, ...), custom_call_target="tpu_custom_call" | custom-call | tf_op jit(solution)/shard_map/pallas_call | solution.py:365
  30.1 1.6 %collective-permute-start.12 = (bf16[256,256]{1,0:T(8,128)(2,1)S(1)}, bf16[256,256]{1,0:T(8,128)(2,1)S(1)}, u32[]{:S(2)}, u32[]{:S(2)}) collective-permute-start(bf16[256,256]{1,0:T(8,128)(2,1)S(1)} %shard_map.51.refs_0_), channel_id=1, source_target_pairs={{0,8},{1,9},{2,10},{3,11},{4,20},{5,21},{6,22},{7,23},{8,0},{9,1},... | collective-permute-start | bytes 393224 | tf_op jit(solution)/shard_map/ppermute | solution.py:287
  31.7 1.4 %collective-permute-start.10 = (bf16[256,256]{1,0:T(8,128)(2,1)S(1)}, bf16[256,256]{1,0:T(8,128)(2,1)S(1)}, u32[]{:S(2)}, u32[]{:S(2)}) collective-permute-start(bf16[256,256]{1,0:T(8,128)(2,1)S(1)} %shard_map.51.refs_0_), channel_id=1, source_target_pairs={{0,16},{1,17},{2,18},{3,19},{4,12},{5,13},{6,14},{7,15},{8,24},{9,... | collective-permute-start | bytes 393224 | tf_op jit(solution)/shard_map/ppermute | solution.py:287
  33.1 0.0 collective-permute-start.8
  33.1 0.7 %collective-permute-start.7 = (bf16[256,256]{1,0:T(8,128)(2,1)S(1)}, bf16[256,256]{1,0:T(8,128)(2,1)S(1)}, u32[]{:S(2)}, u32[]{:S(2)}) collective-permute-start(bf16[256,256]{1,0:T(8,128)(2,1)S(1)} %shard_map.51.refs_0_), channel_id=1, source_target_pairs={{0,4},{1,5},{2,6},{3,7},{4,0},{5,1},{6,2},{7,3},{8,12},{9,13},{10,... | collective-permute-start | bytes 393224 | tf_op jit(solution)/shard_map/ppermute | solution.py:287
  33.8 2.7 %collective-permute-done.12.refs_6_ = bf16[256,256]{1,0:T(8,128)(2,1)S(1)} collective-permute-done((bf16[256,256]{1,0:T(8,128)(2,1)S(1)}, bf16[256,256]{1,0:T(8,128)(2,1)S(1)}, u32[]{:S(2)}, u32[]{:S(2)}) %collective-permute-start.12) | collective-permute-done | bytes 131104 | tf_op jit(solution)/shard_map/ppermute | solution.py:287
  36.5 0.0 collective-permute-start.13
  36.5 0.2 collective-permute-done.10.refs_4_
  36.7 0.3 collective-permute-start.11
  37.0 2.5 %collective-permute-done.8.refs_2_ = bf16[256,256]{1,0:T(8,128)(2,1)S(1)} collective-permute-done((bf16[256,256]{1,0:T(8,128)(2,1)S(1)}, bf16[256,256]{1,0:T(8,128)(2,1)S(1)}, u32[]{:S(2)}, u32[]{:S(2)}) %collective-permute-start.8) | collective-permute-done | bytes 131104 | tf_op jit(solution)/shard_map/ppermute | solution.py:287
  39.5 0.0 collective-permute-start.9
  39.5 0.0 collective-permute-done.7.refs_1_
  39.5 0.0 collective-permute-done.13.refs_7_
  39.5 0.0 collective-permute-done.11.refs_5_
  39.5 1.3 %collective-permute-done.9.refs_3_ = bf16[256,256]{1,0:T(8,128)(2,1)S(1)} collective-permute-done((bf16[256,256]{1,0:T(8,128)(2,1)S(1)}, bf16[256,256]{1,0:T(8,128)(2,1)S(1)}, u32[]{:S(2)}, u32[]{:S(2)}) %collective-permute-start.9) | collective-permute-done | bytes 131104 | tf_op jit(solution)/shard_map/ppermute | solution.py:287
  40.8 1.0 %shard_map.52 = bf16[2048,256]{1,0:T(8,128)(2,1)} custom-call(bf16[256,256]{1,0:T(8,128)(2,1)S(1)} %shard_map.51.refs_0_, bf16[256,256]{1,0:T(8,128)(2,1)S(1)} %collective-permute-done.7.refs_1_, bf16[256,256]{1,0:T(8,128)(2,1)S(1)} %collective-permute-done.8.refs_2_, bf16[256,256]{1,0:T(8,128)(2,1)S(1)} %collective-permute-done.9.refs_3_, ...), custom_call_target="tpu_custom_call" | custom-call | tf_op jit(solution)/shard_map/pallas_call | solution.py:384
  (1 shorter events, 0.0 us)
Async XLA Ops:
  4.8 8.4 %collective-permute-start = (bf16[256,256]{1,0:T(8,128)(2,1)S(1)}, bf16[256,256]{1,0:T(8,128)(2,1)S(1)}, u32[]{:S(2)}, u32[]{:S(2)}) collective-permute-start(bf16[256,256]{1,0:T(8,128)(2,1)S(1)} %get-tuple-element.18), channel_id=1, source_target_pairs={{0,24},{1,25},{2,26},{3,27},{4,28},{5,29},{6,30},{7,31},{8,16},{9,... | collective-permute-start | bytes 393224 | tf_op jit(solution)/shard_map/ppermute | solution.py:287
  9.4 6.8 %collective-permute-start.1 = (bf16[256,256]{1,0:T(8,128)(2,1)S(1)}, bf16[256,256]{1,0:T(8,128)(2,1)S(1)}, u32[]{:S(2)}, u32[]{:S(2)}) collective-permute-start(bf16[256,256]{1,0:T(8,128)(2,1)S(1)} %get-tuple-element.19), channel_id=1, source_target_pairs={{0,8},{1,9},{2,10},{3,11},{4,12},{5,13},{6,14},{7,15},{8,0},{9,1},... | collective-permute-start | bytes 393224 | tf_op jit(solution)/shard_map/ppermute | solution.py:287
  10.0 7.4 %collective-permute-start.2 = (bf16[256,256]{1,0:T(8,128)(2,1)S(1)}, bf16[256,256]{1,0:T(8,128)(2,1)S(1)}, u32[]{:S(2)}, u32[]{:S(2)}) collective-permute-start(bf16[256,256]{1,0:T(8,128)(2,1)S(1)} %get-tuple-element.20), channel_id=1, source_target_pairs={{0,16},{1,17},{2,18},{3,19},{4,20},{5,21},{6,22},{7,23},{8,24},{9,... | collective-permute-start | bytes 393224 | tf_op jit(solution)/shard_map/ppermute | solution.py:287
  10.0 8.0 %collective-permute-start.3 = (bf16[256,256]{1,0:T(8,128)(2,1)S(1)}, bf16[256,256]{1,0:T(8,128)(2,1)S(1)}, u32[]{:S(2)}, u32[]{:S(2)}) collective-permute-start(bf16[256,256]{1,0:T(8,128)(2,1)S(1)} %get-tuple-element.21), channel_id=1, source_target_pairs={{0,28},{1,29},{2,30},{3,31},{4,24},{5,25},{6,26},{7,27},{8,20},{9,... | collective-permute-start | bytes 393224 | tf_op jit(solution)/shard_map/ppermute | solution.py:287
  11.5 8.6 %collective-permute-start.4 = (bf16[256,256]{1,0:T(8,128)(2,1)S(1)}, bf16[256,256]{1,0:T(8,128)(2,1)S(1)}, u32[]{:S(2)}, u32[]{:S(2)}) collective-permute-start(bf16[256,256]{1,0:T(8,128)(2,1)S(1)} %get-tuple-element.22), channel_id=1, source_target_pairs={{0,12},{1,13},{2,14},{3,15},{4,8},{5,9},{6,10},{7,11},{8,4},{9,5},... | collective-permute-start | bytes 393224 | tf_op jit(solution)/shard_map/ppermute | solution.py:287
  13.2 7.6 %collective-permute-start.5 = (bf16[256,256]{1,0:T(8,128)(2,1)S(1)}, bf16[256,256]{1,0:T(8,128)(2,1)S(1)}, u32[]{:S(2)}, u32[]{:S(2)}) collective-permute-start(bf16[256,256]{1,0:T(8,128)(2,1)S(1)} %get-tuple-element.23), channel_id=1, source_target_pairs={{0,20},{1,21},{2,22},{3,23},{4,16},{5,17},{6,18},{7,19},{8,28},{9,... | collective-permute-start | bytes 393224 | tf_op jit(solution)/shard_map/ppermute | solution.py:287
  16.1 4.7 %collective-permute-start.6 = (bf16[256,256]{1,0:T(8,128)(2,1)S(1)}, bf16[256,256]{1,0:T(8,128)(2,1)S(1)}, u32[]{:S(2)}, u32[]{:S(2)}) collective-permute-start(bf16[256,256]{1,0:T(8,128)(2,1)S(1)} %shard_map.48), channel_id=1, source_target_pairs={{0,4},{1,5},{2,6},{3,7},{4,0},{5,1},{6,2},{7,3},{8,12},{9,13},{10,... | collective-permute-start | bytes 393224 | tf_op jit(solution)/shard_map/ppermute | solution.py:287
  30.1 6.4 %collective-permute-start.12 = (bf16[256,256]{1,0:T(8,128)(2,1)S(1)}, bf16[256,256]{1,0:T(8,128)(2,1)S(1)}, u32[]{:S(2)}, u32[]{:S(2)}) collective-permute-start(bf16[256,256]{1,0:T(8,128)(2,1)S(1)} %shard_map.51.refs_0_), channel_id=1, source_target_pairs={{0,8},{1,9},{2,10},{3,11},{4,20},{5,21},{6,22},{7,23},{8,0},{9,1},... | collective-permute-start | bytes 393224 | tf_op jit(solution)/shard_map/ppermute | solution.py:287
  31.7 5.0 %collective-permute-start.10 = (bf16[256,256]{1,0:T(8,128)(2,1)S(1)}, bf16[256,256]{1,0:T(8,128)(2,1)S(1)}, u32[]{:S(2)}, u32[]{:S(2)}) collective-permute-start(bf16[256,256]{1,0:T(8,128)(2,1)S(1)} %shard_map.51.refs_0_), channel_id=1, source_target_pairs={{0,16},{1,17},{2,18},{3,19},{4,12},{5,13},{6,14},{7,15},{8,24},{9,... | collective-permute-start | bytes 393224 | tf_op jit(solution)/shard_map/ppermute | solution.py:287
  33.1 6.3 %collective-permute-start.8 = (bf16[256,256]{1,0:T(8,128)(2,1)S(1)}, bf16[256,256]{1,0:T(8,128)(2,1)S(1)}, u32[]{:S(2)}, u32[]{:S(2)}) collective-permute-start(bf16[256,256]{1,0:T(8,128)(2,1)S(1)} %shard_map.51.refs_0_), channel_id=1, source_target_pairs={{0,28},{1,29},{2,30},{3,31},{4,24},{5,25},{6,26},{7,27},{8,20},{9,... | collective-permute-start | bytes 393224 | tf_op jit(solution)/shard_map/ppermute | solution.py:287
  33.1 6.3 %collective-permute-start.7 = (bf16[256,256]{1,0:T(8,128)(2,1)S(1)}, bf16[256,256]{1,0:T(8,128)(2,1)S(1)}, u32[]{:S(2)}, u32[]{:S(2)}) collective-permute-start(bf16[256,256]{1,0:T(8,128)(2,1)S(1)} %shard_map.51.refs_0_), channel_id=1, source_target_pairs={{0,4},{1,5},{2,6},{3,7},{4,0},{5,1},{6,2},{7,3},{8,12},{9,13},{10,... | collective-permute-start | bytes 393224 | tf_op jit(solution)/shard_map/ppermute | solution.py:287
  36.5 3.0 %collective-permute-start.13 = (bf16[256,256]{1,0:T(8,128)(2,1)S(1)}, bf16[256,256]{1,0:T(8,128)(2,1)S(1)}, u32[]{:S(2)}, u32[]{:S(2)}) collective-permute-start(bf16[256,256]{1,0:T(8,128)(2,1)S(1)} %collective-permute-done.12.refs_6_), channel_id=1, source_target_pairs={{0,4},{1,5},{2,6},{3,7},{4,0},{5,1},{6,2},{7,3},{8,12},{9,13},{10,... | collective-permute-start | bytes 393224 | tf_op jit(solution)/shard_map/ppermute | solution.py:287
  36.7 2.8 %collective-permute-start.11 = (bf16[256,256]{1,0:T(8,128)(2,1)S(1)}, bf16[256,256]{1,0:T(8,128)(2,1)S(1)}, u32[]{:S(2)}, u32[]{:S(2)}) collective-permute-start(bf16[256,256]{1,0:T(8,128)(2,1)S(1)} %collective-permute-done.10.refs_4_), channel_id=1, source_target_pairs={{0,4},{1,5},{2,6},{3,7},{4,0},{5,1},{6,2},{7,3},{8,12},{9,13},{10,... | collective-permute-start | bytes 393224 | tf_op jit(solution)/shard_map/ppermute | solution.py:287
  39.5 1.3 %collective-permute-start.9 = (bf16[256,256]{1,0:T(8,128)(2,1)S(1)}, bf16[256,256]{1,0:T(8,128)(2,1)S(1)}, u32[]{:S(2)}, u32[]{:S(2)}) collective-permute-start(bf16[256,256]{1,0:T(8,128)(2,1)S(1)} %collective-permute-done.8.refs_2_), channel_id=1, source_target_pairs={{0,4},{1,5},{2,6},{3,7},{4,0},{5,1},{6,2},{7,3},{8,12},{9,13},{10,... | collective-permute-start | bytes 393224 | tf_op jit(solution)/shard_map/ppermute | solution.py:287
